TPU v7x, 32 devices: a whole 2x2x4 slice. The times are simulated.
32 devices in a mesh: dp: 8 (over z, x), seq: 4 (over y, core).
Axes of the slice: x: 2, y: 2, z: 4, core: 2. Of those that a mesh axis runs over, the one named last changes fastest.
Arguments:
- passages: bfloat16 [32, 512, 768], P('dp', 'seq'), may hold values from -6 to 6
- lengths: int32 [32], P('dp'), may hold values from 32 to 512, as said below
- attn_gain: float32 [768], replicated, may hold values from 0.5 to 1.5
- w_query: bfloat16 [768, 768], P('dp'), may hold values from -0.0546875 to 0.0546875
- w_key: bfloat16 [768, 768], P('dp'), may hold values from -0.21875 to 0.21875
- w_value: bfloat16 [768, 768], P('dp'), may hold values from -0.21875 to 0.21875
- w_attn_out: bfloat16 [768, 768], P('dp'), may hold values from -0.625 to 0.625
- bias_table: float32 [32, 12], replicated, may hold values from -4 to 4
- ffn_gain: float32 [768], replicated, may hold values from 0.5 to 1.5
- w_in: bfloat16 [768, 3072], P('dp'), may hold values from -0.21875 to 0.21875
- w_ff_out: bfloat16 [3072, 768], P('dp'), may hold values from -0.109375 to 0.109375
- cotangent: bfloat16 [32, 512, 768], P('dp', 'seq'), may hold values from -6 to 6
Outputs:
- layer_out: bfloat16 [32, 512, 768], P('dp', 'seq')
- pooled: float32 [32, 768], P('dp')
- grad_passages: bfloat16 [32, 512, 768], P('dp', 'seq')
- grad_attn_gain: float32 [768], replicated
- grad_w_query: float32 [768, 768], P('dp')
- grad_w_key: float32 [768, 768], P('dp')
- grad_w_value: float32 [768, 768], P('dp')
- grad_w_attn_out: float32 [768, 768], P('dp')
- grad_bias_table: float32 [32, 12], replicated
- grad_ffn_gain: float32 [768], replicated
- grad_w_in: float32 [768, 3072], P('dp')
- grad_w_ff_out: float32 [3072, 768], P('dp')
Inputs may be any that keep to these rules, and one draw needn't show every extreme that they name: `lengths`: among the 4 passages of each index of dp (aligned blocks of 4 passages) one has exactly 512 tokens.
All inputs are finite; a program needn't handle non-finite values.
Results may differ from a plain program's by a relative error of at most 0.018.
Values may be sent and summed in bfloat16 or wider, within the bound.
A program may use at most 192 MiB of HBM per device.

v0:
```python
import math

import jax
import jax.numpy as jnp
from jax import lax
from jax.sharding import PartitionSpec as P

MAXDIST = 128


EPS = 1e-06
HIGH = lax.Precision.HIGHEST
FLOOR = -1e30


def bucket_index(relative, buckets, reach):
    half_count = buckets // 2
    exact_count = half_count // 2
    distance = jnp.abs(relative)
    result = jnp.minimum(distance, exact_count)
    for power in range(1, half_count - exact_count):
        bound_at = math.ceil(
            exact_count * (reach / exact_count) ** (power / (half_count - exact_count)) - 1e-06
        )
        result = result + (distance >= bound_at).astype(jnp.int32)
    return result + (relative > 0).astype(jnp.int32) * half_count


def rms_norm(values, gain_vec):
    return values * lax.rsqrt(jnp.mean(values * values, axis=-1, keepdims=True) + EPS) * gain_vec


def attend_forward(query_four, key_four, value_four, bias_rows, key_valid):
    scores = (
        jnp.einsum("pqhe,pkhe->phqk", query_four, key_four, preferred_element_type=jnp.float32)
        + bias_rows[None]
    )
    scores = jnp.where(key_valid[:, None, None, :], scores, FLOOR)
    row_top = jnp.max(scores, axis=-1, keepdims=True)
    expo = jnp.exp(scores - row_top)
    row_total = jnp.sum(expo, axis=-1, keepdims=True)
    log_total = row_top + jnp.log(row_total)
    attn_probs = (expo / row_total).astype(jnp.bfloat16)
    mixed_rows = jnp.einsum(
        "phqk,pkhe->pqhe", attn_probs, value_four, preferred_element_type=jnp.float32
    )
    return (mixed_rows.astype(jnp.bfloat16), log_total)


def attend_backward(query_four, key_four, value_four, grad_mixed, log_total, key_valid, bias_rows):

    def one_passage(score_sum, pieces):
        query_p, key_p, value_p, grad_p, log_p, valid_p = pieces
        score_p = (
            jnp.einsum("qhe,khe->hqk", query_p, key_p, preferred_element_type=jnp.float32)
            + bias_rows
        )
        score_p = jnp.where(valid_p[None, None, :], score_p, FLOOR)
        prob_p = jnp.exp(score_p - log_p)
        grad_prob = jnp.einsum("qhe,khe->hqk", grad_p, value_p, preferred_element_type=jnp.float32)
        grad_score = (
            prob_p * (grad_prob - jnp.sum(prob_p * grad_prob, axis=-1, keepdims=True))
        ).astype(jnp.bfloat16)
        grad_query_p = jnp.einsum(
            "hqk,khe->qhe", grad_score, key_p, preferred_element_type=jnp.float32
        ).astype(jnp.bfloat16)
        grad_key_p = jnp.einsum(
            "hqk,qhe->khe", grad_score, query_p, preferred_element_type=jnp.float32
        )
        grad_value_p = jnp.einsum(
            "hqk,qhe->khe", prob_p.astype(jnp.bfloat16), grad_p, preferred_element_type=jnp.float32
        )
        return (
            score_sum + grad_score.astype(jnp.float32),
            (grad_query_p, grad_key_p, grad_value_p),
        )

    start_sum = jnp.zeros(bias_rows.shape, jnp.float32)
    return lax.scan(
        one_passage, start_sum, (query_four, key_four, value_four, grad_mixed, log_total, key_valid)
    )


def shards(
    passages,
    lengths,
    attn_gain,
    w_query,
    w_key,
    w_value,
    w_attn_out,
    bias_table,
    ffn_gain,
    w_in,
    w_ff_out,
    cotangent,
):
    n_pass, local_rows, width = passages.shape
    n_buckets, n_heads = bias_table.shape
    head_dim = width // n_heads
    seq_count = lax.axis_size("seq")
    full_len = local_rows * seq_count
    row_count = n_pass * local_rows
    first_row = lax.axis_index("seq") * local_rows
    gathered = (
        lax.all_gather(w_query, "dp", axis=0, tiled=True),
        lax.all_gather(w_key, "dp", axis=0, tiled=True),
        lax.all_gather(w_value, "dp", axis=0, tiled=True),
        lax.all_gather(w_attn_out, "dp", axis=0, tiled=True),
        lax.all_gather(w_in, "dp", axis=0, tiled=True),
        lax.all_gather(w_ff_out, "dp", axis=0, tiled=True),
    )
    wq_full, wk_full, wv_full, wo_full, win_full, wff_full = gathered
    key_pos = jnp.arange(full_len, dtype=jnp.int32)
    query_pos = first_row + jnp.arange(local_rows, dtype=jnp.int32)
    key_valid = key_pos[None, :] < lengths[:, None]
    query_valid = query_pos[None, :] < lengths[:, None]
    inputs = passages.astype(jnp.float32).reshape(row_count, width)
    normed = rms_norm(inputs, attn_gain).astype(jnp.bfloat16)
    query_rows = jnp.dot(normed, wq_full, preferred_element_type=jnp.float32).astype(jnp.bfloat16)
    key_rows = jnp.dot(normed, wk_full, preferred_element_type=jnp.float32).astype(jnp.bfloat16)
    value_rows = jnp.dot(normed, wv_full, preferred_element_type=jnp.float32).astype(jnp.bfloat16)
    query_local = query_rows.reshape(n_pass, local_rows, n_heads, head_dim)
    relative = key_pos[None, :] - query_pos[:, None]
    one_hot = (
        bucket_index(relative, n_buckets, MAXDIST)[:, :, None]
        == jnp.arange(n_buckets, dtype=jnp.int32)
    ).astype(jnp.float32)
    bias_rows = jnp.einsum("qkb,bh->hqk", one_hot, bias_table, precision=HIGH)
    key_all, value_all = (
        lax.all_gather(key_rows.reshape(n_pass, local_rows, width), "seq", axis=1, tiled=True),
        lax.all_gather(value_rows.reshape(n_pass, local_rows, width), "seq", axis=1, tiled=True),
    )
    key_four = key_all.reshape(n_pass, full_len, n_heads, head_dim)
    value_four = value_all.reshape(n_pass, full_len, n_heads, head_dim)
    mixed_four, log_total = attend_forward(query_local, key_four, value_four, bias_rows, key_valid)
    mixed_rows = mixed_four.reshape(row_count, width)
    hidden = inputs + jnp.dot(mixed_rows, wo_full, preferred_element_type=jnp.float32)
    normed_ffn = rms_norm(hidden, ffn_gain).astype(jnp.bfloat16)
    up_rows = jnp.dot(normed_ffn, win_full, preferred_element_type=jnp.float32)
    activated = jax.nn.gelu(up_rows).astype(jnp.bfloat16)
    output_rows = hidden + jnp.dot(activated, wff_full, preferred_element_type=jnp.float32)
    pool_part = jnp.sum(
        output_rows.reshape(n_pass, local_rows, width)
        * query_valid[:, :, None].astype(jnp.float32),
        axis=1,
    )
    pooled = lax.psum(pool_part, "seq") / lengths[:, None].astype(jnp.float32)
    gathered = (
        lax.all_gather(w_query, "dp", axis=0, tiled=True),
        lax.all_gather(w_key, "dp", axis=0, tiled=True),
        lax.all_gather(w_value, "dp", axis=0, tiled=True),
        lax.all_gather(w_attn_out, "dp", axis=0, tiled=True),
        lax.all_gather(w_in, "dp", axis=0, tiled=True),
        lax.all_gather(w_ff_out, "dp", axis=0, tiled=True),
    )
    wq_full, wk_full, wv_full, wo_full, win_full, wff_full = gathered
    grad_out = cotangent.astype(jnp.float32).reshape(row_count, width)
    grad_branch = grad_out.astype(jnp.bfloat16)
    g_ff_out = jnp.einsum("rf,rd->fd", activated, grad_branch, preferred_element_type=jnp.float32)
    grad_act = jnp.einsum("rd,fd->rf", grad_branch, wff_full, preferred_element_type=jnp.float32)
    _, gelu_pull = jax.vjp(jax.nn.gelu, up_rows)
    grad_up = gelu_pull(grad_act)[0].astype(jnp.bfloat16)
    g_in = jnp.einsum("rd,rf->df", normed_ffn, grad_up, preferred_element_type=jnp.float32)
    grad_normed_ffn = jnp.einsum("rf,df->rd", grad_up, win_full, preferred_element_type=jnp.float32)
    _, ffn_pull = jax.vjp(rms_norm, hidden, ffn_gain)
    grad_hidden_norm, g_ffn_gain = ffn_pull(grad_normed_ffn)
    grad_hidden = grad_out + grad_hidden_norm
    grad_attn = grad_hidden.astype(jnp.bfloat16)
    g_attn_out = jnp.einsum("rd,re->de", mixed_rows, grad_attn, preferred_element_type=jnp.float32)
    grad_mixed = jnp.einsum("re,de->rd", grad_attn, wo_full, preferred_element_type=jnp.float32)
    grad_mixed = grad_mixed.astype(jnp.bfloat16).reshape(n_pass, local_rows, n_heads, head_dim)
    score_sum, (grad_query, grad_key, grad_value) = attend_backward(
        query_local, key_four, value_four, grad_mixed, log_total, key_valid, bias_rows
    )
    grad_key, grad_value = (
        lax.psum_scatter(
            grad_key.reshape(n_pass, full_len, width).astype(jnp.bfloat16),
            "seq",
            scatter_dimension=1,
            tiled=True,
        ).astype(jnp.float32),
        lax.psum_scatter(
            grad_value.reshape(n_pass, full_len, width).astype(jnp.bfloat16),
            "seq",
            scatter_dimension=1,
            tiled=True,
        ).astype(jnp.float32),
    )
    grad_query = grad_query.reshape(row_count, width)
    grad_key = grad_key.astype(jnp.bfloat16).reshape(row_count, width)
    grad_value = grad_value.astype(jnp.bfloat16).reshape(row_count, width)
    g_table = jnp.einsum("qkb,hqk->bh", one_hot, score_sum, precision=HIGH)
    g_query = jnp.einsum("rd,re->de", normed, grad_query, preferred_element_type=jnp.float32)
    g_key = jnp.einsum("rd,re->de", normed, grad_key, preferred_element_type=jnp.float32)
    g_value = jnp.einsum("rd,re->de", normed, grad_value, preferred_element_type=jnp.float32)
    grad_normed = jnp.einsum("re,de->rd", grad_query, wq_full, preferred_element_type=jnp.float32)
    grad_normed = grad_normed + jnp.einsum(
        "re,de->rd", grad_key, wk_full, preferred_element_type=jnp.float32
    )
    grad_normed = grad_normed + jnp.einsum(
        "re,de->rd", grad_value, wv_full, preferred_element_type=jnp.float32
    )
    _, attn_pull = jax.vjp(rms_norm, inputs, attn_gain)
    grad_inputs_norm, g_attn_gain = attn_pull(grad_normed)
    grad_input = (
        (grad_hidden + grad_inputs_norm).astype(jnp.bfloat16).reshape(n_pass, local_rows, width)
    )
    row_grads = (
        lax.psum_scatter(g_query, "dp", scatter_dimension=0, tiled=True),
        lax.psum_scatter(g_key, "dp", scatter_dimension=0, tiled=True),
        lax.psum_scatter(g_value, "dp", scatter_dimension=0, tiled=True),
        lax.psum_scatter(g_attn_out, "dp", scatter_dimension=0, tiled=True),
        lax.psum_scatter(g_in, "dp", scatter_dimension=0, tiled=True),
        lax.psum_scatter(g_ff_out, "dp", scatter_dimension=0, tiled=True),
    )
    row_grads = (
        lax.psum(row_grads[0].astype(jnp.bfloat16), "seq").astype(jnp.float32),
        lax.psum(row_grads[1].astype(jnp.bfloat16), "seq").astype(jnp.float32),
        lax.psum(row_grads[2].astype(jnp.bfloat16), "seq").astype(jnp.float32),
        lax.psum(row_grads[3].astype(jnp.bfloat16), "seq").astype(jnp.float32),
        lax.psum(row_grads[4].astype(jnp.bfloat16), "seq").astype(jnp.float32),
        lax.psum(row_grads[5].astype(jnp.bfloat16), "seq").astype(jnp.float32),
    )
    small_sums = lax.psum((g_attn_gain, g_ffn_gain, g_table), ("dp", "seq"))
    layer_out = output_rows.astype(jnp.bfloat16).reshape(n_pass, local_rows, width)
    return (
        layer_out,
        pooled,
        grad_input,
        small_sums[0],
        row_grads[0],
        row_grads[1],
        row_grads[2],
        row_grads[3],
        small_sums[2],
        small_sums[1],
        row_grads[4],
        row_grads[5],
    )


def solution(mesh):
    return jax.shard_map(
        shards,
        mesh=mesh,
        in_specs=(
            P("dp", "seq", None),
            P("dp"),
            P(),
            P("dp", None),
            P("dp", None),
            P("dp", None),
            P("dp", None),
            P(),
            P(),
            P("dp", None),
            P("dp", None),
            P("dp", "seq", None),
        ),
        out_specs=(
            P("dp", "seq", None),
            P("dp", None),
            P("dp", "seq", None),
            P(),
            P("dp", None),
            P("dp", None),
            P("dp", None),
            P("dp", None),
            P(),
            P(),
            P("dp", None),
            P("dp", None),
        ),
        check_vma=False,
    )
```

profile of v0, /device:TPU:0, one launch (start us, length us, event | category | flops | bytes accessed | tf_op | source)
XLA Modules:
  0.0 1246.7 jit_solution(2147909948730425185)
XLA Ops:
  12.2 41.8 %all-gather.9.cloned.1.call-done = bf16[768,768]{1,0:T(8,128)(2,1)} async-done(((bf16[96,768]{1,0:T(8,128)(2,1)}), bf16[768,768]{1,0:T(8,128)(2,1)}) %all-gather.9.cloned.1.call-update) | async-done | bytes 1179664 | tf_op jit(solution)/shard_map/all_gather | solution.py:108
  57.0 39.0 %all-gather.15.cloned.1.call-done = bf16[768,768]{1,0:T(8,128)(2,1)} async-done(((bf16[96,768]{1,0:T(8,128)(2,1)}), bf16[768,768]{1,0:T(8,128)(2,1)}) %all-gather.15.cloned.1.call-update) | async-done | bytes 1179664 | tf_op jit(solution)/shard_map/all_gather | solution.py:107
  103.2 37.9 %copy.41 = pred[128,512,32]{1,2,0:T(32,128)(4,1)S(1)} copy(pred[128,512,32]{0,2,1:T(32,128)(4,1)S(1)} %iota_compare_fusion) | data formatting | bytes 4194304 | tf_op jit(solution)/shard_map/eq | solution.py:126
  155.8 11.6 all-gather.11.cloned.1.call-done
  172.2 25.8 %all-gather.17.cloned.1.call-done = bf16[4,512,768]{2,1,0:T(8,128)(2,1)} async-done(((bf16[4,128,768]{2,1,0:T(8,128)(2,1)}), bf16[4,512,768]{2,1,0:T(8,128)(2,1)}) %all-gather.17.cloned.1.call-update) | async-done | bytes 3145744 | tf_op jit(solution)/shard_map/all_gather | solution.py:131
  219.6 21.5 %all-gather.19.cloned.1.call-done = bf16[768,768]{1,0:T(8,128)(2,1)} async-done(((bf16[96,768]{1,0:T(8,128)(2,1)}), bf16[768,768]{1,0:T(8,128)(2,1)}) %all-gather.19.cloned.1.call-update) | async-done | bytes 1179664 | tf_op jit(solution)/shard_map/all_gather | solution.py:109
  244.9 77.1 %all-gather.23.cloned.1.call-done = bf16[3072,768]{1,0:T(8,128)(2,1)} async-done(((bf16[384,768]{1,0:T(8,128)(2,1)}), bf16[3072,768]{1,0:T(8,128)(2,1)}) %all-gather.23.cloned.1.call-update) | async-done | bytes 4718608 | tf_op jit(solution)/shard_map/all_gather | solution.py:111
  322.0 7.9 fusion.81
  329.9 72.3 %all-gather.21.cloned.1.call-done = bf16[768,3072]{1,0:T(8,128)(2,1)} async-done(((bf16[96,3072]{1,0:T(8,128)(2,1)}), bf16[768,3072]{1,0:T(8,128)(2,1)}) %all-gather.21.cloned.1.call-update) | async-done | bytes 4718608 | tf_op jit(solution)/shard_map/all_gather | solution.py:110
  402.2 12.1 fusion.34
  427.9 50.3 %while.17 = (s32[]{:T(128)}, f32[12,128,512]{2,1,0:T(8,128)}, bf16[4,128,12,64]{1,3,2,0:T(8,128)(2,1)}, bf16[4,512,12,64]{1,3,2,0:T(8,128)(2,1)}, bf16[4,512,12,...) while((s32[]{:T(128)}, f32[12,128,512]{2,1,0:T(8,128)}, ...), condition=%wide.region_9.10_spmd.clone, body=%wide.region_7.0_spmd.clone.sunk | while | flops 512850432 | bytes 130784128 | solution.py:79
  495.3 23.9 %reduce-scatter.9.cloned.1.call-done = bf16[4,128,768]{2,1,0:T(8,128)(2,1)} async-done(((bf16[4,512,768]{2,1,0:T(8,128)(2,1)}), bf16[4,128,768]{2,1,0:T(8,128)(2,1)}) %reduce-scatter.9.cloned.1.call-update) | async-done | bytes 786448 | tf_op jit(solution)/shard_map/reduce_scatter | solution.py:177
  522.6 37.1 %reduce-scatter.11.cloned.1.call-done = bf16[4,128,768]{2,1,0:T(8,128)(2,1)} async-done(((bf16[4,512,768]{2,1,0:T(8,128)(2,1)}), bf16[4,128,768]{2,1,0:T(8,128)(2,1)}) %reduce-scatter.11.cloned.1.call-update) | async-done | bytes 786448 | tf_op jit(solution)/shard_map/reduce_scatter | solution.py:183
  563.1 7.1 fusion.77
  571.4 9.6 fusion.79
  586.5 9.3 fusion.80
  596.0 11.0 psum.70
  615.8 16.4 %reduce-scatter.13.cloned.1.call-done = f32[96,768]{1,0:T(8,128)} async-done(((f32[768,768]{1,0:T(8,128)}), f32[96,768]{1,0:T(8,128)}) %reduce-scatter.13.cloned.1.call-update) | async-done | bytes 294928 | tf_op jit(solution)/shard_map/reduce_scatter | solution.py:210
  633.8 69.8 %reduce-scatter.19.cloned.1.call-done = f32[96,768]{1,0:T(8,128)} async-done(((f32[768,768]{1,0:T(8,128)}), f32[96,768]{1,0:T(8,128)}) %reduce-scatter.19.cloned.1.call-update) | async-done | bytes 294928 | tf_op jit(solution)/shard_map/reduce_scatter | solution.py:213
  708.3 66.8 %reduce-scatter.15.cloned.1.call-done = f32[96,768]{1,0:T(8,128)} async-done(((f32[768,768]{1,0:T(8,128)}), f32[96,768]{1,0:T(8,128)}) %reduce-scatter.15.cloned.1.call-update) | async-done | bytes 294928 | tf_op jit(solution)/shard_map/reduce_scatter | solution.py:211
  776.8 69.8 %reduce-scatter.17.cloned.1.call-done = f32[96,768]{1,0:T(8,128)} async-done(((f32[768,768]{1,0:T(8,128)}), f32[96,768]{1,0:T(8,128)}) %reduce-scatter.17.cloned.1.call-update) | async-done | bytes 294928 | tf_op jit(solution)/shard_map/reduce_scatter | solution.py:212
  848.2 164.3 %reduce-scatter.21.cloned.1.call-done = f32[96,3072]{1,0:T(8,128)} async-done(((f32[768,3072]{1,0:T(8,128)}), f32[96,3072]{1,0:T(8,128)}) %reduce-scatter.21.cloned.1.call-update) | async-done | bytes 1179664 | tf_op jit(solution)/shard_map/reduce_scatter | solution.py:214
  1014.6 163.9 %reduce-scatter.23.cloned.1.call-done = f32[384,768]{1,0:T(8,128)} async-done(((f32[3072,768]{1,0:T(8,128)}), f32[384,768]{1,0:T(8,128)}) %reduce-scatter.23.cloned.1.call-update) | async-done | bytes 1179664 | tf_op jit(solution)/shard_map/reduce_scatter | solution.py:215
  1185.8 40.5 %all-reduce = (f32[768]{0:T(1024)}, f32[32,12]{0,1:T(8,128)}, f32[768]{0:T(1024)}) all-reduce(f32[768]{0:T(1024)} %get-tuple-element.146, f32[32,12]{0,1:T(8,128)S(1)} %convolution_bitcast_fusion.3, f32[768]{0:T(1024)} %get-tuple-element.144), channel_id=1, replica_groups=mesh['dp'=8,'seq'=4] {'dp','seq'}, use_global_device_ids=true, to_apply=%region_14.15 | all-reduce | flops 1920 | bytes 15360 | tf_op jit(solution)/shard_map/psum | solution.py:225
  (269 shorter events, 194.7 us)
Async XLA Ops:
  7.2 133.9 %copy-start = (f32[32,12]{0,1:T(8,128)S(1)}, f32[32,12]{0,1:T(8,128)}, u32[]{:S(2)}) copy-start(f32[32,12]{0,1:T(8,128)} %param.21) | copy-start | bytes 4612
  7.2 46.8 %all-gather.9.cloned.1.call-start = ((), (), s32[]{:S(2)}) async-start(), calls=%async_computation.8 | async-start | bytes 1327104 | tf_op jit(solution)/shard_map/all_gather | solution.py:108
  7.9 88.1 %all-gather.15.cloned.1.call-start = ((), (), s32[]{:S(2)}) async-start(), calls=%async_computation.11 | async-start | bytes 1327104 | tf_op jit(solution)/shard_map/all_gather | solution.py:107
  8.7 136.8 %all-gather.13.cloned.1.call-start = ((), (), s32[]{:S(2)}) async-start(), calls=%async_computation.10 | async-start | bytes 1327104 | tf_op jit(solution)/shard_map/all_gather | solution.py:106
  9.4 158.0 %all-gather.11.cloned.1.call-start = ((), (), s32[]{:S(2)}) async-start(), calls=%async_computation.9 | async-start | bytes 3932160 | tf_op jit(solution)/shard_map/all_gather | solution.py:132
  10.8 88.1 %copy-start.34 = (f32[512]{0:T(512)}, f32[512]{0:T(512)S(1)}, u32[]{:S(2)}) copy-start(f32[512]{0:T(512)S(1)} %bitcast_rsqrt_fusion) | copy-start | bytes 6148
  12.2 86.7 %copy-start.28 = (bf16[512,768]{1,0:T(8,128)(2,1)}, bf16[512,768]{1,0:T(8,128)(2,1)S(1)}, u32[]{:S(2)}) copy-start(bf16[512,768]{1,0:T(8,128)(2,1)S(1)} %fusion.41) | copy-start | bytes 2359300
  57.0 141.0 %all-gather.17.cloned.1.call-start = ((), (), s32[]{:S(2)}) async-start(), calls=%async_computation.12 | async-start | bytes 3932160 | tf_op jit(solution)/shard_map/all_gather | solution.py:131
  99.0 142.1 %all-gather.19.cloned.1.call-start = ((), (), s32[]{:S(2)}) async-start(), calls=%async_computation.13 | async-start | bytes 1327104 | tf_op jit(solution)/shard_map/all_gather | solution.py:109
  99.6 222.4 %all-gather.23.cloned.1.call-start = ((), (), s32[]{:S(2)}) async-start(), calls=%async_computation.15 | async-start | bytes 5308416 | tf_op jit(solution)/shard_map/all_gather | solution.py:111
  100.3 301.9 %all-gather.21.cloned.1.call-start = ((), (), s32[]{:S(2)}) async-start(), calls=%async_computation.14 | async-start | bytes 5308416 | tf_op jit(solution)/shard_map/all_gather | solution.py:110
  101.1 418.1 %reduce-scatter.9.cloned.1.call-start = ((), (), s32[]{:S(2)}) async-start(), calls=%async_computation.16 | async-start | bytes 3932160 | tf_op jit(solution)/shard_map/reduce_scatter | solution.py:177
  322.0 80.2 %copy-start.32 = (f32[768]{0:T(1024)S(1)}, f32[768]{0:T(1024)}, u32[]{:S(2)}) copy-start(f32[768]{0:T(1024)} %param.22) | copy-start | bytes 9220
  482.9 76.8 %reduce-scatter.11.cloned.1.call-start = ((), (), s32[]{:S(2)}) async-start(), calls=%async_computation.17 | async-start | bytes 3932160 | tf_op jit(solution)/shard_map/reduce_scatter | solution.py:183
  487.6 144.6 %reduce-scatter.13.cloned.1.call-start = ((), (), s32[]{:S(2)}) async-start(), calls=%async_computation.18 | async-start | bytes 2654208 | tf_op jit(solution)/shard_map/reduce_scatter | solution.py:210
  492.9 210.7 %reduce-scatter.19.cloned.1.call-start = ((), (), s32[]{:S(2)}) async-start(), calls=%async_computation.21 | async-start | bytes 2654208 | tf_op jit(solution)/shard_map/reduce_scatter | solution.py:213
  495.2 279.9 %reduce-scatter.15.cloned.1.call-start = ((), (), s32[]{:S(2)}) async-start(), calls=%async_computation.19 | async-start | bytes 2654208 | tf_op jit(solution)/shard_map/reduce_scatter | solution.py:211
  522.6 324.0 %reduce-scatter.17.cloned.1.call-start = ((), (), s32[]{:S(2)}) async-start(), calls=%async_computation.20 | async-start | bytes 2654208 | tf_op jit(solution)/shard_map/reduce_scatter | solution.py:212
  563.0 449.4 %reduce-scatter.21.cloned.1.call-start = ((), (), s32[]{:S(2)}) async-start(), calls=%async_computation.22 | async-start | bytes 10616832 | tf_op jit(solution)/shard_map/reduce_scatter | solution.py:214
  570.3 608.3 %reduce-scatter.23.cloned.1.call-start = ((), (), s32[]{:S(2)}) async-start(), calls=%async_computation.23 | async-start | bytes 10616832 | tf_op jit(solution)/shard_map/reduce_scatter | solution.py:215
  581.0 648.7 %all-reduce.4.cloned.1.call-start = ((), (), s32[]{:S(2)}) async-start(), calls=%async_computation.24 | async-start | bytes 3538944 | tf_op jit(solution)/shard_map/psum | solution.py:218
  613.8 91.4 %copy-start.40 = (bf16[768,768]{1,0:T(8,128)(2,1)S(1)}, bf16[768,768]{1,0:T(8,128)(2,1)}, u32[]{:S(2)}) copy-start(bf16[768,768]{1,0:T(8,128)(2,1)} %all-gather.15.cloned.1.call-done) | copy-start | bytes 3538948
  708.3 472.4 %copy-start.7 = (bf16[4,128,768]{2,1,0:T(8,128)(2,1)S(1)}, bf16[4,128,768]{2,1,0:T(8,128)(2,1)}, u32[]{:S(2)}) copy-start(bf16[4,128,768]{2,1,0:T(8,128)(2,1)} %param.14) | copy-start | bytes 2359300
  708.3 472.4 %copy-start.26 = (bf16[768,768]{1,0:T(8,128)(2,1)S(1)}, bf16[768,768]{1,0:T(8,128)(2,1)}, u32[]{:S(2)}) copy-start(bf16[768,768]{1,0:T(8,128)(2,1)} %all-gather.9.cloned.1.call-done) | copy-start | bytes 3538948
  (60 other events, 319.1 us)
Sparse Core Ops, SparseCore 0:
  10.2 43.7 all-gather.8
  56.2 39.8 all-gather.14
  98.2 39.8 all-gather.12
  140.1 27.2 all-gather.10
  169.4 28.5 all-gather.16
  200.0 41.0 all-gather.18
  243.3 78.6 all-gather.22
  324.1 78.0 all-gather.20
  483.0 36.0 reduce-scatter.8
  521.7 37.9 reduce-scatter.10
  563.2 68.9 reduce-scatter.12
  635.5 68.0 reduce-scatter.18
  707.1 68.0 reduce-scatter.14
  778.5 68.0 reduce-scatter.16
  850.0 162.4 reduce-scatter.20
  1015.9 162.5 reduce-scatter.22
  1182.3 47.4 all-reduce.3
where the time goes:
time: 1250 us
  waiting for transfers between devices  905 us (72%)
  matrix products  130 us (10%)
  local copies, waits for them, and re-layouts  105 us (8%)
  blocking collectives  51.5 us (4%)
  other arithmetic  38 us (3%)
  between operations  14.9 us (1%)
    reduce_scatter x1, waiting for transfers between devices, shards(): lax.psum_scatter(g_in, 'dp', scatter_dimension=0, tiled=True)  164 us
    reduce_scatter x1, waiting for transfers between devices, shards(): lax.psum_scatter(g_ff_out, 'dp', scatter_dimension=0, tiled=True)  164 us
    all_gather x1, waiting for transfers between devices, shards(): lax.all_gather(w_ff_out, 'dp', axis=0, tiled=True)  77.1 us
    all_gather x1, waiting for transfers between devices, shards(): lax.all_gather(w_in, 'dp', axis=0, tiled=True)  72.3 us
    reduce_scatter x1, waiting for transfers between devices, shards(): lax.psum_scatter(g_attn_out, 'dp', scatter_dimension=0, tiled=True)  69.8 us
    reduce_scatter x1, waiting for transfers between devices, shards(): lax.psum_scatter(g_value, 'dp', scatter_dimension=0, tiled=True)  69.8 us
    reduce_scatter x1, waiting for transfers between devices, shards(): lax.psum_scatter(g_key, 'dp', scatter_dimension=0, tiled=True)  66.8 us
    all_gather x1, waiting for transfers between devices, shards(): lax.all_gather(w_value, 'dp', axis=0, tiled=True)  41.8 us
  transfers between devices with their start and end apart: 17, of which 15 were waited for; matrix products, arithmetic and copies ran while one was open for 14% of the time, Pallas kernels for 0%

commit v1 on v0

--- a/solution.py
+++ b/solution.py
@@ -3,6 +3,8 @@
 import jax
 import jax.numpy as jnp
 from jax import lax
+from jax.experimental import pallas as pl
+from jax.experimental.pallas import tpu as pltpu
 from jax.sharding import PartitionSpec as P
 
 MAXDIST = 128
@@ -240,9 +242,736 @@
     )
 
 
+DP, SEQ = 8, 4
+LAST = DP - 1
+BF, F32 = jnp.bfloat16, jnp.float32
+MESH_ID = pl.DeviceIdType.MESH
+TOKENS, WIDTH, HIDDEN, HEAD_N = 512, 768, 3072, 12
+PAIRS = HEAD_N // 2
+GELU_A, GELU_B = math.sqrt(2 / math.pi), 0.044715
+
+
+def dg(left, right, on_left, on_right):
+    return lax.dot_general(
+        left, right, (((on_left,), (on_right,)), ((), ())), preferred_element_type=F32
+    )
+
+
+def ring_dp(place):
+    high = place // 4
+    return 2 * (place * (1 - high) + (7 - place) * high) + high
+
+
+def times(start, size, step):
+    return pl.ds(pl.multiple_of(start, step), size)
+
+
+def band_bucket(n_buckets):
+    lane = lax.broadcasted_iota(jnp.int32, (n_buckets, 512), 1)
+    relative = jnp.where(lane < 384, lane - 128, lane - 640)
+    row = lax.broadcasted_iota(jnp.int32, (n_buckets, 512), 0)
+    return (bucket_index(relative, n_buckets, MAXDIST) == row).astype(F32)
+
+
+def layer_kernel(
+    x_hbm, cot_hbm, wq_hbm, wk_hbm, wv_hbm, wo_hbm, win_hbm, wff_hbm, lengths, attn_gain, ffn_gain, table,
+    out_hbm, gx_hbm, gatt_hbm, gin_hbm, gff_hbm, pool_hbm, small_out,
+    watt, win, wff, gin, gff, big, probs, xs, cot, normed, qkv, mixed, nf, lay, hid, acc, band, diag,
+    sib_ff, y_ff, y_in, y_att, r_ffa, r_ffb, r_ina, r_inb, r_ata, r_atb, f_ff, f_in, f_att, sums, sums_in, pool,
+    ag_s, ag_r, sb_s, sb_r, yf_s, yf_r, yb_s, yb_r, rr_s, rr_r, loc, a2_s, a2_r, hs_s, hs_r, yx_s, yx_r,
+    fa_s, fa_r, fo_s, fo_r, fl, bf_s, bf_r, free_sem,
+):
+    dp, sq = lax.axis_index("dp"), lax.axis_index("seq")
+    z, x, y, c = dp // 2, dp % 2, sq // 2, sq % 2
+    place = x * (7 - z) + (1 - x) * z
+    turn = 1 - 2 * c
+
+    def owner(steps):
+        return ring_dp((place + steps * turn + 16) % 8)
+
+    nxt, prv = (owner(1), sq), (owner(-1), sq)
+    sib, yp, ysib = (dp, 2 * y + 1 - c), (dp, 2 * (1 - y) + c), (dp, 2 * (1 - y) + 1 - c)
+    xp = (2 * z + 1 - x, sq)
+    z1 = (2 * (z + 1 - 2 * (z % 2)) + x, sq)
+    z2 = (2 * ((z + 2) % 4) + x, sq)
+    peers = (sib, yp, ysib)
+
+    def send(src, dst, ss, rs, dev):
+        return pltpu.make_async_remote_copy(
+            src_ref=src, dst_ref=dst, send_sem=ss, recv_sem=rs, device_id=dev, device_id_type=MESH_ID
+        )
+
+    barrier = pltpu.get_barrier_semaphore()
+    for dev in (sib, yp, ysib, nxt, prv, xp, z1, z2):
+        pl.semaphore_signal(barrier, inc=1, device_id=dev, device_id_type=MESH_ID)
+
+    r96 = times(96 * dp, 96, 96)
+    own = [pltpu.make_async_copy(w, watt.at[i, r96], loc.at[i]) for i, w in enumerate((wq_hbm, wk_hbm, wv_hbm, wo_hbm))]
+    own.append(pltpu.make_async_copy(win_hbm, win.at[r96], loc.at[4]))
+    own.append(pltpu.make_async_copy(wff_hbm, wff.at[times(384 * dp, 384, 384)], loc.at[5]))
+    mine = times(128 * sq, 128, 128)
+    own.append(pltpu.make_async_copy(x_hbm.at[sq], xs.at[mine], loc.at[6]))
+    own.append(pltpu.make_async_copy(cot_hbm.at[sq], cot.at[mine], loc.at[7]))
+    for copy in own:
+        copy.start()
+    pl.semaphore_wait(barrier, 8)
+
+    def swap(k, src_hbm, dst, at):
+        dev = peers[k]
+        return send(src_hbm.at[dev[1]], dst.at[mine], a2_s.at[at, k], a2_r.at[at, k], dev)
+
+    def swap_wait(dst, at):
+        for k in range(3):
+            theirs = dst.at[times(128 * peers[k][1], 128, 128)]
+            send(theirs, theirs, a2_s.at[at, k], a2_r.at[at, k], peers[k]).wait_recv()
+
+    for k in range(3):
+        swap(k, x_hbm, xs, 0).start()
+
+    def piece(ch, d, cc, yy):
+        if ch < 2:
+            cols = pl.ds(256, 256) if ch == 0 else times(512 * yy, 256, 256)
+            return watt.at[:, times(96 * d + 48 * cc, 48, 48), cols]
+        if ch < 4:
+            cols = pl.ds(1024, 1024) if ch == 2 else times(2048 * yy, 1024, 1024)
+            return win.at[times(96 * d + 48 * cc, 48, 48), cols]
+        cols = pl.ds(256, 256) if ch == 4 else times(512 * yy, 256, 256)
+        return wff.at[times(384 * d + 192 * cc, 192, 192), cols]
+
+    def ring_send(ch, s):
+        part = piece(ch, owner(-s), c, y)
+        return send(part, part, ag_s.at[ch, s], ag_r.at[ch, s], nxt)
+
+    def hand_on(ch, s):
+        part = piece(ch, owner(-s - 1), c, y)
+        return send(part, part, sb_s.at[ch, s], sb_r.at[ch, s], sib)
+
+    def cross(ch, s):
+        part = piece(ch, owner(-s - 1), c, y)
+        return send(part, part, yf_s.at[ch // 2, s], yf_r.at[ch // 2, s], yp)
+
+    def cross_on(ch, s):
+        part = piece(ch, owner(-s - 1), c, 1 - y)
+        return send(part, part, yb_s.at[ch // 2, s], yb_r.at[ch // 2, s], sib)
+
+    def tick(ch, s):
+        part = piece(ch, owner(-s - 1), c, y)
+        send(part, part, ag_s.at[ch, s], ag_r.at[ch, s], nxt).wait_recv()
+
+        @pl.when(s < LAST - 1)
+        def _():
+            ring_send(ch, s + 1).start()
+
+        hand_on(ch, s).start()
+        if ch % 2:
+            cross(ch, s).start()
+
+    def cross_tick(ch, s):
+        part = piece(ch, owner(-s - 1), c, 1 - y)
+        send(part, part, yf_s.at[ch // 2, s], yf_r.at[ch // 2, s], yp).wait_recv()
+        cross_on(ch, s).start()
+
+    def gathered(group):
+        def step(s, _):
+            d = owner(s + 1)
+            for ch in (2 * group, 2 * group + 1):
+                part = piece(ch, d, 1 - c, y)
+                send(part, part, sb_s.at[ch, s], sb_r.at[ch, s], sib).wait_recv()
+            part = piece(2 * group + 1, d, 1 - c, 1 - y)
+            send(part, part, yb_s.at[group, s], yb_r.at[group, s], sib).wait_recv()
+            return 0
+
+        lax.fori_loop(0, LAST, step, 0)
+
+    def gather_sent():
+        def step(s, _):
+            for ch in range(6):
+                ring_send(ch, s).wait_send()
+                hand_on(ch, s).wait_send()
+                if ch % 2:
+                    cross(ch, s).wait_send()
+                    cross_on(ch, s).wait_send()
+            return 0
+
+        lax.fori_loop(0, LAST, step, 0)
+
+    for i in range(5):
+        own[i].wait()
+    for ch in (0, 1, 2):
+        ring_send(ch, 0).start()
+    own[5].wait()
+    for k in range(3):
+        swap(k, cot_hbm, cot, 1).start()
+
+    one_hot = band_bucket(32)
+    band[pl.ds(0, HEAD_N), :] = lax.dot_general(
+        table[...], one_hot, (((0,), (0,)), ((), ())), precision=HIGH, preferred_element_type=F32
+    )
+
+    own[6].wait()
+    swap_wait(xs, 0)
+
+    def norm_rows(src, gain, dst):
+        def step(b, _):
+            rows = times(128 * b, 128, 128)
+            v = src[rows, :].astype(F32)
+            s = lax.rsqrt(jnp.mean(v * v, axis=-1, keepdims=True) + EPS)
+            dst[rows, :] = (v * s * gain[...]).astype(BF)
+            return 0
+
+        lax.fori_loop(0, 4, step, 0)
+
+    norm_rows(xs, attn_gain, normed)
+
+    def first_steps(s, _):
+        tick(1, s)
+        tick(0, s)
+
+        @pl.when(s > 0)
+        def _():
+            cross_tick(1, s - 1)
+
+        tick(2, s)
+
+        @pl.when(s == LAST - 2)
+        def _():
+            ring_send(3, 0).start()
+            ring_send(5, 0).start()
+
+        return 0
+
+    lax.fori_loop(0, LAST, first_steps, 0)
+    ring_send(4, 0).start()
+    cross_tick(1, LAST - 1)
+    gathered(0)
+
+    def later_steps(s):
+        tick(3, s)
+        tick(5, s)
+
+        @pl.when(s > 0)
+        def _():
+            cross_tick(3, s - 1)
+            cross_tick(5, s - 1)
+
+        tick(4, s)
+
+    def project(m, _):
+        qkv[m] = dg(normed[...], watt[m], 1, 0).astype(BF)
+        return 0
+
+    lax.fori_loop(0, 3, project, 0)
+    later_steps(0)
+
+    count = lengths[sq]
+    valid = lax.broadcasted_iota(jnp.int32, (1, TOKENS), 1) < count
+    lane = lax.broadcasted_iota(jnp.int32, (1, 128), 1)
+    keep = (lane < 64, lane >= 64)
+
+    def only(h, v):
+        return jnp.where(keep[h], v, jnp.zeros_like(v))
+
+    def attend(hp, _):
+        cols = times(128 * hp, 128, 128)
+        key, value = qkv[1, :, cols], qkv[2, :, cols]
+        total = [None] * 4
+        for h in range(2):
+            row = band[pl.ds(2 * hp + h, 1), :]
+            tilted = pltpu.roll(jnp.broadcast_to(row, (128, 512)), 0, 1, stride=1, stride_axis=0)
+            before = jnp.broadcast_to(row[:, 384:], (128, 128))
+            after = jnp.broadcast_to(row[:, 256:384], (128, 128))
+            value_h = only(h, value)
+            for ib in range(4):
+                rows = pl.ds(128 * ib, 128)
+                blocks = []
+                for jb in range(4):
+                    off = jb - ib
+                    if off < -1:
+                        blocks.append(before)
+                    elif off > 1:
+                        blocks.append(after)
+                    else:
+                        blocks.append(tilted[:, 128 * (off + 1) : 128 * (off + 2)])
+                scores = dg(only(h, qkv[0, rows, cols]), key, 1, 1) + jnp.concatenate(blocks, axis=1)
+                scores = jnp.where(valid, scores, FLOOR)
+                top = jnp.max(scores, axis=-1, keepdims=True)
+                expo = jnp.exp(scores - top)
+                part = jnp.sum(expo, axis=-1, keepdims=True)
+                low = (expo * (1.0 / part)).astype(BF)
+                probs[2 * hp + h, rows, :] = low
+                one = dg(low, value_h, 1, 0)
+                total[ib] = one if h == 0 else total[ib] + one
+        for ib in range(4):
+            mixed[pl.ds(128 * ib, 128), cols] = total[ib].astype(BF)
+        later_steps(hp + 1)
+        return 0
+
+    lax.fori_loop(0, PAIRS, attend, 0)
+    cross_tick(3, LAST - 1)
+    cross_tick(5, LAST - 1)
+
+    def residual(b, _):
+        rows = times(128 * b, 128, 128)
+        v = xs[rows, :].astype(F32) + dg(mixed[rows, :], watt[3], 1, 0)
+        hid[rows, :] = v
+        s = lax.rsqrt(jnp.mean(v * v, axis=-1, keepdims=True) + EPS)
+        nf[rows, :] = (v * s * ffn_gain[...]).astype(BF)
+        return 0
+
+    lax.fori_loop(0, 4, residual, 0)
+
+    gathered(1)
+    up_rows, down_rows = pl.ds(0, TOKENS), pl.ds(TOKENS, TOKENS)
+
+    def block(j):
+        return times(768 * j, 768, 768)
+
+    def widen(j, _):
+        v = dg(nf[...], win[:, block(j)], 1, 0)
+        sq_v = v * v
+        t = jnp.tanh(v * (GELU_A + (GELU_A * GELU_B) * sq_v))
+        half = 0.5 + 0.5 * t
+        big[j, up_rows, :] = (v * half).astype(BF)
+        slope = half + (v * half) * (1.0 - t) * (GELU_A + (3 * GELU_A * GELU_B) * sq_v)
+        big[j, down_rows, :] = slope.astype(BF)
+        return 0
+
+    lax.fori_loop(0, 4, widen, 0)
+    own[7].wait()
+    swap_wait(cot, 1)
+
+    def half_ff(d2, cc):
+        return gff.at[pl.ds(d2, 2), :, times(384 * cc, 384, 384)]
+
+    def grad_ff(j, _):
+        v = dg(big[j, up_rows, :], cot[...], 0, 0).astype(BF)
+        gff[pl.ds(2 * j, 2)] = v.reshape(2, 384, 768)
+        send(half_ff(2 * j, 1 - c), sib_ff.at[pl.ds(2 * j, 2)], hs_s.at[0, j], hs_r.at[0, j], sib).start()
+        return 0
+
+    lax.fori_loop(0, 4, grad_ff, 0)
+    gathered(2)
+
+    def grad_up(j, _):
+        v = dg(cot[...], wff[block(j), :], 1, 1) * big[j, down_rows, :].astype(F32)
+        big[j, down_rows, :] = v.astype(BF)
+        return 0
+
+    lax.fori_loop(0, 4, grad_up, 0)
+
+    def merge_ff(j, _):
+        send(half_ff(2 * j, 1 - c), sib_ff.at[pl.ds(2 * j, 2)], hs_s.at[0, j], hs_r.at[0, j], sib).wait()
+        cols = times(384 * c, 384, 384)
+        for i in range(2):
+            gff[2 * j + i, :, cols] = (gff[2 * j + i, :, cols].astype(F32) + sib_ff[2 * j + i].astype(F32)).astype(BF)
+        return 0
+
+    lax.fori_loop(0, 4, merge_ff, 0)
+
+    def cross_src(g, yy):
+        if g == 0:
+            return gff.at[:, times(320 * yy, 64, 64), times(384 * c, 384, 384)]
+        if g == 1:
+            return gin.at[:, times(1536 * c + 1280 * yy, 256, 256)]
+        return big.at[:, pl.ds(0, 768), times(384 * c + 256 * yy, 128, 128)]
+
+    cross_dst = (y_ff, y_in, y_att)
+
+    def cross_sum(g):
+        return send(cross_src(g, 1 - y), cross_dst[g], yx_s.at[g], yx_r.at[g], yp)
+
+    def add_cross(g):
+        cross_sum(g).wait()
+        here, came = cross_src(g, y), cross_dst[g]
+        here[...] = (here[...].astype(F32) + came[...].astype(F32)).astype(BF)
+
+    def rs_piece(ch, d, yy):
+        if ch < 2:
+            rows = pl.ds(64, 256) if ch == 0 else times(320 * yy, 64, 64)
+            return gff.at[d, rows, times(384 * c, 384, 384)]
+        rows = times(96 * d, 96, 96)
+        if ch < 4:
+            cols = times(1536 * c + 256, 1024, 256) if ch == 2 else times(1536 * c + 1280 * yy, 256, 256)
+            return gin.at[rows, cols]
+        cols = times(384 * c + 128, 128, 128) if ch == 4 else times(384 * c + 256 * yy, 128, 128)
+        return big.at[:, rows, cols]
+
+    landing = (r_ffa, r_ffb, r_ina, r_inb, r_ata, r_atb)
+
+    def rs_send(ch, s):
+        return send(rs_piece(ch, owner(-s - 1), y), landing[ch].at[s], rr_s.at[ch, s], rr_r.at[ch, s], nxt)
+
+    def rs_tick(ch, s):
+        rs_send(ch, s).wait_recv()
+        here = rs_piece(ch, owner(-s - 2), y)
+        here[...] = (here[...].astype(F32) + landing[ch][s].astype(F32)).astype(BF)
+
+        @pl.when(s < LAST - 1)
+        def _():
+            rs_send(ch, s + 1).start()
+
+    def rs_sent(ch):
+        def step(s, _):
+            rs_send(ch, s).wait_send()
+            return 0
+
+        lax.fori_loop(0, LAST, step, 0)
+
+    cross_sum(0).start()
+    rs_send(0, 0).start()
+    add_cross(0)
+    rs_send(1, 0).start()
+
+    acc[...] = hid[...]
+
+    def narrow(j, _):
+        acc[...] += dg(big[j, up_rows, :], wff[block(j), :], 1, 0)
+        return 0
+
+    lax.fori_loop(0, 4, narrow, 0)
+    lay[...] = acc[...].astype(BF)
+
+    def give(src, dst_hbm, at, k):
+        dev = peers[k]
+        return send(src.at[times(128 * dev[1], 128, 128)], dst_hbm.at[sq], a2_s.at[at, k], a2_r.at[at, k], dev)
+
+    def give_wait(src, dst_hbm, at):
+        for k in range(3):
+            give(src, dst_hbm, at, k).wait_send()
+            theirs = dst_hbm.at[peers[k][1]]
+            send(theirs, theirs, a2_s.at[at, k], a2_r.at[at, k], peers[k]).wait_recv()
+
+    for k in range(3):
+        give(lay, out_hbm, 2, k).start()
+    lay_own = pltpu.make_async_copy(lay.at[mine], out_hbm.at[sq], loc.at[0])
+    lay_own.start()
+    here_t = lax.broadcasted_iota(jnp.int32, (TOKENS, 1), 0) < count
+    mean = jnp.sum(jnp.where(here_t, acc[...], 0.0), axis=0, keepdims=True) / count.astype(F32)
+    pool[...] = jnp.broadcast_to(mean, (8, WIDTH))
+    pool_own = pltpu.make_async_copy(pool, pool_hbm.at[sq], loc.at[1])
+    pool_own.start()
+
+    def pool_send(k):
+        return send(pool, pool_hbm.at[sq], a2_s.at[4, k], a2_r.at[4, k], peers[k])
+
+    for k in range(3):
+        pool_send(k).start()
+
+    gather_sent()
+    pl.semaphore_signal(free_sem, inc=1, device_id=sib, device_id_type=MESH_ID)
+
+    def grad_in(j, _):
+        gin[:, block(j)] = dg(nf[...], big[j, down_rows, :], 0, 0).astype(BF)
+        return 0
+
+    lax.fori_loop(0, 4, grad_in, 0)
+    pl.semaphore_wait(free_sem, 1)
+
+    def half_in(k):
+        src = gin.at[:, times(1536 * (1 - c) + 384 * k, 384, 384)]
+        return send(src, wff.at[times(768 * k, 768, 768), pl.ds(384, 384)], hs_s.at[1, k], hs_r.at[1, k], sib)
+
+    for k in range(4):
+        half_in(k).start()
+
+    acc[...] = jnp.zeros_like(acc)
+
+    def grad_nf(j, _):
+        acc[...] += dg(big[j, down_rows, :], win[:, block(j)], 1, 1)
+        return 0
+
+    lax.fori_loop(0, 4, grad_nf, 0)
+
+    for k in range(4):
+        half_in(k).wait()
+        cols = times(1536 * c + 384 * k, 384, 384)
+        gin[:, cols] = (gin[:, cols].astype(F32) + wff[pl.ds(768 * k, 768), pl.ds(384, 384)].astype(F32)).astype(BF)
+    cross_sum(1).start()
+    rs_send(2, 0).start()
+
+    def norm_back(v, gain, grad):
+        s = lax.rsqrt(jnp.mean(v * v, axis=-1, keepdims=True) + EPS)
+        scaled = grad * gain
+        back = s * scaled - v * (s * s * s) * jnp.mean(v * scaled, axis=-1, keepdims=True)
+        return back, jnp.sum(grad * v * s, axis=0, keepdims=True)
+
+    def ffn_norm_back(b, total):
+        rows = times(128 * b, 128, 128)
+        back, part = norm_back(hid[rows, :], ffn_gain[...], acc[rows, :])
+        v = cot[rows, :].astype(F32) + back
+        hid[rows, :] = v
+        cot[rows, :] = v.astype(BF)
+        return total + part
+
+    g_ffn_gain = lax.fori_loop(0, 4, ffn_norm_back, jnp.zeros((1, WIDTH), F32))
+
+    add_cross(1)
+    rs_send(3, 0).start()
+
+    big[3, pl.ds(0, 768), :] = dg(mixed[...], cot[...], 0, 0).astype(BF)
+    nf[...] = dg(cot[...], watt[3], 1, 1).astype(BF)
+
+    flip_sum = lax.broadcasted_iota(jnp.int32, (128, 128), 0) + lax.broadcasted_iota(jnp.int32, (128, 128), 1)
+    flip = (flip_sum == 127).astype(F32)
+
+    def attend_back(hp, _):
+        cols = times(128 * hp, 128, 128)
+        key, value = qkv[1, :, cols], qkv[2, :, cols]
+        g_key = g_value = jnp.zeros((TOKENS, 128), F32)
+        g_query = [None] * 4
+        for h in range(2):
+            key_h = only(h, key)
+            before = after = jnp.zeros((128, 128), F32)
+            near = [jnp.zeros((128, 128), F32) for _ in range(3)]
+            for ib in range(4):
+                rows = pl.ds(128 * ib, 128)
+                grad_h = only(h, nf[rows, cols])
+                low = probs[2 * hp + h, rows, :]
+                wide = low.astype(F32)
+                d_probs = dg(grad_h, value, 1, 1)
+                mean_d = jnp.sum(wide * d_probs, axis=-1, keepdims=True)
+                d_score = wide * (d_probs - mean_d)
+                for jb in range(4):
+                    off, part = jb - ib, d_score[:, 128 * jb : 128 * (jb + 1)]
+                    if off < -1:
+                        before = before + part
+                    elif off > 1:
+                        after = after + part
+                    else:
+                        near[off + 1] = near[off + 1] + part
+                d_low = d_score.astype(BF)
+                one = dg(d_low, key_h, 1, 0)
+                g_query[ib] = one if h == 0 else g_query[ib] + one
+                g_key = g_key + dg(d_low, only(h, qkv[0, rows, cols]), 0, 0)
+                g_value = g_value + dg(low, grad_h, 0, 0)
+            tilted = lax.dot_general(
+                flip, jnp.concatenate(near, axis=1), (((1,), (0,)), ((), ())), precision=HIGH, preferred_element_type=F32
+            )
+            tilted = jnp.concatenate([tilted, jnp.zeros((128, 128), F32)], axis=1)
+            flat = jnp.sum(pltpu.roll(tilted, 385, 1, stride=1, stride_axis=0), axis=0, keepdims=True)
+            far = jnp.concatenate(
+                [
+                    jnp.zeros((1, 256), F32),
+                    jnp.sum(after, axis=0, keepdims=True),
+                    jnp.sum(before, axis=0, keepdims=True),
+                ],
+                axis=1,
+            )
+            diag[pl.ds(2 * hp + h, 1), :] = flat + far
+        for ib in range(4):
+            qkv[0, pl.ds(128 * ib, 128), cols] = g_query[ib].astype(BF)
+        qkv[1, :, cols] = g_key.astype(BF)
+        qkv[2, :, cols] = g_value.astype(BF)
+        return 0
+
+    lax.fori_loop(0, PAIRS, attend_back, 0)
+
+    def grad_project(m, _):
+        big[m, pl.ds(0, 768), :] = dg(normed[...], qkv[m], 0, 0).astype(BF)
+        return 0
+
+    lax.fori_loop(0, 3, grad_project, 0)
+
+    def half_att(m):
+        src = big.at[m, pl.ds(0, 768), times(384 * (1 - c), 384, 384)]
+        return send(src, wff.at[times(768 * m, 768, 768), pl.ds(0, 384)], hs_s.at[2, m], hs_r.at[2, m], sib)
+
+    for m in range(4):
+        half_att(m).start()
+
+    acc[...] = jnp.zeros_like(acc)
+
+    def grad_normed(m, _):
+        acc[...] += dg(qkv[m], watt[m], 1, 1)
+        return 0
+
+    lax.fori_loop(0, 3, grad_normed, 0)
+
+    for m in range(4):
+        half_att(m).wait()
+        cols = times(384 * c, 384, 384)
+        rows = pl.ds(0, 768)
+        big[m, rows, cols] = (
+            big[m, rows, cols].astype(F32) + wff[pl.ds(768 * m, 768), pl.ds(0, 384)].astype(F32)
+        ).astype(BF)
+    cross_sum(2).start()
+    rs_send(4, 0).start()
+
+    def attn_norm_back(b, total):
+        rows = times(128 * b, 128, 128)
+        back, part = norm_back(xs[rows, :].astype(F32), attn_gain[...], acc[rows, :])
+        mixed[rows, :] = (hid[rows, :] + back).astype(BF)
+        return total + part
+
+    g_attn_gain = lax.fori_loop(0, 4, attn_norm_back, jnp.zeros((1, WIDTH), F32))
+    for k in range(3):
+        give(mixed, gx_hbm, 3, k).start()
+    gx_own = pltpu.make_async_copy(mixed.at[mine], gx_hbm.at[sq], loc.at[2])
+    gx_own.start()
+
+    add_cross(2)
+    rs_send(5, 0).start()
+
+    sums[0] = jnp.zeros((48, 128), F32)
+    diag_all = diag[...]
+    sums[0, 0:32, 0:16] = lax.dot_general(
+        band_bucket(32), diag_all, (((1,), (1,)), ((), ())), precision=HIGH, preferred_element_type=F32
+    )
+    for k in range(6):
+        sums[0, 32 + k : 33 + k, :] = g_attn_gain[:, 128 * k : 128 * (k + 1)]
+        sums[0, 38 + k : 39 + k, :] = g_ffn_gain[:, 128 * k : 128 * (k + 1)]
+    for k, dev in enumerate((sib, yp, xp, z1, z2)):
+        copy = send(sums.at[k], sums_in.at[k], bf_s.at[k], bf_r.at[k], dev)
+        copy.start()
+        copy.wait()
+        sums[k + 1] = sums[k] + sums_in[k]
+    small_out[...] = sums[5]
+
+    def rounds(s, _):
+        for ch in range(6):
+            rs_tick(ch, s)
+        return 0
+
+    lax.fori_loop(0, LAST, rounds, 0)
+
+    def out_piece(g, cc, yy):
+        if g == 0:
+            rows = pl.ds(64, 256) if yy is None else times(320 * yy, 64, 64)
+            return gff_hbm.at[rows, times(384 * cc, 384, 384)]
+        if g == 1:
+            if yy is None:
+                return gin_hbm.at[:, times(1536 * cc + 256, 1024, 256)]
+            return gin_hbm.at[:, times(1536 * cc + 1280 * yy, 256, 256)]
+        if yy is None:
+            return gatt_hbm.at[:, :, times(384 * cc + 128, 128, 128)]
+        return gatt_hbm.at[:, :, times(384 * cc + 256 * yy, 128, 128)]
+
+    final = (f_ff, f_in, f_att)
+
+    def share_a(g):
+        return send(rs_piece(2 * g, dp, y), final[g], fa_s.at[g], fa_r.at[g], yp)
+
+    def share_b(g, k):
+        return send(rs_piece(2 * g + 1, dp, y), out_piece(g, c, y), fo_s.at[g, k], fo_r.at[g, k], peers[k])
+
+    def share_sum(g):
+        return send(final[g], out_piece(g, c, None), fo_s.at[g, 3], fo_r.at[g, 3], sib)
+
+    def keep_b(g):
+        return pltpu.make_async_copy(rs_piece(2 * g + 1, dp, y), out_piece(g, c, y), fl.at[g, 0])
+
+    def keep_sum(g):
+        return pltpu.make_async_copy(final[g], out_piece(g, c, None), fl.at[g, 1])
+
+    for g in range(3):
+        share_a(g).start()
+        for k in range(3):
+            share_b(g, k).start()
+        keep_b(g).start()
+    for g in range(3):
+        share_a(g).wait()
+        here = rs_piece(2 * g, dp, y)
+        final[g][...] = (final[g][...].astype(F32) + here[...].astype(F32)).astype(BF)
+        share_sum(g).start()
+        keep_sum(g).start()
+    for g in range(3):
+        keep_b(g).wait()
+        keep_sum(g).wait()
+        for k, (cc, yy) in enumerate(((1 - c, y), (c, 1 - y), (1 - c, 1 - y))):
+            share_b(g, k).wait_send()
+            came = out_piece(g, cc, yy)
+            send(came, came, fo_s.at[g, k], fo_r.at[g, k], peers[k]).wait_recv()
+        share_sum(g).wait_send()
+        came = out_piece(g, 1 - c, None)
+        send(came, came, fo_s.at[g, 3], fo_r.at[g, 3], sib).wait_recv()
+    for ch in range(6):
+        rs_sent(ch)
+    give_wait(lay, out_hbm, 2)
+    give_wait(mixed, gx_hbm, 3)
+    lay_own.wait()
+    gx_own.wait()
+    pool_own.wait()
+    for k in range(3):
+        pool_send(k).wait_send()
+        theirs = pool_hbm.at[peers[k][1]]
+        send(theirs, theirs, a2_s.at[4, k], a2_r.at[4, k], peers[k]).wait_recv()
+        swap(k, x_hbm, xs, 0).wait_send()
+        swap(k, cot_hbm, cot, 1).wait_send()
+
+
+def passage_shards(
+    passages, lengths, attn_gain, w_query, w_key, w_value, w_attn_out, bias_table, ffn_gain, w_in, w_ff_out, cotangent
+):
+    any_space = pl.BlockSpec(memory_space=pl.ANY)
+    vmem = pl.BlockSpec(memory_space=pltpu.VMEM)
+    dma = pltpu.SemaphoreType.DMA
+    scratch = [
+        pltpu.VMEM(shape, BF)
+        for shape in (
+            (4, 768, 768), (768, 3072), (3072, 768), (768, 3072), (8, 384, 768), (4, 1024, 768), (12, 512, 512),
+            (512, 768), (512, 768), (512, 768), (3, 512, 768), (512, 768), (512, 768), (512, 768),
+        )
+    ]
+    scratch += [pltpu.VMEM(shape, F32) for shape in ((512, 768), (512, 768), (16, 512), (16, 512))]
+    scratch += [
+        pltpu.VMEM(shape, BF)
+        for shape in (
+            (8, 384, 384), (8, 64, 384), (768, 256), (4, 768, 128),
+            (7, 256, 384), (7, 64, 384), (7, 96, 1024), (7, 96, 256), (7, 4, 96, 128), (7, 4, 96, 128),
+            (256, 384), (96, 1024), (4, 96, 128),
+        )
+    ]
+    scratch += [pltpu.VMEM((6, 48, 128), F32), pltpu.VMEM((5, 48, 128), F32), pltpu.VMEM((8, 768), F32)]
+    scratch += [
+        dma(shape)
+        for shape in (
+            (6, 7), (6, 7), (6, 7), (6, 7), (3, 7), (3, 7), (3, 7), (3, 7), (6, 7), (6, 7), (8,), (5, 3), (5, 3),
+            (3, 4), (3, 4), (3,), (3,), (3,), (3,), (3, 4), (3, 4), (3, 2), (5,), (5,),
+        )
+    ]
+    scratch.append(pltpu.SemaphoreType.REGULAR)
+    outs = pl.pallas_call(
+        layer_kernel,
+        out_shape=(
+            jax.ShapeDtypeStruct((4, 128, 768), BF),
+            jax.ShapeDtypeStruct((4, 128, 768), BF),
+            jax.ShapeDtypeStruct((4, 96, 768), BF),
+            jax.ShapeDtypeStruct((96, 3072), BF),
+            jax.ShapeDtypeStruct((384, 768), BF),
+            jax.ShapeDtypeStruct((4, 8, 768), F32),
+            jax.ShapeDtypeStruct((48, 128), F32),
+        ),
+        in_specs=[any_space] * 8 + [pl.BlockSpec(memory_space=pltpu.SMEM)] + [vmem] * 3,
+        out_specs=(any_space,) * 6 + (vmem,),
+        scratch_shapes=scratch,
+        compiler_params=pltpu.CompilerParams(collective_id=0, has_side_effects=True, vmem_limit_bytes=64 * 2**20),
+        name="layer",
+    )(
+        passages, cotangent, w_query, w_key, w_value, w_attn_out, w_in, w_ff_out, lengths,
+        attn_gain.reshape(1, WIDTH), ffn_gain.reshape(1, WIDTH), bias_table,
+    )
+    layer_out, grad_input, g_att, g_in, g_ff, pooled, small = outs
+    g_att = g_att.astype(F32)
+    return (
+        layer_out,
+        pooled[:, 0],
+        grad_input,
+        small[32:38].reshape(WIDTH),
+        g_att[0],
+        g_att[1],
+        g_att[2],
+        g_att[3],
+        small[:32, :HEAD_N],
+        small[38:44].reshape(WIDTH),
+        g_in.astype(F32),
+        g_ff.astype(F32),
+    )
+
+
 def solution(mesh):
+    ring = (mesh.shape["dp"], mesh.shape["seq"]) == (DP, SEQ)
     return jax.shard_map(
-        shards,
+        passage_shards if ring else shards,
         mesh=mesh,
         in_specs=(
             P("dp", "seq", None),

time: 1250 us -> 278 us (0.22)
  waiting for transfers between devices: 905 us -> 0 us
  Pallas kernels: 0 us -> 261 us
  matrix products: 130 us -> 0 us
  local copies, waits for them, and re-layouts: 105 us -> 12.2 us
  blocking collectives: 51.5 us -> 0 us
  other arithmetic: 38 us -> 3.36 us
  between operations: 14.9 us -> 0.68 us
    reduce_scatter x8 -> x0, waiting for transfers between devices: 612 us -> none  [the longest x1 164 us: shards(): lax.psum_scatter(g_in, 'dp', scatter_dimension=0, tiled=True)]
    all_gather x8 -> x0, waiting for transfers between devices: 289 us -> none  [the longest x1 77.1 us: shards(): lax.all_gather(w_ff_out, 'dp', axis=0, tiled=True)]
    pallas_call x0 -> x1, Pallas kernels: none -> 261 us  [passage_shards(): pl.pallas_call(layer_kernel, out_shape=(jax.ShapeDtypeStruct((4, 128, 768...]
    dot_general x42 -> x0, matrix products: 130 us -> none  [the longest x1 12.1 us: shards(): up_rows = jnp.dot(normed_ffn, win_full, preferred_element_type=jnp.float32)]
    psum x2 -> x0, blocking collectives: 51.5 us -> none  [the longest x1 40.5 us: shards(): small_sums = lax.psum((g_attn_gain, g_ffn_gain, g_table), ('dp', 'seq'))]
    eq x1 -> x0, local copies, waits for them, and re-layouts: 37.9 us -> none  [shards(): bucket_index(relative, n_buckets, MAXDIST)[:, :, None]]
    while x66 -> x0, local copies, waits for them, and re-layouts: 24.8 us -> none
    convert_element_type x17 -> x3, other arithmetic: 25.2 us -> 3.36 us  [the longest x1 1.15 us: passage_shards(): g_att = g_att.astype(F32)]
  transfers between devices with their start and end apart: 17 -> 0, of which waited for: 15 -> 0; matrix products, arithmetic and copies ran while one was open for 14% -> 0% of each run, Pallas kernels for 0% -> 0%
where the time goes in v1:
time: 278 us; the launch traced here: 277 us
  Pallas kernels  261 us (94%)
  local copies, waits for them, and re-layouts  12.2 us (4%)
  other arithmetic  3.36 us (1%)
    pallas_call x1, Pallas kernels, passage_shards(): pl.pallas_call(layer_kernel, out_shape=(jax.ShapeDtypeStruct((4, 128, 768...  261 us
    unnamed x13, local copies, waits for them, and re-layouts  5.71 us

profile of v1, /device:TPU:0, one launch (start us, length us, event | category | flops | bytes accessed | tf_op | source)
XLA Modules:
  0.0 277.5 jit_solution(2507614696239121672)
XLA Ops:
  0.6 1.3 reshape.36.attn_gain
  1.9 1.3 reshape.37.ffn_gain
  3.2 1.4 copy.24.table
  4.6 261.2 %layer.1 = (bf16[4,128,768]{2,1,0:T(8,128)(2,1)}, bf16[4,128,768]{2,1,0:T(8,128)(2,1)}, bf16[4,96,768]{2,1,0:T(8,128)(2,1)}, bf16[96,3072]{1,0:T(8,128)(2,1)}, b...) custom-call(bf16[4,128,768]{2,1,0:T(8,128)(2,1)} %x_hbm.1, bf16[4,128,768]{2,1,0:T(8,128)(2,1)} %cot_hbm.1, ...), custom_call_target="tpu_custom_call" | custom-call | tf_op jit(solution)/shard_map/layer/pallas_call | solution.py:933
  265.8 1.3 slice_bitcast_fusion.4
  267.1 0.7 slice.30
  267.8 0.7 copy.25
  268.5 0.9 slice.24
  269.4 0.6 copy.28
  270.0 1.2 convert_element_type.9
  271.2 0.0 copy-start.3
  271.2 1.0 slice_bitcast_fusion
  272.2 0.0 copy-start.2
  272.2 0.4 copy-done.3
  272.6 1.1 convert_element_type.10
  273.7 0.0 copy-done.2
  273.7 0.0 copy-start.1
  273.7 1.1 convert_element_type.11
  274.8 0.4 copy-done.1
  275.2 0.0 copy-start
  275.2 0.9 copy.31
  276.0 0.5 copy-done
  276.6 0.9 copy.32
Async XLA Ops:
  271.2 1.4 copy-start.3
  272.2 1.5 copy-start.2
  273.7 1.5 copy-start.1
  275.2 1.4 copy-start

commit v2 on v0

--- a/solution.py
+++ b/solution.py
@@ -3,6 +3,8 @@
 import jax
 import jax.numpy as jnp
 from jax import lax
+from jax.experimental import pallas as pl
+from jax.experimental.pallas import tpu as pltpu
 from jax.sharding import PartitionSpec as P
 
 MAXDIST = 128
@@ -240,9 +242,842 @@
     )
 
 
+DP, SEQ = 8, 4
+FAR, EVENTS = 4, 7
+BF, F32 = jnp.bfloat16, jnp.float32
+MESH_ID = pl.DeviceIdType.MESH
+TOKENS, WIDTH, HIDDEN, HEAD_N = 512, 768, 3072, 12
+PAIRS = HEAD_N // 2
+GELU_A, GELU_B = math.sqrt(2 / math.pi), 0.044715
+
+
+def dg(left, right, on_left, on_right):
+    return lax.dot_general(
+        left, right, (((on_left,), (on_right,)), ((), ())), preferred_element_type=F32
+    )
+
+
+def exact(left, right, on_left, on_right):
+    return lax.dot_general(
+        left, right, (((on_left,), (on_right,)), ((), ())), precision=HIGH, preferred_element_type=F32
+    )
+
+
+def ring_dp(place):
+    high = place // 4
+    return 2 * (place * (1 - high) + (7 - place) * high) + high
+
+
+def times(start, size, step):
+    return pl.ds(pl.multiple_of(start, step), size)
+
+
+def band_bucket(n_buckets):
+    lane = lax.broadcasted_iota(jnp.int32, (n_buckets, 512), 1)
+    relative = jnp.where(lane < 384, lane - 128, lane - 640)
+    row = lax.broadcasted_iota(jnp.int32, (n_buckets, 512), 0)
+    return (bucket_index(relative, n_buckets, MAXDIST) == row).astype(F32)
+
+
+def layer_kernel(
+    x_hbm, cot_hbm, wq_hbm, wk_hbm, wv_hbm, wo_hbm, win_hbm, wff_hbm, lengths, attn_gain, ffn_gain, table,
+    out_hbm, gx_hbm, gatt_hbm, gin_hbm, gff_hbm, pool_hbm, small_out,
+    watt, win, wff, gin, gff, big, probs, xs, cot, normed, qkv, mixed, nf, hid, acc, band, diag, d_both,
+    sib_ff, sib_in, y_ff, y_in, r_ffa, r_ffb, r_ina, r_inb, r_att, f_ff, f_in, f_att, sums, sums_in, pool,
+    ag_s, ag_r, sb_s, sb_r, yf_s, yf_r, yb_s, yb_r, rr_s, rr_r, loc, a2_s, a2_r, hs_s, hs_r, yx_s, yx_r,
+    fa_s, fa_r, fo_s, fo_r, fl, bf_s, bf_r,
+):
+    dp, sq = lax.axis_index("dp"), lax.axis_index("seq")
+    z, x, y, c = dp // 2, dp % 2, sq // 2, sq % 2
+    place = x * (7 - z) + (1 - x) * z
+    turn = 1 - 2 * c
+
+    def owner(steps):
+        return ring_dp((place + steps * turn + 16) % 8)
+
+    nxt, prv = (owner(1), sq), (owner(-1), sq)
+    sib, yp, ysib = (dp, 2 * y + 1 - c), (dp, 2 * (1 - y) + c), (dp, 2 * (1 - y) + 1 - c)
+    xp = (2 * z + 1 - x, sq)
+    z1 = (2 * (z + 1 - 2 * (z % 2)) + x, sq)
+    z2 = (2 * ((z + 2) % 4) + x, sq)
+    peers = (sib, yp, ysib)
+
+    def send(src, dst, ss, rs, dev):
+        return pltpu.make_async_remote_copy(
+            src_ref=src, dst_ref=dst, send_sem=ss, recv_sem=rs, device_id=dev, device_id_type=MESH_ID
+        )
+
+    def when(condition, body):
+        if isinstance(condition, bool):
+            if condition:
+                body()
+        else:
+            pl.when(condition)(body)
+
+    def loop(count, body):
+        def step(i, _):
+            body(i)
+            return 0
+
+        lax.fori_loop(0, count, step, 0)
+
+    barrier = pltpu.get_barrier_semaphore()
+    for dev in (sib, yp, ysib, nxt, prv, xp, z1, z2):
+        pl.semaphore_signal(barrier, inc=1, device_id=dev, device_id_type=MESH_ID)
+
+    r96 = times(96 * dp, 96, 96)
+    own = [pltpu.make_async_copy(w, watt.at[i, r96], loc.at[i]) for i, w in enumerate((wq_hbm, wk_hbm, wv_hbm, wo_hbm))]
+    for i in range(2):
+        own.append(pltpu.make_async_copy(win_hbm.at[pl.ds(48 * i, 48)], win.at[dp, i], loc.at[4 + i]))
+    own.append(pltpu.make_async_copy(wff_hbm, wff.at[times(384 * dp, 384, 384)], loc.at[6]))
+    mine = times(128 * sq, 128, 128)
+    own.append(pltpu.make_async_copy(x_hbm.at[sq], xs.at[mine], loc.at[7]))
+    own.append(pltpu.make_async_copy(cot_hbm.at[sq], cot.at[mine], loc.at[8]))
+    for copy in own:
+        copy.start()
+    pl.semaphore_wait(barrier, 8)
+
+    def swap(k, src_hbm, dst, at):
+        dev = peers[k]
+        return send(src_hbm.at[dev[1]], dst.at[mine], a2_s.at[at, k], a2_r.at[at, k], dev)
+
+    def swap_wait(dst, at):
+        for k in range(3):
+            theirs = dst.at[times(128 * peers[k][1], 128, 128)]
+            send(theirs, theirs, a2_s.at[at, k], a2_r.at[at, k], peers[k]).wait_recv()
+
+    for k in range(3):
+        swap(k, x_hbm, xs, 0).start()
+
+    def piece(ch, d, cc, yy):
+        if ch < 3:
+            cols = pl.ds(128 + 256 * ch, 256) if ch < 2 else times(640 * yy, 128, 128)
+            return watt.at[:, times(96 * d + 48 * cc, 48, 48), cols]
+        if ch < 5:
+            cols = pl.ds(1024, 1024) if ch == 3 else times(2048 * yy, 1024, 1024)
+            return win.at[d, cc, :, cols]
+        cols = pl.ds(256, 256) if ch == 5 else times(512 * yy, 256, 256)
+        return wff.at[times(384 * d + 192 * cc, 192, 192), cols]
+
+    crossing = (2, 4, 6)
+    groups = ((0, 1, 2), (3, 4), (5, 6))
+
+    def came_from(e):
+        ahead = e // FAR
+        return (1 - ahead) * (-e - 1) + ahead * (e - 3)
+
+    def side(e):
+        return (owner(1 - 2 * (e // FAR)), sq)
+
+    def ring_send(ch, e):
+        ahead = e // FAR
+        part = piece(ch, owner((1 - ahead) * -e + ahead * (e - FAR)), c, y)
+        return send(part, part, ag_s.at[ch, e], ag_r.at[ch, e], side(e))
+
+    def hand_on(ch, e):
+        part = piece(ch, owner(came_from(e)), c, y)
+        return send(part, part, sb_s.at[ch, e], sb_r.at[ch, e], sib)
+
+    def cross(ch, e):
+        part = piece(ch, owner(came_from(e)), c, y)
+        return send(part, part, yf_s.at[ch // 2 - 1, e], yf_r.at[ch // 2 - 1, e], yp)
+
+    def cross_on(ch, e):
+        part = piece(ch, owner(came_from(e)), c, 1 - y)
+        return send(part, part, yb_s.at[ch // 2 - 1, e], yb_r.at[ch // 2 - 1, e], sib)
+
+    def arrive(ch, e):
+        part = piece(ch, owner(came_from(e)), c, y)
+        send(part, part, ag_s.at[ch, e], ag_r.at[ch, e], side(e)).wait_recv()
+        if e not in (FAR - 1, EVENTS - 1):
+            ring_send(ch, e + 1).start()
+        if ch in crossing:
+            cross(ch, e).start()
+        hand_on(ch, e).start()
+
+    def arrive_cross(ch, e):
+        part = piece(ch, owner(came_from(e)), c, 1 - y)
+        send(part, part, yf_s.at[ch // 2 - 1, e], yf_r.at[ch // 2 - 1, e], yp).wait_recv()
+        cross_on(ch, e).start()
+
+    def both(s):
+        return (s, FAR + s) if s < FAR - 1 else (s,)
+
+    def ticks(group, s):
+        for ch in reversed(groups[group]):
+            for e in both(s):
+                arrive(ch, e)
+        if s > 0:
+            for e in both(s - 1):
+                arrive_cross(groups[group][-1], e)
+
+    def gathered(group):
+        arrive_cross(groups[group][-1], FAR - 1)
+
+        def step(e):
+            d = owner(-came_from(e))
+            for ch in groups[group]:
+                part = piece(ch, d, 1 - c, y)
+                send(part, part, sb_s.at[ch, e], sb_r.at[ch, e], sib).wait_recv()
+            part = piece(groups[group][-1], d, 1 - c, 1 - y)
+            send(part, part, yb_s.at[group, e], yb_r.at[group, e], sib).wait_recv()
+
+        loop(EVENTS, step)
+
+    def gather_sent(group):
+        def step(e):
+            for ch in groups[group]:
+                ring_send(ch, e).wait_send()
+                hand_on(ch, e).wait_send()
+            cross(groups[group][-1], e).wait_send()
+            cross_on(groups[group][-1], e).wait_send()
+
+        loop(EVENTS, step)
+
+    def begin(group):
+        for ch in reversed(groups[group]):
+            ring_send(ch, 0).start()
+            ring_send(ch, FAR).start()
+
+    for i in range(4):
+        own[i].wait()
+    begin(0)
+
+    band[pl.ds(0, HEAD_N), :] = exact(table[...], band_bucket(32), 1, 0)
+    gain_a = attn_gain[...].reshape(1, WIDTH)
+    gain_f = ffn_gain[...].reshape(1, WIDTH)
+
+    ticks(0, 0)
+    own[7].wait()
+    swap_wait(xs, 0)
+    for k in range(3):
+        swap(k, cot_hbm, cot, 1).start()
+    for i in range(4, 7):
+        own[i].wait()
+
+    def norm_rows(b):
+        rows = times(128 * b, 128, 128)
+        v = xs[rows, :].astype(F32)
+        s = lax.rsqrt(jnp.mean(v * v, axis=-1, keepdims=True) + EPS)
+        normed[rows, :] = (v * s * gain_a).astype(BF)
+
+    loop(4, norm_rows)
+
+    ticks(0, 1)
+    ticks(0, 2)
+    begin(1)
+    ticks(0, 3)
+    gathered(0)
+
+    def project(m):
+        qkv[m] = dg(normed[...], watt[m], 1, 0).astype(BF)
+
+    loop(3, project)
+    ticks(1, 0)
+
+    count = lengths[sq]
+    valid = lax.broadcasted_iota(jnp.int32, (1, TOKENS), 1) < count
+    lane = lax.broadcasted_iota(jnp.int32, (1, 128), 1)
+    keep = (lane < 64, lane >= 64)
+
+    def only(h, v):
+        return jnp.where(keep[h], v, jnp.zeros_like(v))
+
+    def attend(hp):
+        cols = times(128 * hp, 128, 128)
+        key, value = qkv[1, :, cols], qkv[2, :, cols]
+        total = [None] * 4
+        for h in range(2):
+            row = band[pl.ds(2 * hp + h, 1), :]
+            tilted = pltpu.roll(jnp.broadcast_to(row, (128, 512)), 0, 1, stride=1, stride_axis=0)
+            before = jnp.broadcast_to(row[:, 384:], (128, 128))
+            after = jnp.broadcast_to(row[:, 256:384], (128, 128))
+            value_h = only(h, value)
+            for ib in range(4):
+                rows = pl.ds(128 * ib, 128)
+                blocks = []
+                for jb in range(4):
+                    off = jb - ib
+                    if off < -1:
+                        blocks.append(before)
+                    elif off > 1:
+                        blocks.append(after)
+                    else:
+                        blocks.append(tilted[:, 128 * (off + 1) : 128 * (off + 2)])
+                scores = dg(only(h, qkv[0, rows, cols]), key, 1, 1) + jnp.concatenate(blocks, axis=1)
+                scores = jnp.where(valid, scores, FLOOR)
+                top = jnp.max(scores, axis=-1, keepdims=True)
+                expo = jnp.exp(scores - top)
+                part = jnp.sum(expo, axis=-1, keepdims=True)
+                low = (expo * (1.0 / part)).astype(BF)
+                probs[2 * hp + h, rows, :] = low
+                one = dg(low, value_h, 1, 0)
+                total[ib] = one if h == 0 else total[ib] + one
+        for ib in range(4):
+            mixed[pl.ds(128 * ib, 128), cols] = total[ib].astype(BF)
+
+        @pl.when(hp == 1)
+        def _():
+            ticks(1, 1)
+
+        @pl.when(hp == 3)
+        def _():
+            ticks(1, 2)
+            begin(2)
+
+        @pl.when(hp == 5)
+        def _():
+            ticks(1, 3)
+
+    loop(PAIRS, attend)
+
+    def residual(b):
+        rows = times(256 * b, 256, 256)
+        v = xs[rows, :].astype(F32) + dg(mixed[rows, :], watt[3], 1, 0)
+        hid[rows, :] = v
+        s = lax.rsqrt(jnp.mean(v * v, axis=-1, keepdims=True) + EPS)
+        nf[rows, :] = (v * s * gain_f).astype(BF)
+
+    loop(2, residual)
+
+    ticks(2, 0)
+    gathered(1)
+    up_rows, down_rows = pl.ds(0, TOKENS), pl.ds(TOKENS, TOKENS)
+
+    def block(j):
+        return times(768 * j, 768, 768)
+
+    def win_block(j):
+        return win[:, :, :, block(j)].reshape(768, 768)
+
+    def widen(j):
+        v = dg(nf[...], win_block(j), 1, 0)
+        sq_v = v * v
+        t = jnp.tanh(v * (GELU_A + (GELU_A * GELU_B) * sq_v))
+        half = 0.5 + 0.5 * t
+        big[j, up_rows, :] = (v * half).astype(BF)
+        slope = half + (v * half) * (1.0 - t) * (GELU_A + (3 * GELU_A * GELU_B) * sq_v)
+        big[j, down_rows, :] = slope.astype(BF)
+
+        @pl.when(j == 1)
+        def _():
+            ticks(2, 1)
+
+        @pl.when(j == 3)
+        def _():
+            ticks(2, 2)
+
+    loop(4, widen)
+    own[8].wait()
+    swap_wait(cot, 1)
+
+    def half_ff(j):
+        src = gff.at[pl.ds(2 * j, 2), times(192 * (1 - c), 192, 192)]
+        return send(src, sib_ff.at[pl.ds(2 * j, 2)], hs_s.at[0, j], hs_r.at[0, j], sib)
+
+    def grad_ff(j):
+        v = dg(big[j, up_rows, :], cot[...], 0, 0).astype(BF)
+        gff[pl.ds(2 * j, 2)] = v.reshape(2, 384, 768)
+        half_ff(j).start()
+
+    loop(4, grad_ff)
+    ticks(2, 3)
+
+    def merge_ff(j):
+        half_ff(j).wait()
+        rows = times(192 * c, 192, 192)
+        for i in range(2):
+            gff[2 * j + i, rows] = (gff[2 * j + i, rows].astype(F32) + sib_ff[2 * j + i].astype(F32)).astype(BF)
+
+    loop(4, merge_ff)
+
+    def cross_src(g, yy):
+        if g == 0:
+            return gff.at[:, times(192 * c + 160 * yy, 32, 32)]
+        return gin.at[:, times(1536 * c + 1280 * yy, 256, 256)]
+
+    cross_dst = (y_ff, y_in)
+
+    def cross_sum(g):
+        return send(cross_src(g, 1 - y), cross_dst[g], yx_s.at[g], yx_r.at[g], yp)
+
+    def add_cross(g):
+        cross_sum(g).wait()
+        here, came = cross_src(g, y), cross_dst[g]
+        here[...] = (here[...].astype(F32) + came[...].astype(F32)).astype(BF)
+
+    def rs_piece(ch, d, yy):
+        if ch < 3:
+            rows = times(192 * c + 32 + 64 * ch, 64, 32) if ch < 2 else times(192 * c + 160 * yy, 32, 32)
+            return gff.at[d, rows]
+        if ch < 5:
+            return gin.at[times(96 * d, 96, 96), times(1536 * c + 256 + 512 * (ch - 3), 512, 256)]
+        if ch == 5:
+            return gin.at[times(96 * d, 96, 96), times(1536 * c + 1280 * yy, 256, 256)]
+        return win.at[d, c, :, pl.ds(768 * (ch - 6), 768)]
+
+    landing = [r_ffa.at[0], r_ffa.at[1], r_ffb, r_ina.at[0], r_ina.at[1], r_inb, r_att.at[0]]
+    landing += [r_ffa.at[0, :, pl.ds(0, 48)], r_ffa.at[1, :, pl.ds(0, 48)], r_att.at[1]]
+
+    def rs_send(ch, e):
+        ahead = e // FAR
+        part = rs_piece(ch, owner((1 - ahead) * (FAR - e) + ahead * (e - EVENTS)), y)
+        return send(part, landing[ch].at[e], rr_s.at[ch, e], rr_r.at[ch, e], side(e))
+
+    def rs_begin(ch):
+        rs_send(ch, 0).start()
+        rs_send(ch, FAR).start()
+
+    def rs_round(ch, s):
+        for e in both(s):
+            rs_send(ch, e).wait_recv()
+            here = rs_piece(ch, owner(FAR - 1 - e if e < FAR else e - EVENTS + 1), y)
+            here[...] = (here[...].astype(F32) + landing[ch][e].astype(F32)).astype(BF)
+            if e not in (FAR - 1, EVENTS - 1):
+                rs_send(ch, e + 1).start()
+
+    cross_sum(0).start()
+    rs_begin(0)
+    rs_begin(1)
+    gathered(2)
+
+    def grad_up(j):
+        v = dg(cot[...], wff[block(j), :], 1, 1) * big[j, down_rows, :].astype(F32)
+        big[j, down_rows, :] = v.astype(BF)
+
+    loop(4, grad_up)
+
+    def grad_in(j):
+        gin[:, block(j)] = dg(nf[...], big[j, down_rows, :], 0, 0).astype(BF)
+
+        @pl.when(j == 1)
+        def _():
+            rs_round(0, 0)
+
+        @pl.when(j == 3)
+        def _():
+            rs_round(1, 0)
+
+    loop(4, grad_in)
+
+    def half_in(k):
+        src = gin.at[:, times(1536 * (1 - c) + 384 * k, 384, 384)]
+        return send(src, sib_in.at[k], hs_s.at[1, k], hs_r.at[1, k], sib)
+
+    for k in range(4):
+        half_in(k).start()
+
+    acc[...] = jnp.zeros_like(acc)
+
+    def grad_nf(j):
+        acc[...] += dg(big[j, down_rows, :], win_block(j), 1, 1)
+
+        @pl.when(j == 2)
+        def _():
+            rs_round(0, 1)
+
+    loop(4, grad_nf)
+    add_cross(0)
+    rs_begin(2)
+
+    for k in range(4):
+        half_in(k).wait()
+        cols = times(1536 * c + 384 * k, 384, 384)
+        gin[:, cols] = (gin[:, cols].astype(F32) + sib_in[k].astype(F32)).astype(BF)
+    cross_sum(1).start()
+    rs_begin(3)
+    rs_begin(4)
+
+    def norm_back(v, gain, grad):
+        s = lax.rsqrt(jnp.mean(v * v, axis=-1, keepdims=True) + EPS)
+        scaled = grad * gain
+        back = s * scaled - v * (s * s * s) * jnp.mean(v * scaled, axis=-1, keepdims=True)
+        return back, jnp.sum(grad * v * s, axis=0, keepdims=True)
+
+    def ffn_norm_back(b, total):
+        rows = times(128 * b, 128, 128)
+        v = hid[rows, :]
+        back, part = norm_back(v, gain_f, acc[rows, :])
+        grad = cot[rows, :].astype(F32) + back
+        acc[rows, :] = grad
+        cot[rows, :] = grad.astype(BF)
+        return total + part
+
+    g_ffn_gain = lax.fori_loop(0, 4, ffn_norm_back, jnp.zeros((1, WIDTH), F32))
+
+    rs_round(1, 1)
+    gather_sent(1)
+    win[:, :, :, block(3)] = dg(mixed[...], cot[...], 0, 0).astype(BF).reshape(8, 2, 48, 768)
+
+    def sib_rows(t):
+        return sib_ff.at[:, times(48 * t, 48, 48)]
+
+    def half_att(t):
+        return send(win.at[:, 1 - c, :, block(t)], sib_rows(t), hs_s.at[2, t], hs_r.at[2, t], sib)
+
+    def merge_att(t):
+        half_att(t).wait()
+        win[:, c, :, block(t)] = (win[:, c, :, block(t)].astype(F32) + sib_rows(t)[...].astype(F32)).astype(BF)
+
+    half_att(3).start()
+    nf[...] = dg(cot[...], watt[3], 1, 1).astype(BF)
+
+    final = [f_ff, f_in] + [f_att.at[t] for t in range(4)]
+
+    def own_piece(g):
+        if g == 0:
+            return gff.at[dp, times(192 * c + 32, 128, 32)]
+        if g == 1:
+            return gin.at[r96, times(1536 * c + 256, 1024, 256)]
+        return rs_piece(4 + g, dp, y)
+
+    def out_piece(g, cc, yy):
+        if g == 0:
+            return gff_hbm.at[times(192 * cc + 32, 128, 32) if yy is None else times(192 * cc + 160 * yy, 32, 32)]
+        if g == 1:
+            if yy is None:
+                return gin_hbm.at[:, times(1536 * cc + 256, 1024, 256)]
+            return gin_hbm.at[:, times(1536 * cc + 1280 * yy, 256, 256)]
+        return gatt_hbm.at[g - 2, times(48 * cc, 48, 48)]
+
+    def share_a(g):
+        return send(own_piece(g), final[g], fa_s.at[g], fa_r.at[g], yp)
+
+    def share_b(g, k):
+        return send(rs_piece(3 * g + 2, dp, y), out_piece(g, c, y), fo_s.at[g, k], fo_r.at[g, k], peers[k])
+
+    def share_sum(g):
+        return send(final[g], out_piece(g, c, None), fo_s.at[g, 3], fo_r.at[g, 3], sib)
+
+    def keep_b(g):
+        return pltpu.make_async_copy(rs_piece(3 * g + 2, dp, y), out_piece(g, c, y), fl.at[g, 0])
+
+    def keep_sum(g):
+        return pltpu.make_async_copy(final[g], out_piece(g, c, None), fl.at[g, 1])
+
+    def finish_b(g):
+        for k in range(3):
+            share_b(g, k).start()
+        keep_b(g).start()
+
+    def finish_sum(g):
+        share_a(g).wait()
+        final[g][...] = (final[g][...].astype(F32) + own_piece(g)[...].astype(F32)).astype(BF)
+        share_sum(g).start()
+        keep_sum(g).start()
+
+    rs_round(0, 2)
+
+    flip_sum = lax.broadcasted_iota(jnp.int32, (128, 128), 0) + lax.broadcasted_iota(jnp.int32, (128, 128), 1)
+    flip = (flip_sum == 127).astype(F32)
+
+    def attend_back(hp):
+        cols = times(128 * hp, 128, 128)
+        key, value = qkv[1, :, cols], qkv[2, :, cols]
+        query, grad = qkv[0, :, cols], nf[:, cols]
+        g_query = [None] * 4
+        for h in range(2):
+            key_h = only(h, key)
+            before = after = jnp.zeros((128, 128), F32)
+            near = [jnp.zeros((128, 128), F32) for _ in range(3)]
+            for ib in range(4):
+                rows = pl.ds(128 * ib, 128)
+                wide = probs[2 * hp + h, rows, :].astype(F32)
+                d_probs = dg(only(h, nf[rows, cols]), value, 1, 1)
+                mean_d = jnp.sum(wide * d_probs, axis=-1, keepdims=True)
+                d_score = wide * (d_probs - mean_d)
+                for jb in range(4):
+                    off, part = jb - ib, d_score[:, 128 * jb : 128 * (jb + 1)]
+                    if off < -1:
+                        before = before + part
+                    elif off > 1:
+                        after = after + part
+                    else:
+                        near[off + 1] = near[off + 1] + part
+                d_low = d_score.astype(BF)
+                d_both[pl.ds(512 * h + 128 * ib, 128), :] = d_low
+                one = dg(d_low, key_h, 1, 0)
+                g_query[ib] = one if h == 0 else g_query[ib] + one
+            tilted = exact(flip, jnp.concatenate(near, axis=1), 1, 0)
+            tilted = jnp.concatenate([tilted, jnp.zeros((128, 128), F32)], axis=1)
+            flat = jnp.sum(pltpu.roll(tilted, 385, 1, stride=1, stride_axis=0), axis=0, keepdims=True)
+            far = jnp.concatenate(
+                [
+                    jnp.zeros((1, 256), F32),
+                    jnp.sum(after, axis=0, keepdims=True),
+                    jnp.sum(before, axis=0, keepdims=True),
+                ],
+                axis=1,
+            )
+            diag[pl.ds(2 * hp + h, 1), :] = flat + far
+        both_query = jnp.concatenate([only(0, query), only(1, query)], axis=0)
+        both_grad = jnp.concatenate([only(0, grad), only(1, grad)], axis=0)
+        qkv[1, :, cols] = dg(d_both[...], both_query, 0, 0).astype(BF)
+        qkv[2, :, cols] = dg(probs[pl.ds(2 * hp, 2)].reshape(1024, 512), both_grad, 0, 0).astype(BF)
+        for ib in range(4):
+            qkv[0, pl.ds(128 * ib, 128), cols] = g_query[ib].astype(BF)
+
+        @pl.when(hp % 2 == 1)
+        def _():
+            t = hp // 2
+            three = times(256 * t, 256, 256)
+            grads = jnp.concatenate([qkv[0, :, three], qkv[1, :, three], qkv[2, :, three]], axis=1)
+            win[:, :, :, block(t)] = dg(normed[...], grads, 0, 0).astype(BF).reshape(8, 2, 48, 768)
+            half_att(t).start()
+
+        def plan(at, *steps):
+            @pl.when(hp == at)
+            def _():
+                for step in steps:
+                    step()
+
+        def round_of(ch, s):
+            return lambda: rs_round(ch, s)
+
+        def start_block(t):
+            def run():
+                merge_att(t)
+                rs_begin(6 + t)
+
+            return run
+
+        def start_in():
+            add_cross(1)
+            rs_begin(5)
+
+        plan(0, round_of(1, 2), round_of(0, 3), round_of(2, 0), start_block(3))
+        plan(1, round_of(1, 3), round_of(2, 1), share_a(0).start, round_of(3, 0), round_of(9, 0))
+        plan(2, round_of(4, 0), round_of(2, 2), round_of(3, 1), round_of(9, 1), start_in, start_block(0))
+        plan(3, lambda: finish_sum(0), round_of(4, 1), round_of(2, 3), round_of(9, 2), round_of(5, 0), round_of(6, 0))
+        plan(4, round_of(3, 2), round_of(4, 2), round_of(9, 3), round_of(5, 1), round_of(6, 1), start_block(1))
+        plan(5, round_of(3, 3), round_of(4, 3), round_of(5, 2), round_of(6, 2), round_of(7, 0))
+
+    loop(PAIRS, attend_back)
+    finish_b(0)
+    share_a(1).start()
+    share_a(5).start()
+
+    merge_att(2)
+    rs_begin(8)
+
+    def attn_norm_back(b, total):
+        rows = times(256 * b, 256, 256)
+        grad = dg(qkv[0, rows, :], watt[0], 1, 1) + dg(qkv[1, rows, :], watt[1], 1, 1) + dg(qkv[2, rows, :], watt[2], 1, 1)
+        back, part = norm_back(xs[rows, :].astype(F32), gain_a, grad)
+        mixed[rows, :] = (acc[rows, :] + back).astype(BF)
+        return total + part
+
+    g_attn_gain = lax.fori_loop(0, 2, attn_norm_back, jnp.zeros((1, WIDTH), F32))
+
+    def give(src, dst_hbm, at, k):
+        dev = peers[k]
+        return send(src.at[times(128 * dev[1], 128, 128)], dst_hbm.at[sq], a2_s.at[at, k], a2_r.at[at, k], dev)
+
+    def give_wait(src, dst_hbm, at):
+        for k in range(3):
+            give(src, dst_hbm, at, k).wait_send()
+            theirs = dst_hbm.at[peers[k][1]]
+            send(theirs, theirs, a2_s.at[at, k], a2_r.at[at, k], peers[k]).wait_recv()
+
+    for k in range(3):
+        give(mixed, gx_hbm, 3, k).start()
+    gx_own = pltpu.make_async_copy(mixed.at[mine], gx_hbm.at[sq], loc.at[0])
+    gx_own.start()
+
+    sums[0] = jnp.zeros((32, 128), F32)
+    sums[0, 0:16, 0:32] = exact(diag[...], band_bucket(32), 1, 1)
+    for k in range(6):
+        sums[0, 16 + k : 17 + k, :] = g_attn_gain[:, 128 * k : 128 * (k + 1)]
+        sums[0, 22 + k : 23 + k, :] = g_ffn_gain[:, 128 * k : 128 * (k + 1)]
+
+    def hop(k):
+        dev = (sib, yp, xp, z1, z2)[k]
+        return send(sums.at[k], sums_in.at[k], bf_s.at[k], bf_r.at[k], dev)
+
+    def hop_done(k):
+        hop(k).wait()
+        sums[k + 1] = sums[k] + sums_in[k]
+
+    def pool_send(k):
+        return send(pool, pool_hbm.at[sq], a2_s.at[4, k], a2_r.at[4, k], peers[k])
+
+    pool_own = pltpu.make_async_copy(pool, pool_hbm.at[sq], loc.at[2])
+    lay_own = pltpu.make_async_copy(nf.at[mine], out_hbm.at[sq], loc.at[1])
+    hop(0).start()
+    for r in range(5):
+        if r < 4:
+            part = dg(big[r, up_rows, :], wff[block(r), :], 1, 0)
+            acc[...] = part + (hid[...] if r == 0 else acc[...])
+        if r == 0:
+            rs_round(6, 3)
+            share_a(2).start()
+            rs_round(5, 3)
+            finish_b(1)
+        if r < 3:
+            rs_round(7, r + 1)
+        if r == 2:
+            share_a(3).start()
+        if r > 0:
+            rs_round(8, r - 1)
+        hop_done(r)
+        if r < 4:
+            hop(r + 1).start()
+        if r == 1:
+            finish_sum(1)
+            finish_sum(5)
+        if r == 3:
+            nf[...] = acc[...].astype(BF)
+            for k in range(3):
+                give(nf, out_hbm, 2, k).start()
+            lay_own.start()
+            here_t = lax.broadcasted_iota(jnp.int32, (TOKENS, 1), 0) < count
+            mean = jnp.sum(jnp.where(here_t, acc[...], 0.0), axis=0, keepdims=True) / count.astype(F32)
+            pool[...] = jnp.broadcast_to(mean, (8, WIDTH))
+            pool_own.start()
+            for k in range(3):
+                pool_send(k).start()
+            finish_sum(2)
+    share_a(4).start()
+    small_out[...] = sums[5]
+    finish_sum(3)
+    finish_sum(4)
+
+    for g in range(6):
+        if g < 2:
+            keep_b(g).wait()
+            for k, (cc, yy) in enumerate(((1 - c, y), (c, 1 - y), (1 - c, 1 - y))):
+                share_b(g, k).wait_send()
+                came = out_piece(g, cc, yy)
+                send(came, came, fo_s.at[g, k], fo_r.at[g, k], peers[k]).wait_recv()
+        keep_sum(g).wait()
+        share_sum(g).wait_send()
+        came = out_piece(g, 1 - c, None)
+        send(came, came, fo_s.at[g, 3], fo_r.at[g, 3], sib).wait_recv()
+
+    def ring_sent(e):
+        for ch in range(10):
+            rs_send(ch, e).wait_send()
+
+    loop(EVENTS, ring_sent)
+    gather_sent(0)
+    gather_sent(2)
+    give_wait(nf, out_hbm, 2)
+    give_wait(mixed, gx_hbm, 3)
+    lay_own.wait()
+    gx_own.wait()
+    pool_own.wait()
+    for k in range(3):
+        pool_send(k).wait_send()
+        theirs = pool_hbm.at[peers[k][1]]
+        send(theirs, theirs, a2_s.at[4, k], a2_r.at[4, k], peers[k]).wait_recv()
+        swap(k, x_hbm, xs, 0).wait_send()
+        swap(k, cot_hbm, cot, 1).wait_send()
+
+
+def finish_kernel(
+    out_in, gx_in, g_att, g_in, g_ff, pooled, small,
+    out, gx, pool_out, gain_a, gq, gk, gv, go, g_table, gain_f, gin_out, gff_out, sem,
+):
+    copies = [pltpu.make_async_copy(out_in, out, sem.at[0]), pltpu.make_async_copy(gx_in, gx, sem.at[1])]
+    for copy in copies:
+        copy.start()
+    for t in range(3):
+        for i, ref in enumerate((gq, gk, gv)):
+            ref[:, 256 * t : 256 * (t + 1)] = g_att[t, :, 256 * i : 256 * (i + 1)].astype(F32)
+    go[...] = g_att[3].astype(F32)
+    gin_out[...] = g_in[...].astype(F32)
+    gff_out[...] = g_ff[...].astype(F32)
+    for p in range(SEQ):
+        pool_out[p : p + 1, :] = pooled[p, 0:1, :]
+    g_table[...] = small[0:HEAD_N, 0:32]
+    for k in range(6):
+        gain_a[128 * k : 128 * (k + 1)] = small[16 + k : 17 + k, :].reshape(128)
+        gain_f[128 * k : 128 * (k + 1)] = small[22 + k : 23 + k, :].reshape(128)
+    for copy in copies:
+        copy.wait()
+
+
+def passage_shards(
+    passages, lengths, attn_gain, w_query, w_key, w_value, w_attn_out, bias_table, ffn_gain, w_in, w_ff_out, cotangent
+):
+    any_space = pl.BlockSpec(memory_space=pl.ANY)
+    vmem = pl.BlockSpec(memory_space=pltpu.VMEM)
+    dma = pltpu.SemaphoreType.DMA
+    scratch = [
+        pltpu.VMEM(shape, BF)
+        for shape in (
+            (4, 768, 768), (8, 2, 48, 3072), (3072, 768), (768, 3072), (8, 384, 768), (4, 1024, 768), (12, 512, 512),
+            (512, 768), (512, 768), (512, 768), (3, 512, 768), (512, 768), (512, 768),
+        )
+    ]
+    scratch += [pltpu.VMEM(shape, F32) for shape in ((512, 768), (512, 768), (16, 512), (16, 512))]
+    scratch += [
+        pltpu.VMEM(shape, BF)
+        for shape in (
+            (1024, 512), (8, 192, 768), (4, 768, 384), (8, 32, 768), (768, 256),
+            (2, 7, 64, 768), (7, 32, 768), (2, 7, 96, 512), (7, 96, 256), (2, 7, 48, 768),
+            (128, 768), (96, 1024), (4, 48, 768),
+        )
+    ]
+    scratch += [pltpu.VMEM((6, 32, 128), F32), pltpu.VMEM((5, 32, 128), F32), pltpu.VMEM((8, 768), F32)]
+    scratch += [
+        dma(shape)
+        for shape in (
+            (7, 7), (7, 7), (7, 7), (7, 7), (3, 7), (3, 7), (3, 7), (3, 7), (10, 7), (10, 7), (9,), (5, 3), (5, 3),
+            (3, 4), (3, 4), (2,), (2,), (6,), (6,), (6, 4), (6, 4), (6, 2), (5,), (5,),
+        )
+    ]
+    sums = pl.pallas_call(
+        layer_kernel,
+        out_shape=(
+            jax.ShapeDtypeStruct((4, 128, 768), BF),
+            jax.ShapeDtypeStruct((4, 128, 768), BF),
+            jax.ShapeDtypeStruct((4, 96, 768), BF),
+            jax.ShapeDtypeStruct((96, 3072), BF),
+            jax.ShapeDtypeStruct((384, 768), BF),
+            jax.ShapeDtypeStruct((4, 8, 768), F32),
+            jax.ShapeDtypeStruct((32, 128), F32),
+        ),
+        in_specs=[any_space] * 8 + [pl.BlockSpec(memory_space=pltpu.SMEM)] + [vmem] * 3,
+        out_specs=(any_space,) * 6 + (vmem,),
+        scratch_shapes=scratch,
+        compiler_params=pltpu.CompilerParams(collective_id=0, has_side_effects=True, vmem_limit_bytes=64 * 2**20),
+        name="layer",
+    )(
+        passages, cotangent, w_query, w_key, w_value, w_attn_out, w_in, w_ff_out, lengths,
+        attn_gain, ffn_gain, bias_table.T,
+    )
+    square = jax.ShapeDtypeStruct((96, 768), F32)
+    gain = jax.ShapeDtypeStruct((WIDTH,), F32)
+    outs = pl.pallas_call(
+        finish_kernel,
+        out_shape=(
+            jax.ShapeDtypeStruct((4, 128, 768), BF),
+            jax.ShapeDtypeStruct((4, 128, 768), BF),
+            jax.ShapeDtypeStruct((4, 768), F32),
+            gain,
+            square,
+            square,
+            square,
+            square,
+            jax.ShapeDtypeStruct((HEAD_N, 32), F32),
+            gain,
+            jax.ShapeDtypeStruct((96, 3072), F32),
+            jax.ShapeDtypeStruct((384, 768), F32),
+        ),
+        in_specs=[vmem] * 7,
+        out_specs=(any_space,) * 2 + (vmem,) * 10,
+        scratch_shapes=[dma((2,))],
+        compiler_params=pltpu.CompilerParams(vmem_limit_bytes=64 * 2**20),
+        name="finish",
+    )(*sums)
+    return (outs[0], outs[2], outs[1], *outs[3:8], outs[8].T, *outs[9:])
+
+
 def solution(mesh):
+    ring = (mesh.shape["dp"], mesh.shape["seq"]) == (DP, SEQ)
     return jax.shard_map(
-        shards,
+        passage_shards if ring else shards,
         mesh=mesh,
         in_specs=(
             P("dp", "seq", None),

time: 1250 us -> 178 us (0.14)
  waiting for transfers between devices: 905 us -> 0 us
  Pallas kernels: 0 us -> 177 us
  matrix products: 130 us -> 0 us
  local copies, waits for them, and re-layouts: 105 us -> 0 us
  blocking collectives: 51.5 us -> 0 us
  other arithmetic: 38 us -> 0 us
  between operations: 14.9 us -> 0.82 us
    reduce_scatter x8 -> x0, waiting for transfers between devices: 612 us -> none  [the longest x1 164 us: shards(): lax.psum_scatter(g_in, 'dp', scatter_dimension=0, tiled=True)]
    all_gather x8 -> x0, waiting for transfers between devices: 289 us -> none  [the longest x1 77.1 us: shards(): lax.all_gather(w_ff_out, 'dp', axis=0, tiled=True)]
    pallas_call x0 -> x2, Pallas kernels: none -> 177 us  [the longest x1 172 us: passage_shards(): pl.pallas_call(layer_kernel, out_shape=(jax.ShapeDtypeStruct((4, 128, 768...]
    dot_general x42 -> x0, matrix products: 130 us -> none  [the longest x1 12.1 us: shards(): up_rows = jnp.dot(normed_ffn, win_full, preferred_element_type=jnp.float32)]
    psum x2 -> x0, blocking collectives: 51.5 us -> none  [the longest x1 40.5 us: shards(): small_sums = lax.psum((g_attn_gain, g_ffn_gain, g_table), ('dp', 'seq'))]
    eq x1 -> x0, local copies, waits for them, and re-layouts: 37.9 us -> none  [shards(): bucket_index(relative, n_buckets, MAXDIST)[:, :, None]]
    convert_element_type x17 -> x0, other arithmetic: 25.2 us -> none  [the longest x1 2.76 us: shards(): (grad_hidden + grad_inputs_norm).astype(jnp.bfloat16)]
    while x66 -> x0, local copies, waits for them, and re-layouts: 24.8 us -> none
  transfers between devices with their start and end apart: 17 -> 0, of which waited for: 15 -> 0; matrix products, arithmetic and copies ran while one was open for 14% -> 0% of each run, Pallas kernels for 0% -> 0%
where the time goes in v2:
time: 178 us
  Pallas kernels  177 us (99%)
    pallas_call x1, Pallas kernels, passage_shards(): pl.pallas_call(layer_kernel, out_shape=(jax.ShapeDtypeStruct((4, 128, 768...  172 us
    pallas_call x1, Pallas kernels, passage_shards(): pl.pallas_call(finish_kernel, out_shape=(jax.ShapeDtypeStruct((4, 128, 76...  4.92 us

profile of v2, /device:TPU:0, one launch (start us, length us, event | category | flops | bytes accessed | tf_op | source)
XLA Modules:
  0.0 177.8 jit_solution(3232093251438966811)
XLA Ops:
  0.6 172.0 %layer.1 = (bf16[4,128,768]{2,1,0:T(8,128)(2,1)}, bf16[4,128,768]{2,1,0:T(8,128)(2,1)}, bf16[4,96,768]{2,1,0:T(8,128)(2,1)}, bf16[96,3072]{1,0:T(8,128)(2,1)}, b...) custom-call(bf16[4,128,768]{2,1,0:T(8,128)(2,1)} %x_hbm.1, bf16[4,128,768]{2,1,0:T(8,128)(2,1)} %cot_hbm.1, ...), custom_call_target="tpu_custom_call" | custom-call | tf_op jit(solution)/shard_map/layer/pallas_call | solution.py:1030
  172.7 4.9 %finish.1 = (bf16[4,128,768]{2,1,0:T(8,128)(2,1)}, bf16[4,128,768]{2,1,0:T(8,128)(2,1)}, f32[4,768]{1,0:T(4,128)}, f32[768]{0:T(1024)}, f32[96,768]{1,0:T(8,128)...) custom-call(bf16[4,128,768]{2,1,0:T(8,128)(2,1)} %get-tuple-element., ...), custom_call_target="tpu_custom_call" | custom-call | tf_op jit(solution)/shard_map/finish/pallas_call | solution.py:1052

commit v3 on v2

--- a/solution.py
+++ b/solution.py
@@ -251,6 +251,171 @@
 GELU_A, GELU_B = math.sqrt(2 / math.pi), 0.044715
 
 
+AG, CR, BEGIN, RS, HALF, GO, XC, SHARE_A, FIN_B, FSUM, HOP = range(11)
+(
+    AT_A1, AT_NORM, AT_ATT, AT_WO, AT_IN, AT_COTW, AT_MFF, AT_FF, AT_FNORM, AT_PREWO, AT_GWO, AT_GMIX, AT_LAY,
+    AT_GX, AT_TAIL, AT_PROJECT, AT_ATTEND, AT_RESIDUAL, AT_WIDEN, AT_GFF, AT_GUP, AT_GIN, AT_GNF, AT_NARROW, AT_AB,
+    AT_GN,
+) = range(26)
+PLAN = {
+    AT_A1: (
+        (AG, 2, 0), (AG, 2, 4), (AG, 1, 0), (AG, 1, 4), (AG, 0, 0), (AG, 0, 4), (AG, 2, 1), (AG, 2, 5), (AG, 1, 1),
+        (AG, 1, 5), (AG, 0, 1), (AG, 0, 5), (AG, 2, 2),
+    ),
+    AT_NORM: (
+        (AG, 2, 6),
+    ),
+    AT_ATT: (
+        (CR, 2, 0), (AG, 1, 2), (CR, 2, 4), (AG, 1, 6), (CR, 2, 1), (AG, 0, 2), (BEGIN, 3), (BEGIN, 1), (CR, 2, 5),
+        (AG, 0, 6), (AG, 2, 3), (CR, 2, 2), (AG, 1, 3), (CR, 2, 6), (AG, 0, 3), (AG, 7, 0), (CR, 2, 3), (AG, 7, 4),
+        (AG, 4, 0),
+    ),
+    (AT_PROJECT, 0): (
+        (AG, 4, 4),
+    ),
+    (AT_PROJECT, 2): (
+        (AG, 3, 0),
+    ),
+    (AT_ATTEND, 0): (
+        (CR, 4, 0), (AG, 3, 4), (AG, 7, 1),
+    ),
+    (AT_ATTEND, 1): (
+        (AG, 7, 5), (AG, 4, 1), (AG, 4, 5),
+    ),
+    (AT_ATTEND, 2): (
+        (AG, 3, 1),
+    ),
+    (AT_ATTEND, 3): (
+        (AG, 3, 5), (AG, 7, 2),
+    ),
+    (AT_ATTEND, 4): (
+        (AG, 7, 6), (AG, 4, 2), (AG, 4, 6), (CR, 4, 4),
+    ),
+    (AT_ATTEND, 5): (
+        (AG, 3, 2), (CR, 4, 1), (BEGIN, 2),
+    ),
+    AT_WO: (
+        (AG, 3, 6), (CR, 4, 5), (AG, 7, 3), (AG, 4, 3), (CR, 4, 2),
+    ),
+    (AT_RESIDUAL, 1): (
+        (AG, 3, 3), (CR, 4, 6),
+    ),
+    AT_IN: (
+        (AG, 6, 0), (CR, 4, 3), (AG, 6, 4), (AG, 5, 0),
+    ),
+    (AT_WIDEN, 0): (
+        (AG, 5, 4),
+    ),
+    (AT_WIDEN, 1): (
+        (CR, 6, 0), (AG, 6, 1), (AG, 6, 5),
+    ),
+    (AT_WIDEN, 2): (
+        (CR, 6, 4), (AG, 5, 1),
+    ),
+    (AT_WIDEN, 3): (
+        (AG, 5, 5),
+    ),
+    (AT_GFF, 0): (
+        (AG, 6, 2),
+    ),
+    (AT_GFF, 1): (
+        (CR, 6, 1), (AG, 6, 6),
+    ),
+    (AT_GFF, 2): (
+        (AG, 5, 2),
+    ),
+    (AT_GFF, 3): (
+        (CR, 6, 5), (AG, 5, 6), (HALF, 0, 0),
+    ),
+    AT_MFF: (
+        (AG, 6, 3), (HALF, 0, 1), (CR, 6, 2), (AG, 5, 3), (HALF, 0, 2), (HALF, 0, 3), (GO, 0), (CR, 6, 6),
+    ),
+    AT_FF: (
+        (CR, 6, 3), (RS, 0, 0),
+    ),
+    (AT_GUP, 0): (
+        (RS, 0, 4),
+    ),
+    (AT_GUP, 1): (
+        (RS, 1, 0),
+    ),
+    (AT_GUP, 3): (
+        (RS, 1, 4),
+    ),
+    (AT_GIN, 0): (
+        (RS, 0, 1),
+    ),
+    (AT_GIN, 1): (
+        (RS, 0, 5),
+    ),
+    (AT_GIN, 2): (
+        (RS, 1, 1),
+    ),
+    (AT_GIN, 3): (
+        (RS, 1, 5), (XC, 0),
+    ),
+    (AT_GNF, 0): (
+        (RS, 0, 2),
+    ),
+    (AT_GNF, 2): (
+        (RS, 0, 6), (HALF, 1, 0),
+    ),
+    (AT_GNF, 3): (
+        (RS, 1, 2), (HALF, 1, 1), (RS, 1, 6),
+    ),
+    AT_FNORM: (
+        (RS, 2, 0), (HALF, 1, 2), (RS, 2, 4),
+    ),
+    AT_GWO: (
+        (HALF, 1, 3), (GO, 1), (RS, 0, 3),
+    ),
+    AT_GMIX: (
+        (RS, 1, 3), (SHARE_A, 0),
+    ),
+    (AT_NARROW, 0): (
+        (RS, 2, 1), (RS, 2, 5),
+    ),
+    (AT_NARROW, 1): (
+        (HALF, 2, 3), (GO, 5), (RS, 3, 0),
+    ),
+    (AT_NARROW, 3): (
+        (RS, 3, 4),
+    ),
+    AT_LAY: (
+        (RS, 4, 0),
+    ),
+    (AT_AB, 0): (
+        (RS, 4, 4), (RS, 2, 2), (RS, 2, 6), (RS, 9, 0),
+    ),
+    (AT_AB, 1): (
+        (RS, 9, 4), (RS, 3, 1), (XC, 1), (RS, 3, 5), (RS, 4, 1),
+    ),
+    (AT_AB, 2): (
+        (RS, 4, 5), (RS, 2, 3), (FIN_B, 0), (RS, 9, 1), (FSUM, 0), (HALF, 2, 0), (GO, 2), (RS, 9, 5),
+    ),
+    (AT_AB, 3): (
+        (RS, 3, 2), (RS, 5, 0), (RS, 5, 4), (RS, 3, 6), (RS, 4, 2), (RS, 4, 6),
+    ),
+    (AT_AB, 4): (
+        (RS, 9, 2), (RS, 6, 0), (RS, 6, 4), (HALF, 2, 1), (GO, 3), (RS, 9, 6),
+    ),
+    (AT_AB, 5): (
+        (RS, 3, 3), (RS, 5, 1), (RS, 5, 5), (RS, 4, 3), (SHARE_A, 1), (RS, 9, 3), (SHARE_A, 5),
+    ),
+    (AT_GN, 0): (
+        (RS, 6, 1), (RS, 6, 5),
+    ),
+    (AT_GN, 1): (
+        (RS, 7, 0), (RS, 7, 4), (HALF, 2, 2), (GO, 4),
+    ),
+    AT_TAIL: (
+        (RS, 5, 2), (RS, 5, 6), (RS, 6, 2), (RS, 6, 6), (RS, 7, 1), (FSUM, 1), (RS, 7, 5), (RS, 8, 0), (FSUM, 5),
+        (HOP, 0), (RS, 8, 4), (RS, 5, 3), (FIN_B, 1), (RS, 6, 3), (SHARE_A, 2), (HOP, 1), (RS, 7, 2), (RS, 7, 6),
+        (RS, 8, 1), (RS, 8, 5), (RS, 7, 3), (SHARE_A, 3), (HOP, 2), (RS, 8, 2), (RS, 8, 6), (RS, 8, 3), (SHARE_A, 4),
+        (HOP, 3), (FSUM, 2), (HOP, 4), (FSUM, 3), (FSUM, 4),
+    ),
+}
+
 def dg(left, right, on_left, on_right):
     return lax.dot_general(
         left, right, (((on_left,), (on_right,)), ((), ())), preferred_element_type=F32
@@ -352,15 +517,17 @@
     def piece(ch, d, cc, yy):
         if ch < 3:
             cols = pl.ds(128 + 256 * ch, 256) if ch < 2 else times(640 * yy, 128, 128)
-            return watt.at[:, times(96 * d + 48 * cc, 48, 48), cols]
+            return watt.at[0:3, times(96 * d + 48 * cc, 48, 48), cols]
         if ch < 5:
-            cols = pl.ds(1024, 1024) if ch == 3 else times(2048 * yy, 1024, 1024)
+            cols = pl.ds(768, 1536) if ch == 3 else times(2304 * yy, 768, 768)
             return win.at[d, cc, :, cols]
+        if ch == 7:
+            return watt.at[3, times(96 * d + 48 * cc, 48, 48)]
         cols = pl.ds(256, 256) if ch == 5 else times(512 * yy, 256, 256)
         return wff.at[times(384 * d + 192 * cc, 192, 192), cols]
 
     crossing = (2, 4, 6)
-    groups = ((0, 1, 2), (3, 4), (5, 6))
+    groups = ((0, 1, 2), (3, 4), (5, 6), (7,))
 
     def came_from(e):
         ahead = e // FAR
@@ -400,27 +567,17 @@
         send(part, part, yf_s.at[ch // 2 - 1, e], yf_r.at[ch // 2 - 1, e], yp).wait_recv()
         cross_on(ch, e).start()
 
-    def both(s):
-        return (s, FAR + s) if s < FAR - 1 else (s,)
-
-    def ticks(group, s):
-        for ch in reversed(groups[group]):
-            for e in both(s):
-                arrive(ch, e)
-        if s > 0:
-            for e in both(s - 1):
-                arrive_cross(groups[group][-1], e)
-
-    def gathered(group):
-        arrive_cross(groups[group][-1], FAR - 1)
+    def settled(group):
+        last = groups[group][-1]
 
         def step(e):
             d = owner(-came_from(e))
             for ch in groups[group]:
                 part = piece(ch, d, 1 - c, y)
                 send(part, part, sb_s.at[ch, e], sb_r.at[ch, e], sib).wait_recv()
-            part = piece(groups[group][-1], d, 1 - c, 1 - y)
-            send(part, part, yb_s.at[group, e], yb_r.at[group, e], sib).wait_recv()
+            if last in crossing:
+                part = piece(last, d, 1 - c, 1 - y)
+                send(part, part, yb_s.at[group, e], yb_r.at[group, e], sib).wait_recv()
 
         loop(EVENTS, step)
 
@@ -429,8 +586,9 @@
             for ch in groups[group]:
                 ring_send(ch, e).wait_send()
                 hand_on(ch, e).wait_send()
-            cross(groups[group][-1], e).wait_send()
-            cross_on(groups[group][-1], e).wait_send()
+            if groups[group][-1] in crossing:
+                cross(groups[group][-1], e).wait_send()
+                cross_on(groups[group][-1], e).wait_send()
 
         loop(EVENTS, step)
 
@@ -439,6 +597,20 @@
             ring_send(ch, 0).start()
             ring_send(ch, FAR).start()
 
+    acts = {AG: arrive, CR: arrive_cross, BEGIN: begin}
+
+    def serve(slot):
+        for name, *place in PLAN.get(slot, ()):
+            acts[name](*place)
+
+    def serve_at(slot, count, i):
+        for k in range(count):
+            if (slot, k) in PLAN:
+
+                @pl.when(i == k)
+                def _(k=k):
+                    serve((slot, k))
+
     for i in range(4):
         own[i].wait()
     begin(0)
@@ -447,11 +619,9 @@
     gain_a = attn_gain[...].reshape(1, WIDTH)
     gain_f = ffn_gain[...].reshape(1, WIDTH)
 
-    ticks(0, 0)
+    serve(AT_A1)
     own[7].wait()
     swap_wait(xs, 0)
-    for k in range(3):
-        swap(k, cot_hbm, cot, 1).start()
     for i in range(4, 7):
         own[i].wait()
 
@@ -463,17 +633,17 @@
 
     loop(4, norm_rows)
 
-    ticks(0, 1)
-    ticks(0, 2)
-    begin(1)
-    ticks(0, 3)
-    gathered(0)
+    serve(AT_NORM)
+    serve(AT_ATT)
+    settled(0)
+    for k in range(3):
+        swap(k, cot_hbm, cot, 1).start()
 
     def project(m):
         qkv[m] = dg(normed[...], watt[m], 1, 0).astype(BF)
+        serve_at(AT_PROJECT, 3, m)
 
     loop(3, project)
-    ticks(1, 0)
 
     count = lengths[sq]
     valid = lax.broadcasted_iota(jnp.int32, (1, TOKENS), 1) < count
@@ -515,21 +685,11 @@
                 total[ib] = one if h == 0 else total[ib] + one
         for ib in range(4):
             mixed[pl.ds(128 * ib, 128), cols] = total[ib].astype(BF)
-
-        @pl.when(hp == 1)
-        def _():
-            ticks(1, 1)
-
-        @pl.when(hp == 3)
-        def _():
-            ticks(1, 2)
-            begin(2)
-
-        @pl.when(hp == 5)
-        def _():
-            ticks(1, 3)
+        serve_at(AT_ATTEND, PAIRS, hp)
 
     loop(PAIRS, attend)
+    serve(AT_WO)
+    settled(3)
 
     def residual(b):
         rows = times(256 * b, 256, 256)
@@ -537,11 +697,12 @@
         hid[rows, :] = v
         s = lax.rsqrt(jnp.mean(v * v, axis=-1, keepdims=True) + EPS)
         nf[rows, :] = (v * s * gain_f).astype(BF)
+        serve_at(AT_RESIDUAL, 2, b)
 
     loop(2, residual)
 
-    ticks(2, 0)
-    gathered(1)
+    serve(AT_IN)
+    settled(1)
     up_rows, down_rows = pl.ds(0, TOKENS), pl.ds(TOKENS, TOKENS)
 
     def block(j):
@@ -558,16 +719,10 @@
         big[j, up_rows, :] = (v * half).astype(BF)
         slope = half + (v * half) * (1.0 - t) * (GELU_A + (3 * GELU_A * GELU_B) * sq_v)
         big[j, down_rows, :] = slope.astype(BF)
-
-        @pl.when(j == 1)
-        def _():
-            ticks(2, 1)
-
-        @pl.when(j == 3)
-        def _():
-            ticks(2, 2)
+        serve_at(AT_WIDEN, 4, j)
 
     loop(4, widen)
+    serve(AT_COTW)
     own[8].wait()
     swap_wait(cot, 1)
 
@@ -579,17 +734,14 @@
         v = dg(big[j, up_rows, :], cot[...], 0, 0).astype(BF)
         gff[pl.ds(2 * j, 2)] = v.reshape(2, 384, 768)
         half_ff(j).start()
-
-    loop(4, grad_ff)
-    ticks(2, 3)
+        serve_at(AT_GFF, 4, j)
+
 
     def merge_ff(j):
         half_ff(j).wait()
         rows = times(192 * c, 192, 192)
         for i in range(2):
             gff[2 * j + i, rows] = (gff[2 * j + i, rows].astype(F32) + sib_ff[2 * j + i].astype(F32)).astype(BF)
-
-    loop(4, merge_ff)
 
     def cross_src(g, yy):
         if g == 0:
@@ -628,41 +780,126 @@
         rs_send(ch, 0).start()
         rs_send(ch, FAR).start()
 
-    def rs_round(ch, s):
-        for e in both(s):
-            rs_send(ch, e).wait_recv()
-            here = rs_piece(ch, owner(FAR - 1 - e if e < FAR else e - EVENTS + 1), y)
-            here[...] = (here[...].astype(F32) + landing[ch][e].astype(F32)).astype(BF)
-            if e not in (FAR - 1, EVENTS - 1):
-                rs_send(ch, e + 1).start()
-
-    cross_sum(0).start()
-    rs_begin(0)
-    rs_begin(1)
-    gathered(2)
+    def rs_event(ch, e):
+        rs_send(ch, e).wait_recv()
+        here = rs_piece(ch, owner(FAR - 1 - e if e < FAR else e - EVENTS + 1), y)
+        here[...] = (here[...].astype(F32) + landing[ch][e].astype(F32)).astype(BF)
+        if e not in (FAR - 1, EVENTS - 1):
+            rs_send(ch, e + 1).start()
+
+    def half_in(k):
+        src = gin.at[:, times(1536 * (1 - c) + 384 * k, 384, 384)]
+        return send(src, sib_in.at[k], hs_s.at[1, k], hs_r.at[1, k], sib)
+
+    def merge_in(k):
+        half_in(k).wait()
+        cols = times(1536 * c + 384 * k, 384, 384)
+        gin[:, cols] = (gin[:, cols].astype(F32) + sib_in[k].astype(F32)).astype(BF)
+
+    def sib_rows(t):
+        return sib_ff.at[:, times(48 * t, 48, 48)]
+
+    def half_att(t):
+        return send(win.at[:, 1 - c, :, block(t)], sib_rows(t), hs_s.at[2, t], hs_r.at[2, t], sib)
+
+    def merge_att(t):
+        half_att(t).wait()
+        win[:, c, :, block(t)] = (win[:, c, :, block(t)].astype(F32) + sib_rows(t)[...].astype(F32)).astype(BF)
+
+    final = [f_ff, f_in] + [f_att.at[t] for t in range(4)]
+
+    def own_piece(g):
+        if g == 0:
+            return gff.at[dp, times(192 * c + 32, 128, 32)]
+        if g == 1:
+            return gin.at[r96, times(1536 * c + 256, 1024, 256)]
+        return rs_piece(4 + g, dp, y)
+
+    def out_piece(g, cc, yy):
+        if g == 0:
+            return gff_hbm.at[times(192 * cc + 32, 128, 32) if yy is None else times(192 * cc + 160 * yy, 32, 32)]
+        if g == 1:
+            if yy is None:
+                return gin_hbm.at[:, times(1536 * cc + 256, 1024, 256)]
+            return gin_hbm.at[:, times(1536 * cc + 1280 * yy, 256, 256)]
+        return gatt_hbm.at[g - 2, times(48 * cc, 48, 48)]
+
+    def share_a(g):
+        return send(own_piece(g), final[g], fa_s.at[g], fa_r.at[g], yp)
+
+    def share_b(g, k):
+        return send(rs_piece(3 * g + 2, dp, y), out_piece(g, c, y), fo_s.at[g, k], fo_r.at[g, k], peers[k])
+
+    def share_sum(g):
+        return send(final[g], out_piece(g, c, None), fo_s.at[g, 3], fo_r.at[g, 3], sib)
+
+    def keep_b(g):
+        return pltpu.make_async_copy(rs_piece(3 * g + 2, dp, y), out_piece(g, c, y), fl.at[g, 0])
+
+    def keep_sum(g):
+        return pltpu.make_async_copy(final[g], out_piece(g, c, None), fl.at[g, 1])
+
+    def finish_b(g):
+        for k in range(3):
+            share_b(g, k).start()
+        keep_b(g).start()
+
+    def finish_sum(g):
+        share_a(g).wait()
+        final[g][...] = (final[g][...].astype(F32) + own_piece(g)[...].astype(F32)).astype(BF)
+        share_sum(g).start()
+        keep_sum(g).start()
+
+    def hop(k):
+        dev = (yp, sib, xp, z1, z2)[k]
+        return send(sums.at[k], sums_in.at[k], bf_s.at[k], bf_r.at[k], dev)
+
+    def hop_done(k):
+        hop(k).wait()
+        sums[k + 1] = sums[k] + sums_in[k]
+
+    def merge(g, k):
+        (merge_ff, merge_in, merge_att)[g](k)
+
+    def go(g):
+        if g < 2:
+            cross_sum(g).start()
+            rs_begin(3 * g)
+            rs_begin(3 * g + 1)
+        else:
+            rs_begin(4 + g)
+
+    def cross_in(g):
+        add_cross(g)
+        rs_begin(3 * g + 2)
+
+    def hop_on(k):
+        hop_done(k)
+        if k < 4:
+            hop(k + 1).start()
+
+    acts |= {
+        RS: rs_event, HALF: merge, GO: go, XC: cross_in, SHARE_A: lambda g: share_a(g).start(), FIN_B: finish_b,
+        FSUM: finish_sum, HOP: hop_on,
+    }
+
+    loop(4, grad_ff)
+    serve(AT_MFF)
+    serve(AT_FF)
+    settled(2)
 
     def grad_up(j):
         v = dg(cot[...], wff[block(j), :], 1, 1) * big[j, down_rows, :].astype(F32)
         big[j, down_rows, :] = v.astype(BF)
+        serve_at(AT_GUP, 4, j)
 
     loop(4, grad_up)
 
     def grad_in(j):
         gin[:, block(j)] = dg(nf[...], big[j, down_rows, :], 0, 0).astype(BF)
-
-        @pl.when(j == 1)
-        def _():
-            rs_round(0, 0)
-
-        @pl.when(j == 3)
-        def _():
-            rs_round(1, 0)
+        serve_at(AT_GIN, 4, j)
 
     loop(4, grad_in)
-
-    def half_in(k):
-        src = gin.at[:, times(1536 * (1 - c) + 384 * k, 384, 384)]
-        return send(src, sib_in.at[k], hs_s.at[1, k], hs_r.at[1, k], sib)
 
     for k in range(4):
         half_in(k).start()
@@ -671,22 +908,9 @@
 
     def grad_nf(j):
         acc[...] += dg(big[j, down_rows, :], win_block(j), 1, 1)
-
-        @pl.when(j == 2)
-        def _():
-            rs_round(0, 1)
+        serve_at(AT_GNF, 4, j)
 
     loop(4, grad_nf)
-    add_cross(0)
-    rs_begin(2)
-
-    for k in range(4):
-        half_in(k).wait()
-        cols = times(1536 * c + 384 * k, 384, 384)
-        gin[:, cols] = (gin[:, cols].astype(F32) + sib_in[k].astype(F32)).astype(BF)
-    cross_sum(1).start()
-    rs_begin(3)
-    rs_begin(4)
 
     def norm_back(v, gain, grad):
         s = lax.rsqrt(jnp.mean(v * v, axis=-1, keepdims=True) + EPS)
@@ -705,68 +929,50 @@
 
     g_ffn_gain = lax.fori_loop(0, 4, ffn_norm_back, jnp.zeros((1, WIDTH), F32))
 
-    rs_round(1, 1)
+    serve(AT_FNORM)
+    serve(AT_PREWO)
     gather_sent(1)
     win[:, :, :, block(3)] = dg(mixed[...], cot[...], 0, 0).astype(BF).reshape(8, 2, 48, 768)
 
-    def sib_rows(t):
-        return sib_ff.at[:, times(48 * t, 48, 48)]
-
-    def half_att(t):
-        return send(win.at[:, 1 - c, :, block(t)], sib_rows(t), hs_s.at[2, t], hs_r.at[2, t], sib)
-
-    def merge_att(t):
-        half_att(t).wait()
-        win[:, c, :, block(t)] = (win[:, c, :, block(t)].astype(F32) + sib_rows(t)[...].astype(F32)).astype(BF)
-
     half_att(3).start()
+    serve(AT_GWO)
     nf[...] = dg(cot[...], watt[3], 1, 1).astype(BF)
-
-    final = [f_ff, f_in] + [f_att.at[t] for t in range(4)]
-
-    def own_piece(g):
-        if g == 0:
-            return gff.at[dp, times(192 * c + 32, 128, 32)]
-        if g == 1:
-            return gin.at[r96, times(1536 * c + 256, 1024, 256)]
-        return rs_piece(4 + g, dp, y)
-
-    def out_piece(g, cc, yy):
-        if g == 0:
-            return gff_hbm.at[times(192 * cc + 32, 128, 32) if yy is None else times(192 * cc + 160 * yy, 32, 32)]
-        if g == 1:
-            if yy is None:
-                return gin_hbm.at[:, times(1536 * cc + 256, 1024, 256)]
-            return gin_hbm.at[:, times(1536 * cc + 1280 * yy, 256, 256)]
-        return gatt_hbm.at[g - 2, times(48 * cc, 48, 48)]
-
-    def share_a(g):
-        return send(own_piece(g), final[g], fa_s.at[g], fa_r.at[g], yp)
-
-    def share_b(g, k):
-        return send(rs_piece(3 * g + 2, dp, y), out_piece(g, c, y), fo_s.at[g, k], fo_r.at[g, k], peers[k])
-
-    def share_sum(g):
-        return send(final[g], out_piece(g, c, None), fo_s.at[g, 3], fo_r.at[g, 3], sib)
-
-    def keep_b(g):
-        return pltpu.make_async_copy(rs_piece(3 * g + 2, dp, y), out_piece(g, c, y), fl.at[g, 0])
-
-    def keep_sum(g):
-        return pltpu.make_async_copy(final[g], out_piece(g, c, None), fl.at[g, 1])
-
-    def finish_b(g):
+    serve(AT_GMIX)
+
+
+    def give(src, dst_hbm, at, k):
+        dev = peers[k]
+        return send(src.at[times(128 * dev[1], 128, 128)], dst_hbm.at[sq], a2_s.at[at, k], a2_r.at[at, k], dev)
+
+    def give_wait(src, dst_hbm, at):
         for k in range(3):
-            share_b(g, k).start()
-        keep_b(g).start()
-
-    def finish_sum(g):
-        share_a(g).wait()
-        final[g][...] = (final[g][...].astype(F32) + own_piece(g)[...].astype(F32)).astype(BF)
-        share_sum(g).start()
-        keep_sum(g).start()
-
-    rs_round(0, 2)
+            give(src, dst_hbm, at, k).wait_send()
+            theirs = dst_hbm.at[peers[k][1]]
+            send(theirs, theirs, a2_s.at[at, k], a2_r.at[at, k], peers[k]).wait_recv()
+
+    def pool_send(k):
+        return send(pool, pool_hbm.at[sq], a2_s.at[4, k], a2_r.at[4, k], peers[k])
+
+    pool_own = pltpu.make_async_copy(pool, pool_hbm.at[sq], loc.at[2])
+    lay = big.at[0, up_rows]
+    lay_own = pltpu.make_async_copy(lay.at[mine], out_hbm.at[sq], loc.at[1])
+    def narrow(j):
+        part = dg(big[j, up_rows, :], wff[block(j), :], 1, 0)
+        hid[...] += part
+        serve_at(AT_NARROW, 4, j)
+
+    loop(4, narrow)
+    lay[...] = hid[...].astype(BF)
+    for k in range(3):
+        give(lay, out_hbm, 2, k).start()
+    lay_own.start()
+    here_t = lax.broadcasted_iota(jnp.int32, (TOKENS, 1), 0) < count
+    mean = jnp.sum(jnp.where(here_t, hid[...], 0.0), axis=0, keepdims=True) / count.astype(F32)
+    pool[...] = jnp.broadcast_to(mean, (8, WIDTH))
+    pool_own.start()
+    for k in range(3):
+        pool_send(k).start()
+    serve(AT_LAY)
 
     flip_sum = lax.broadcasted_iota(jnp.int32, (128, 128), 0) + lax.broadcasted_iota(jnp.int32, (128, 128), 1)
     flip = (flip_sum == 127).astype(F32)
@@ -825,64 +1031,18 @@
             win[:, :, :, block(t)] = dg(normed[...], grads, 0, 0).astype(BF).reshape(8, 2, 48, 768)
             half_att(t).start()
 
-        def plan(at, *steps):
-            @pl.when(hp == at)
-            def _():
-                for step in steps:
-                    step()
-
-        def round_of(ch, s):
-            return lambda: rs_round(ch, s)
-
-        def start_block(t):
-            def run():
-                merge_att(t)
-                rs_begin(6 + t)
-
-            return run
-
-        def start_in():
-            add_cross(1)
-            rs_begin(5)
-
-        plan(0, round_of(1, 2), round_of(0, 3), round_of(2, 0), start_block(3))
-        plan(1, round_of(1, 3), round_of(2, 1), share_a(0).start, round_of(3, 0), round_of(9, 0))
-        plan(2, round_of(4, 0), round_of(2, 2), round_of(3, 1), round_of(9, 1), start_in, start_block(0))
-        plan(3, lambda: finish_sum(0), round_of(4, 1), round_of(2, 3), round_of(9, 2), round_of(5, 0), round_of(6, 0))
-        plan(4, round_of(3, 2), round_of(4, 2), round_of(9, 3), round_of(5, 1), round_of(6, 1), start_block(1))
-        plan(5, round_of(3, 3), round_of(4, 3), round_of(5, 2), round_of(6, 2), round_of(7, 0))
+        serve_at(AT_AB, PAIRS, hp)
 
     loop(PAIRS, attend_back)
-    finish_b(0)
-    share_a(1).start()
-    share_a(5).start()
-
-    merge_att(2)
-    rs_begin(8)
-
     def attn_norm_back(b, total):
         rows = times(256 * b, 256, 256)
         grad = dg(qkv[0, rows, :], watt[0], 1, 1) + dg(qkv[1, rows, :], watt[1], 1, 1) + dg(qkv[2, rows, :], watt[2], 1, 1)
         back, part = norm_back(xs[rows, :].astype(F32), gain_a, grad)
         mixed[rows, :] = (acc[rows, :] + back).astype(BF)
+        serve_at(AT_GN, 2, b)
         return total + part
 
     g_attn_gain = lax.fori_loop(0, 2, attn_norm_back, jnp.zeros((1, WIDTH), F32))
-
-    def give(src, dst_hbm, at, k):
-        dev = peers[k]
-        return send(src.at[times(128 * dev[1], 128, 128)], dst_hbm.at[sq], a2_s.at[at, k], a2_r.at[at, k], dev)
-
-    def give_wait(src, dst_hbm, at):
-        for k in range(3):
-            give(src, dst_hbm, at, k).wait_send()
-            theirs = dst_hbm.at[peers[k][1]]
-            send(theirs, theirs, a2_s.at[at, k], a2_r.at[at, k], peers[k]).wait_recv()
-
-    for k in range(3):
-        give(mixed, gx_hbm, 3, k).start()
-    gx_own = pltpu.make_async_copy(mixed.at[mine], gx_hbm.at[sq], loc.at[0])
-    gx_own.start()
 
     sums[0] = jnp.zeros((32, 128), F32)
     sums[0, 0:16, 0:32] = exact(diag[...], band_bucket(32), 1, 1)
@@ -890,57 +1050,14 @@
         sums[0, 16 + k : 17 + k, :] = g_attn_gain[:, 128 * k : 128 * (k + 1)]
         sums[0, 22 + k : 23 + k, :] = g_ffn_gain[:, 128 * k : 128 * (k + 1)]
 
-    def hop(k):
-        dev = (sib, yp, xp, z1, z2)[k]
-        return send(sums.at[k], sums_in.at[k], bf_s.at[k], bf_r.at[k], dev)
-
-    def hop_done(k):
-        hop(k).wait()
-        sums[k + 1] = sums[k] + sums_in[k]
-
-    def pool_send(k):
-        return send(pool, pool_hbm.at[sq], a2_s.at[4, k], a2_r.at[4, k], peers[k])
-
-    pool_own = pltpu.make_async_copy(pool, pool_hbm.at[sq], loc.at[2])
-    lay_own = pltpu.make_async_copy(nf.at[mine], out_hbm.at[sq], loc.at[1])
     hop(0).start()
-    for r in range(5):
-        if r < 4:
-            part = dg(big[r, up_rows, :], wff[block(r), :], 1, 0)
-            acc[...] = part + (hid[...] if r == 0 else acc[...])
-        if r == 0:
-            rs_round(6, 3)
-            share_a(2).start()
-            rs_round(5, 3)
-            finish_b(1)
-        if r < 3:
-            rs_round(7, r + 1)
-        if r == 2:
-            share_a(3).start()
-        if r > 0:
-            rs_round(8, r - 1)
-        hop_done(r)
-        if r < 4:
-            hop(r + 1).start()
-        if r == 1:
-            finish_sum(1)
-            finish_sum(5)
-        if r == 3:
-            nf[...] = acc[...].astype(BF)
-            for k in range(3):
-                give(nf, out_hbm, 2, k).start()
-            lay_own.start()
-            here_t = lax.broadcasted_iota(jnp.int32, (TOKENS, 1), 0) < count
-            mean = jnp.sum(jnp.where(here_t, acc[...], 0.0), axis=0, keepdims=True) / count.astype(F32)
-            pool[...] = jnp.broadcast_to(mean, (8, WIDTH))
-            pool_own.start()
-            for k in range(3):
-                pool_send(k).start()
-            finish_sum(2)
-    share_a(4).start()
+    for k in range(3):
+        give(mixed, gx_hbm, 3, k).start()
+    gx_own = pltpu.make_async_copy(mixed.at[mine], gx_hbm.at[sq], loc.at[0])
+    gx_own.start()
+    serve(AT_GX)
+    serve(AT_TAIL)
     small_out[...] = sums[5]
-    finish_sum(3)
-    finish_sum(4)
 
     for g in range(6):
         if g < 2:
@@ -961,7 +1078,8 @@
     loop(EVENTS, ring_sent)
     gather_sent(0)
     gather_sent(2)
-    give_wait(nf, out_hbm, 2)
+    gather_sent(3)
+    give_wait(lay, out_hbm, 2)
     give_wait(mixed, gx_hbm, 3)
     lay_own.wait()
     gx_own.wait()
@@ -975,25 +1093,47 @@
 
 
 def finish_kernel(
-    out_in, gx_in, g_att, g_in, g_ff, pooled, small,
-    out, gx, pool_out, gain_a, gq, gk, gv, go, g_table, gain_f, gin_out, gff_out, sem,
+    out_in, gx_in, att_in, in_in, ff_in, pool_in, small_in,
+    out, gx, pool_out, gain_a, gq, gk, gv, go, g_table, gain_f, gin_out, gff_out,
+    v_out, v_gx, v_att, v_in, v_ff, v_pool, w_att, w_in, w_ff, w_pool, sem_in, sem_out,
 ):
-    copies = [pltpu.make_async_copy(out_in, out, sem.at[0]), pltpu.make_async_copy(gx_in, gx, sem.at[1])]
-    for copy in copies:
-        copy.start()
+    sources = (in_in, ff_in, att_in, pool_in, out_in, gx_in)
+    held = (v_in, v_ff, v_att, v_pool, v_out, v_gx)
+    reads = [pltpu.make_async_copy(a, b, sem_in.at[k]) for k, (a, b) in enumerate(zip(sources, held))]
+    for read in reads:
+        read.start()
+    g_table[...] = small_in[0:HEAD_N, 0:32]
+    for k in range(6):
+        gain_a[128 * k : 128 * (k + 1)] = small_in[16 + k : 17 + k, :].reshape(128)
+        gain_f[128 * k : 128 * (k + 1)] = small_in[22 + k : 23 + k, :].reshape(128)
+    writes = []
+
+    def write(src, dst):
+        writes.append(pltpu.make_async_copy(src, dst, sem_out.at[len(writes)]))
+        writes[-1].start()
+
+    reads[0].wait()
+    w_in[...] = v_in[...].astype(F32)
+    write(w_in, gin_out)
+    reads[1].wait()
+    w_ff[...] = v_ff[...].astype(F32)
+    write(w_ff, gff_out)
+    reads[2].wait()
+    w_att[3] = v_att[3].astype(F32)
     for t in range(3):
-        for i, ref in enumerate((gq, gk, gv)):
-            ref[:, 256 * t : 256 * (t + 1)] = g_att[t, :, 256 * i : 256 * (i + 1)].astype(F32)
-    go[...] = g_att[3].astype(F32)
-    gin_out[...] = g_in[...].astype(F32)
-    gff_out[...] = g_ff[...].astype(F32)
+        for i in range(3):
+            w_att[i, :, 256 * t : 256 * (t + 1)] = v_att[t, :, 256 * i : 256 * (i + 1)].astype(F32)
+    for i, ref in enumerate((gq, gk, gv, go)):
+        write(w_att.at[i], ref)
+    reads[3].wait()
     for p in range(SEQ):
-        pool_out[p : p + 1, :] = pooled[p, 0:1, :]
-    g_table[...] = small[0:HEAD_N, 0:32]
-    for k in range(6):
-        gain_a[128 * k : 128 * (k + 1)] = small[16 + k : 17 + k, :].reshape(128)
-        gain_f[128 * k : 128 * (k + 1)] = small[22 + k : 23 + k, :].reshape(128)
-    for copy in copies:
+        w_pool[p : p + 1, :] = v_pool[p, 0:1, :]
+    write(w_pool, pool_out)
+    reads[4].wait()
+    write(v_out, out)
+    reads[5].wait()
+    write(v_gx, gx)
+    for copy in writes:
         copy.wait()
 
 
@@ -1023,7 +1163,7 @@
     scratch += [
         dma(shape)
         for shape in (
-            (7, 7), (7, 7), (7, 7), (7, 7), (3, 7), (3, 7), (3, 7), (3, 7), (10, 7), (10, 7), (9,), (5, 3), (5, 3),
+            (8, 7), (8, 7), (8, 7), (8, 7), (3, 7), (3, 7), (3, 7), (3, 7), (10, 7), (10, 7), (9,), (5, 3), (5, 3),
             (3, 4), (3, 4), (2,), (2,), (6,), (6,), (6, 4), (6, 4), (6, 2), (5,), (5,),
         )
     ]
@@ -1065,9 +1205,22 @@
             jax.ShapeDtypeStruct((96, 3072), F32),
             jax.ShapeDtypeStruct((384, 768), F32),
         ),
-        in_specs=[vmem] * 7,
-        out_specs=(any_space,) * 2 + (vmem,) * 10,
-        scratch_shapes=[dma((2,))],
+        in_specs=[any_space] * 6 + [vmem],
+        out_specs=(any_space,) * 3 + (vmem,) + (any_space,) * 4 + (vmem,) * 2 + (any_space,) * 2,
+        scratch_shapes=[
+            pltpu.VMEM((4, 128, 768), BF),
+            pltpu.VMEM((4, 128, 768), BF),
+            pltpu.VMEM((4, 96, 768), BF),
+            pltpu.VMEM((96, 3072), BF),
+            pltpu.VMEM((384, 768), BF),
+            pltpu.VMEM((4, 8, 768), F32),
+            pltpu.VMEM((4, 96, 768), F32),
+            pltpu.VMEM((96, 3072), F32),
+            pltpu.VMEM((384, 768), F32),
+            pltpu.VMEM((4, 768), F32),
+            dma((6,)),
+            dma((9,)),
+        ],
         compiler_params=pltpu.CompilerParams(vmem_limit_bytes=64 * 2**20),
         name="finish",
     )(*sums)

time: 178 us -> 149 us (0.84)
  Pallas kernels: 177 us -> 148 us
    pallas_call x1, Pallas kernels: 172 us -> 143 us  [passage_shards(): pl.pallas_call(layer_kernel, out_shape=(jax.ShapeDtypeStruct((4, 128, 768...]
where the time goes in v3:
time: 149 us
  Pallas kernels  148 us (99%)
    pallas_call x1, Pallas kernels, passage_shards(): pl.pallas_call(layer_kernel, out_shape=(jax.ShapeDtypeStruct((4, 128, 768...  143 us
    pallas_call x1, Pallas kernels, passage_shards(): pl.pallas_call(finish_kernel, out_shape=(jax.ShapeDtypeStruct((4, 128, 76...  4.9 us

profile of v3, /device:TPU:0, one launch (start us, length us, event | category | flops | bytes accessed | tf_op | source)
XLA Modules:
  0.0 148.7 jit_solution(9376293324991419260)
XLA Ops:
  0.6 143.0 %layer.1 = (bf16[4,128,768]{2,1,0:T(8,128)(2,1)}, bf16[4,128,768]{2,1,0:T(8,128)(2,1)}, bf16[4,96,768]{2,1,0:T(8,128)(2,1)}, bf16[96,3072]{1,0:T(8,128)(2,1)}, b...) custom-call(bf16[4,128,768]{2,1,0:T(8,128)(2,1)} %x_hbm.1, bf16[4,128,768]{2,1,0:T(8,128)(2,1)} %cot_hbm.1, ...), custom_call_target="tpu_custom_call" | custom-call | tf_op jit(solution)/shard_map/layer/pallas_call | solution.py:1170
  143.7 4.9 %finish.1 = (bf16[4,128,768]{2,1,0:T(8,128)(2,1)}, bf16[4,128,768]{2,1,0:T(8,128)(2,1)}, f32[4,768]{1,0:T(4,128)}, f32[768]{0:T(1024)}, f32[96,768]{1,0:T(8,128)...) custom-call(bf16[4,128,768]{2,1,0:T(8,128)(2,1)} %get-tuple-element., ...), custom_call_target="tpu_custom_call" | custom-call | tf_op jit(solution)/shard_map/finish/pallas_call | solution.py:1192

commit v4 on v3

--- a/solution.py
+++ b/solution.py
@@ -251,7 +251,7 @@
 GELU_A, GELU_B = math.sqrt(2 / math.pi), 0.044715
 
 
-AG, CR, BEGIN, RS, HALF, GO, XC, SHARE_A, FIN_B, FSUM, HOP = range(11)
+AG, CR, BEGIN, RS, HALF, GO, XC, SHARE_A, FIN_B, FSUM, HOP, LEAVE = range(12)
 (
     AT_A1, AT_NORM, AT_ATT, AT_WO, AT_IN, AT_COTW, AT_MFF, AT_FF, AT_FNORM, AT_PREWO, AT_GWO, AT_GMIX, AT_LAY,
     AT_GX, AT_TAIL, AT_PROJECT, AT_ATTEND, AT_RESIDUAL, AT_WIDEN, AT_GFF, AT_GUP, AT_GIN, AT_GNF, AT_NARROW, AT_AB,
@@ -280,19 +280,19 @@
         (CR, 4, 0), (AG, 3, 4), (AG, 7, 1),
     ),
     (AT_ATTEND, 1): (
-        (AG, 7, 5), (AG, 4, 1), (AG, 4, 5),
+        (AG, 7, 5), (AG, 4, 1),
     ),
     (AT_ATTEND, 2): (
-        (AG, 3, 1),
+        (AG, 4, 5), (AG, 3, 1),
     ),
     (AT_ATTEND, 3): (
         (AG, 3, 5), (AG, 7, 2),
     ),
     (AT_ATTEND, 4): (
-        (AG, 7, 6), (AG, 4, 2), (AG, 4, 6), (CR, 4, 4),
+        (AG, 7, 6), (AG, 4, 2),
     ),
     (AT_ATTEND, 5): (
-        (AG, 3, 2), (CR, 4, 1), (BEGIN, 2),
+        (AG, 4, 6), (CR, 4, 4), (AG, 3, 2), (CR, 4, 1), (BEGIN, 2),
     ),
     AT_WO: (
         (AG, 3, 6), (CR, 4, 5), (AG, 7, 3), (AG, 4, 3), (CR, 4, 2),
@@ -301,118 +301,113 @@
         (AG, 3, 3), (CR, 4, 6),
     ),
     AT_IN: (
-        (AG, 6, 0), (CR, 4, 3), (AG, 6, 4), (AG, 5, 0),
+        (AG, 6, 0), (AG, 6, 4), (CR, 4, 3), (AG, 5, 0),
     ),
     (AT_WIDEN, 0): (
-        (AG, 5, 4),
+        (AG, 5, 4), (AG, 6, 1), (CR, 6, 0),
     ),
     (AT_WIDEN, 1): (
-        (CR, 6, 0), (AG, 6, 1), (AG, 6, 5),
+        (AG, 6, 5),
     ),
     (AT_WIDEN, 2): (
-        (CR, 6, 4), (AG, 5, 1),
+        (AG, 5, 1), (CR, 6, 4),
     ),
     (AT_WIDEN, 3): (
-        (AG, 5, 5),
-    ),
-    (AT_GFF, 0): (
-        (AG, 6, 2),
+        (AG, 5, 5), (AG, 6, 2), (CR, 6, 1),
     ),
     (AT_GFF, 1): (
-        (CR, 6, 1), (AG, 6, 6),
+        (AG, 6, 6),
     ),
     (AT_GFF, 2): (
-        (AG, 5, 2),
+        (AG, 5, 2), (CR, 6, 5),
     ),
     (AT_GFF, 3): (
-        (CR, 6, 5), (AG, 5, 6), (HALF, 0, 0),
+        (AG, 5, 6), (HALF, 0, 0), (LEAVE, 0),
     ),
     AT_MFF: (
-        (AG, 6, 3), (HALF, 0, 1), (CR, 6, 2), (AG, 5, 3), (HALF, 0, 2), (HALF, 0, 3), (GO, 0), (CR, 6, 6),
+        (AG, 6, 3), (CR, 6, 2), (HALF, 0, 1), (HALF, 0, 2), (LEAVE, 4), (AG, 5, 3), (CR, 6, 6), (HALF, 0, 3), (GO, 0),
+        (RS, 0, 0),
     ),
     AT_FF: (
-        (CR, 6, 3), (RS, 0, 0),
+        (RS, 1, 0), (CR, 6, 3), (RS, 0, 4),
     ),
     (AT_GUP, 0): (
-        (RS, 0, 4),
+        (RS, 1, 4),
     ),
     (AT_GUP, 1): (
-        (RS, 1, 0),
+        (RS, 0, 1),
+    ),
+    (AT_GUP, 2): (
+        (RS, 1, 1),
     ),
     (AT_GUP, 3): (
-        (RS, 1, 4),
-    ),
-    (AT_GIN, 0): (
-        (RS, 0, 1),
+        (RS, 0, 5),
     ),
     (AT_GIN, 1): (
-        (RS, 0, 5),
+        (RS, 1, 5),
     ),
     (AT_GIN, 2): (
-        (RS, 1, 1),
+        (RS, 0, 2),
     ),
     (AT_GIN, 3): (
-        (RS, 1, 5), (XC, 0),
+        (RS, 1, 2),
     ),
     (AT_GNF, 0): (
-        (RS, 0, 2),
+        (RS, 0, 6), (HALF, 1, 0), (XC, 0),
+    ),
+    (AT_GNF, 1): (
+        (RS, 1, 6), (HALF, 1, 1),
     ),
     (AT_GNF, 2): (
-        (RS, 0, 6), (HALF, 1, 0),
+        (RS, 0, 3), (HALF, 1, 2), (RS, 1, 3), (SHARE_A, 0),
     ),
     (AT_GNF, 3): (
-        (RS, 1, 2), (HALF, 1, 1), (RS, 1, 6),
-    ),
-    AT_FNORM: (
-        (RS, 2, 0), (HALF, 1, 2), (RS, 2, 4),
-    ),
-    AT_GWO: (
-        (HALF, 1, 3), (GO, 1), (RS, 0, 3),
-    ),
-    AT_GMIX: (
-        (RS, 1, 3), (SHARE_A, 0),
+        (HALF, 1, 3), (GO, 1), (RS, 2, 0), (RS, 2, 4),
     ),
     (AT_NARROW, 0): (
-        (RS, 2, 1), (RS, 2, 5),
+        (RS, 3, 0),
     ),
     (AT_NARROW, 1): (
-        (HALF, 2, 3), (GO, 5), (RS, 3, 0),
+        (RS, 3, 4), (HALF, 2, 3), (GO, 5),
+    ),
+    (AT_NARROW, 2): (
+        (FSUM, 0), (RS, 4, 0),
     ),
     (AT_NARROW, 3): (
-        (RS, 3, 4),
-    ),
-    AT_LAY: (
-        (RS, 4, 0),
+        (RS, 4, 4), (RS, 2, 1),
     ),
     (AT_AB, 0): (
-        (RS, 4, 4), (RS, 2, 2), (RS, 2, 6), (RS, 9, 0),
+        (RS, 2, 5), (RS, 3, 1), (RS, 3, 5), (RS, 9, 0),
     ),
     (AT_AB, 1): (
-        (RS, 9, 4), (RS, 3, 1), (XC, 1), (RS, 3, 5), (RS, 4, 1),
+        (RS, 9, 4), (RS, 4, 1), (RS, 4, 5), (XC, 1), (RS, 2, 2), (RS, 2, 6),
     ),
     (AT_AB, 2): (
-        (RS, 4, 5), (RS, 2, 3), (FIN_B, 0), (RS, 9, 1), (FSUM, 0), (HALF, 2, 0), (GO, 2), (RS, 9, 5),
+        (RS, 3, 2), (RS, 3, 6), (RS, 9, 1), (HALF, 2, 0), (GO, 2), (RS, 9, 5),
     ),
     (AT_AB, 3): (
-        (RS, 3, 2), (RS, 5, 0), (RS, 5, 4), (RS, 3, 6), (RS, 4, 2), (RS, 4, 6),
+        (RS, 4, 2), (RS, 4, 6), (RS, 5, 0), (RS, 5, 4), (RS, 2, 3), (FIN_B, 0), (RS, 3, 3),
     ),
     (AT_AB, 4): (
         (RS, 9, 2), (RS, 6, 0), (RS, 6, 4), (HALF, 2, 1), (GO, 3), (RS, 9, 6),
     ),
     (AT_AB, 5): (
-        (RS, 3, 3), (RS, 5, 1), (RS, 5, 5), (RS, 4, 3), (SHARE_A, 1), (RS, 9, 3), (SHARE_A, 5),
+        (RS, 4, 3), (SHARE_A, 1), (RS, 5, 1), (RS, 5, 5), (RS, 9, 3), (SHARE_A, 5), (RS, 6, 1),
     ),
     (AT_GN, 0): (
-        (RS, 6, 1), (RS, 6, 5),
+        (RS, 6, 5), (RS, 7, 0),
     ),
     (AT_GN, 1): (
-        (RS, 7, 0), (RS, 7, 4), (HALF, 2, 2), (GO, 4),
+        (RS, 7, 4), (HALF, 2, 2), (GO, 4), (RS, 5, 2),
+    ),
+    AT_GX: (
+        (RS, 5, 6),
     ),
     AT_TAIL: (
-        (RS, 5, 2), (RS, 5, 6), (RS, 6, 2), (RS, 6, 6), (RS, 7, 1), (FSUM, 1), (RS, 7, 5), (RS, 8, 0), (FSUM, 5),
-        (HOP, 0), (RS, 8, 4), (RS, 5, 3), (FIN_B, 1), (RS, 6, 3), (SHARE_A, 2), (HOP, 1), (RS, 7, 2), (RS, 7, 6),
-        (RS, 8, 1), (RS, 8, 5), (RS, 7, 3), (SHARE_A, 3), (HOP, 2), (RS, 8, 2), (RS, 8, 6), (RS, 8, 3), (SHARE_A, 4),
-        (HOP, 3), (FSUM, 2), (HOP, 4), (FSUM, 3), (FSUM, 4),
+        (RS, 6, 2), (RS, 6, 6), (RS, 7, 1), (FSUM, 1), (RS, 7, 5), (RS, 8, 0), (FSUM, 5), (RS, 8, 4), (RS, 5, 3),
+        (FIN_B, 1), (RS, 6, 3), (SHARE_A, 2), (RS, 7, 2), (HOP, 0), (RS, 7, 6), (RS, 8, 1), (RS, 8, 5), (RS, 7, 3),
+        (SHARE_A, 3), (HOP, 1), (RS, 8, 2), (RS, 8, 6), (RS, 8, 3), (SHARE_A, 4), (FSUM, 2), (HOP, 2), (FSUM, 3),
+        (FSUM, 4),
     ),
 }
 
@@ -448,9 +443,9 @@
     x_hbm, cot_hbm, wq_hbm, wk_hbm, wv_hbm, wo_hbm, win_hbm, wff_hbm, lengths, attn_gain, ffn_gain, table,
     out_hbm, gx_hbm, gatt_hbm, gin_hbm, gff_hbm, pool_hbm, small_out,
     watt, win, wff, gin, gff, big, probs, xs, cot, normed, qkv, mixed, nf, hid, acc, band, diag, d_both,
-    sib_ff, sib_in, y_ff, y_in, r_ffa, r_ffb, r_ina, r_inb, r_att, f_ff, f_in, f_att, sums, sums_in, pool,
-    ag_s, ag_r, sb_s, sb_r, yf_s, yf_r, yb_s, yb_r, rr_s, rr_r, loc, a2_s, a2_r, hs_s, hs_r, yx_s, yx_r,
-    fa_s, fa_r, fo_s, fo_r, fl, bf_s, bf_r,
+    sib_ff, sib_in, y_ff, y_in, r_ffa, r_ffb, r_ina, r_inb, r_att, f_ff, f_in, f_att, sums, sums_in, spread, pool,
+    ag_s, ag_r, sb_s, sb_r, yf_s, yf_r, yb_s, yb_r, rr_s, loc, a2_s, a2_r, hs_s, hs_r, yx_s, yx_r,
+    fa_s, fa_r, fb_s, fb_r, fo_s, fo_r, fl, bf_s, bf_r,
 ):
     dp, sq = lax.axis_index("dp"), lax.axis_index("seq")
     z, x, y, c = dp // 2, dp % 2, sq // 2, sq % 2
@@ -460,12 +455,9 @@
     def owner(steps):
         return ring_dp((place + steps * turn + 16) % 8)
 
-    nxt, prv = (owner(1), sq), (owner(-1), sq)
     sib, yp, ysib = (dp, 2 * y + 1 - c), (dp, 2 * (1 - y) + c), (dp, 2 * (1 - y) + 1 - c)
-    xp = (2 * z + 1 - x, sq)
-    z1 = (2 * (z + 1 - 2 * (z % 2)) + x, sq)
-    z2 = (2 * ((z + 2) % 4) + x, sq)
     peers = (sib, yp, ysib)
+    others = [((dp + k) % DP, sq) for k in range(1, DP)]
 
     def send(src, dst, ss, rs, dev):
         return pltpu.make_async_remote_copy(
@@ -487,7 +479,7 @@
         lax.fori_loop(0, count, step, 0)
 
     barrier = pltpu.get_barrier_semaphore()
-    for dev in (sib, yp, ysib, nxt, prv, xp, z1, z2):
+    for dev in (*peers, *others):
         pl.semaphore_signal(barrier, inc=1, device_id=dev, device_id_type=MESH_ID)
 
     r96 = times(96 * dp, 96, 96)
@@ -500,16 +492,17 @@
     own.append(pltpu.make_async_copy(cot_hbm.at[sq], cot.at[mine], loc.at[8]))
     for copy in own:
         copy.start()
-    pl.semaphore_wait(barrier, 8)
+    pl.semaphore_wait(barrier, len(peers) + len(others))
 
     def swap(k, src_hbm, dst, at):
         dev = peers[k]
-        return send(src_hbm.at[dev[1]], dst.at[mine], a2_s.at[at, k], a2_r.at[at, k], dev)
+        return send(src_hbm.at[dev[1]], dst.at[mine], a2_s.at[at], a2_r.at[at], dev)
+
+    def three(ref, at):
+        return send(ref, ref, a2_s.at[at], a2_r.at[at], sib)
 
     def swap_wait(dst, at):
-        for k in range(3):
-            theirs = dst.at[times(128 * peers[k][1], 128, 128)]
-            send(theirs, theirs, a2_s.at[at, k], a2_r.at[at, k], peers[k]).wait_recv()
+        three(dst.at[pl.ds(0, 384)], at).wait_recv()
 
     for k in range(3):
         swap(k, x_hbm, xs, 0).start()
@@ -539,23 +532,23 @@
     def ring_send(ch, e):
         ahead = e // FAR
         part = piece(ch, owner((1 - ahead) * -e + ahead * (e - FAR)), c, y)
-        return send(part, part, ag_s.at[ch, e], ag_r.at[ch, e], side(e))
+        return send(part, part, ag_s.at[ch], ag_r.at[ch, e], side(e))
 
     def hand_on(ch, e):
         part = piece(ch, owner(came_from(e)), c, y)
-        return send(part, part, sb_s.at[ch, e], sb_r.at[ch, e], sib)
+        return send(part, part, sb_s.at[ch], sb_r.at[ch], sib)
 
     def cross(ch, e):
         part = piece(ch, owner(came_from(e)), c, y)
-        return send(part, part, yf_s.at[ch // 2 - 1, e], yf_r.at[ch // 2 - 1, e], yp)
+        return send(part, part, yf_s.at[ch // 2 - 1], yf_r.at[ch // 2 - 1, e], yp)
 
     def cross_on(ch, e):
         part = piece(ch, owner(came_from(e)), c, 1 - y)
-        return send(part, part, yb_s.at[ch // 2 - 1, e], yb_r.at[ch // 2 - 1, e], sib)
+        return send(part, part, yb_s.at[ch // 2 - 1], yb_r.at[ch // 2 - 1], sib)
 
     def arrive(ch, e):
         part = piece(ch, owner(came_from(e)), c, y)
-        send(part, part, ag_s.at[ch, e], ag_r.at[ch, e], side(e)).wait_recv()
+        send(part, part, ag_s.at[ch], ag_r.at[ch, e], side(e)).wait_recv()
         if e not in (FAR - 1, EVENTS - 1):
             ring_send(ch, e + 1).start()
         if ch in crossing:
@@ -564,33 +557,32 @@
 
     def arrive_cross(ch, e):
         part = piece(ch, owner(came_from(e)), c, 1 - y)
-        send(part, part, yf_s.at[ch // 2 - 1, e], yf_r.at[ch // 2 - 1, e], yp).wait_recv()
+        send(part, part, yf_s.at[ch // 2 - 1], yf_r.at[ch // 2 - 1, e], yp).wait_recv()
         cross_on(ch, e).start()
 
+    def seven(ch):
+        if ch < 3:
+            return watt.at[0:3, pl.ds(0, 336), pl.ds(0, 256 if ch < 2 else 128)]
+        if ch < 5:
+            return win.at[pl.ds(0, 7), 0, :, pl.ds(0, 1536 if ch == 3 else 768)]
+        return watt.at[3, pl.ds(0, 336)] if ch == 7 else wff.at[pl.ds(0, 1344), pl.ds(0, 256)]
+
+    def all_seven(ch, ss, rs, dev):
+        return send(seven(ch), seven(ch), ss, rs, dev)
+
     def settled(group):
-        last = groups[group][-1]
-
-        def step(e):
-            d = owner(-came_from(e))
-            for ch in groups[group]:
-                part = piece(ch, d, 1 - c, y)
-                send(part, part, sb_s.at[ch, e], sb_r.at[ch, e], sib).wait_recv()
-            if last in crossing:
-                part = piece(last, d, 1 - c, 1 - y)
-                send(part, part, yb_s.at[group, e], yb_r.at[group, e], sib).wait_recv()
-
-        loop(EVENTS, step)
+        for ch in groups[group]:
+            all_seven(ch, sb_s.at[ch], sb_r.at[ch], sib).wait_recv()
+            if ch in crossing:
+                all_seven(ch, yb_s.at[group], yb_r.at[group], sib).wait_recv()
 
     def gather_sent(group):
-        def step(e):
-            for ch in groups[group]:
-                ring_send(ch, e).wait_send()
-                hand_on(ch, e).wait_send()
-            if groups[group][-1] in crossing:
-                cross(groups[group][-1], e).wait_send()
-                cross_on(groups[group][-1], e).wait_send()
-
-        loop(EVENTS, step)
+        for ch in groups[group]:
+            all_seven(ch, ag_s.at[ch], ag_r.at[ch, 0], sib).wait_send()
+            all_seven(ch, sb_s.at[ch], sb_r.at[ch], sib).wait_send()
+            if ch in crossing:
+                all_seven(ch, yf_s.at[group], yf_r.at[group, 0], yp).wait_send()
+                all_seven(ch, yb_s.at[group], yb_r.at[group], sib).wait_send()
 
     def begin(group):
         for ch in reversed(groups[group]):
@@ -726,19 +718,25 @@
     own[8].wait()
     swap_wait(cot, 1)
 
-    def half_ff(j):
-        src = gff.at[pl.ds(2 * j, 2), times(192 * (1 - c), 192, 192)]
-        return send(src, sib_ff.at[pl.ds(2 * j, 2)], hs_s.at[0, j], hs_r.at[0, j], sib)
-
-    def grad_ff(j):
+    def chunk(i):
+        return (3 - z + (i + 1) // 2 + 2 * (i % 2) * (1 - i // 2)) % 4
+
+    def half_ff(i):
+        two = pl.ds(2 * chunk(i), 2)
+        src = gff.at[two, times(192 * (1 - c), 192, 192)]
+        return send(src, sib_ff.at[two], hs_s.at[0], hs_r.at[0, i], sib)
+
+    def grad_ff(i):
+        j = chunk(i)
         v = dg(big[j, up_rows, :], cot[...], 0, 0).astype(BF)
         gff[pl.ds(2 * j, 2)] = v.reshape(2, 384, 768)
-        half_ff(j).start()
-        serve_at(AT_GFF, 4, j)
-
-
-    def merge_ff(j):
-        half_ff(j).wait()
+        half_ff(i).start()
+        serve_at(AT_GFF, 4, i)
+
+
+    def merge_ff(i):
+        j = chunk(i)
+        half_ff(i).wait_recv()
         rows = times(192 * c, 192, 192)
         for i in range(2):
             gff[2 * j + i, rows] = (gff[2 * j + i, rows].astype(F32) + sib_ff[2 * j + i].astype(F32)).astype(BF)
@@ -774,7 +772,7 @@
     def rs_send(ch, e):
         ahead = e // FAR
         part = rs_piece(ch, owner((1 - ahead) * (FAR - e) + ahead * (e - EVENTS)), y)
-        return send(part, landing[ch].at[e], rr_s.at[ch, e], rr_r.at[ch, e], side(e))
+        return send(part, landing[ch].at[e], rr_s.at[ch], ag_r.at[ch, e], side(e))
 
     def rs_begin(ch):
         rs_send(ch, 0).start()
@@ -789,10 +787,10 @@
 
     def half_in(k):
         src = gin.at[:, times(1536 * (1 - c) + 384 * k, 384, 384)]
-        return send(src, sib_in.at[k], hs_s.at[1, k], hs_r.at[1, k], sib)
+        return send(src, sib_in.at[k], hs_s.at[1], hs_r.at[1, k], sib)
 
     def merge_in(k):
-        half_in(k).wait()
+        half_in(k).wait_recv()
         cols = times(1536 * c + 384 * k, 384, 384)
         gin[:, cols] = (gin[:, cols].astype(F32) + sib_in[k].astype(F32)).astype(BF)
 
@@ -800,10 +798,10 @@
         return sib_ff.at[:, times(48 * t, 48, 48)]
 
     def half_att(t):
-        return send(win.at[:, 1 - c, :, block(t)], sib_rows(t), hs_s.at[2, t], hs_r.at[2, t], sib)
+        return send(win.at[:, 1 - c, :, block(t)], sib_rows(t), hs_s.at[2], hs_r.at[2, t], sib)
 
     def merge_att(t):
-        half_att(t).wait()
+        half_att(t).wait_recv()
         win[:, c, :, block(t)] = (win[:, c, :, block(t)].astype(F32) + sib_rows(t)[...].astype(F32)).astype(BF)
 
     final = [f_ff, f_in] + [f_att.at[t] for t in range(4)]
@@ -828,10 +826,10 @@
         return send(own_piece(g), final[g], fa_s.at[g], fa_r.at[g], yp)
 
     def share_b(g, k):
-        return send(rs_piece(3 * g + 2, dp, y), out_piece(g, c, y), fo_s.at[g, k], fo_r.at[g, k], peers[k])
+        return send(rs_piece(3 * g + 2, dp, y), out_piece(g, c, y), fb_s.at[g], fb_r.at[g], peers[k])
 
     def share_sum(g):
-        return send(final[g], out_piece(g, c, None), fo_s.at[g, 3], fo_r.at[g, 3], sib)
+        return send(final[g], out_piece(g, c, None), fo_s.at[g], fo_r.at[g], sib)
 
     def keep_b(g):
         return pltpu.make_async_copy(rs_piece(3 * g + 2, dp, y), out_piece(g, c, y), fl.at[g, 0])
@@ -851,35 +849,48 @@
         keep_sum(g).start()
 
     def hop(k):
-        dev = (yp, sib, xp, z1, z2)[k]
-        return send(sums.at[k], sums_in.at[k], bf_s.at[k], bf_r.at[k], dev)
-
-    def hop_done(k):
-        hop(k).wait()
-        sums[k + 1] = sums[k] + sums_in[k]
+        return send(sums.at[k], sums_in.at[k], bf_s.at[k], bf_r.at[k], (yp, sib)[k])
+
+    def hop_on(k):
+        if k < 2:
+            hop(k).wait()
+            sums[k + 1] = sums[k] + sums_in[k]
+        if k == 0:
+            hop(1).start()
+        elif k == 1:
+            for dev in others:
+                send(sums.at[2], spread.at[dp], bf_s.at[2], bf_r.at[2], dev).start()
+            spread[dp] = sums[2]
+        else:
+            send(spread.at[pl.ds(0, 7)], spread.at[pl.ds(0, 7)], bf_s.at[2], bf_r.at[2], sib).wait()
+            total = spread[0]
+            for k in range(1, DP):
+                total = total + spread[k]
+            small_out[...] = total
 
     def merge(g, k):
         (merge_ff, merge_in, merge_att)[g](k)
 
     def go(g):
-        if g < 2:
-            cross_sum(g).start()
-            rs_begin(3 * g)
-            rs_begin(3 * g + 1)
+        if g == 0:
+            cross_sum(0).start()
+        elif g == 1:
+            cross_sum(1).start()
+            rs_begin(3)
+            rs_begin(4)
         else:
             rs_begin(4 + g)
+
+    def leave(e):
+        for ch in range(2):
+            rs_send(ch, e).start()
 
     def cross_in(g):
         add_cross(g)
         rs_begin(3 * g + 2)
 
-    def hop_on(k):
-        hop_done(k)
-        if k < 4:
-            hop(k + 1).start()
-
     acts |= {
-        RS: rs_event, HALF: merge, GO: go, XC: cross_in, SHARE_A: lambda g: share_a(g).start(), FIN_B: finish_b,
+        RS: rs_event, HALF: merge, GO: go, LEAVE: leave, XC: cross_in, SHARE_A: lambda g: share_a(g).start(), FIN_B: finish_b,
         FSUM: finish_sum, HOP: hop_on,
     }
 
@@ -895,14 +906,18 @@
 
     loop(4, grad_up)
 
-    def grad_in(j):
+    def grad_in(i):
+        j = (2 * (1 - c) + i) % 4
         gin[:, block(j)] = dg(nf[...], big[j, down_rows, :], 0, 0).astype(BF)
-        serve_at(AT_GIN, 4, j)
+
+        @pl.when(i == 1)
+        def _():
+            for k in range(4):
+                half_in(k).start()
+
+        serve_at(AT_GIN, 4, i)
 
     loop(4, grad_in)
-
-    for k in range(4):
-        half_in(k).start()
 
     acc[...] = jnp.zeros_like(acc)
 
@@ -942,16 +957,10 @@
 
     def give(src, dst_hbm, at, k):
         dev = peers[k]
-        return send(src.at[times(128 * dev[1], 128, 128)], dst_hbm.at[sq], a2_s.at[at, k], a2_r.at[at, k], dev)
-
-    def give_wait(src, dst_hbm, at):
-        for k in range(3):
-            give(src, dst_hbm, at, k).wait_send()
-            theirs = dst_hbm.at[peers[k][1]]
-            send(theirs, theirs, a2_s.at[at, k], a2_r.at[at, k], peers[k]).wait_recv()
+        return send(src.at[times(128 * dev[1], 128, 128)], dst_hbm.at[sq], a2_s.at[at], a2_r.at[at], dev)
 
     def pool_send(k):
-        return send(pool, pool_hbm.at[sq], a2_s.at[4, k], a2_r.at[4, k], peers[k])
+        return send(pool, pool_hbm.at[sq], a2_s.at[4], a2_r.at[4], peers[k])
 
     pool_own = pltpu.make_async_copy(pool, pool_hbm.at[sq], loc.at[2])
     lay = big.at[0, up_rows]
@@ -1057,39 +1066,31 @@
     gx_own.start()
     serve(AT_GX)
     serve(AT_TAIL)
-    small_out[...] = sums[5]
 
     for g in range(6):
         if g < 2:
             keep_b(g).wait()
-            for k, (cc, yy) in enumerate(((1 - c, y), (c, 1 - y), (1 - c, 1 - y))):
-                share_b(g, k).wait_send()
-                came = out_piece(g, cc, yy)
-                send(came, came, fo_s.at[g, k], fo_r.at[g, k], peers[k]).wait_recv()
+            same = (sib_ff.at[pl.ds(0, 3), pl.ds(0, 32)], gin.at[pl.ds(0, 288), pl.ds(0, 256)])[g]
+            send(same, same, fb_s.at[g], fb_r.at[g], sib).wait()
         keep_sum(g).wait()
         share_sum(g).wait_send()
         came = out_piece(g, 1 - c, None)
-        send(came, came, fo_s.at[g, 3], fo_r.at[g, 3], sib).wait_recv()
-
-    def ring_sent(e):
-        for ch in range(10):
-            rs_send(ch, e).wait_send()
-
-    loop(EVENTS, ring_sent)
+        send(came, came, fo_s.at[g], fo_r.at[g], sib).wait_recv()
+    for ch in range(10):
+        send(landing[ch], landing[ch], rr_s.at[ch], ag_r.at[ch, 0], sib).wait_send()
+    for g, same in enumerate((sib_ff, sib_in, sib_ff)):
+        send(same, same, hs_s.at[g], hs_r.at[g, 0], sib).wait_send()
     gather_sent(0)
     gather_sent(2)
     gather_sent(3)
-    give_wait(lay, out_hbm, 2)
-    give_wait(mixed, gx_hbm, 3)
+    three(out_hbm.at[pl.ds(0, 3)], 2).wait()
+    three(gx_hbm.at[pl.ds(0, 3)], 3).wait()
+    three(pool_hbm.at[pl.ds(0, 3)], 4).wait()
+    three(xs.at[pl.ds(0, 384)], 0).wait_send()
+    three(cot.at[pl.ds(0, 384)], 1).wait_send()
     lay_own.wait()
     gx_own.wait()
     pool_own.wait()
-    for k in range(3):
-        pool_send(k).wait_send()
-        theirs = pool_hbm.at[peers[k][1]]
-        send(theirs, theirs, a2_s.at[4, k], a2_r.at[4, k], peers[k]).wait_recv()
-        swap(k, x_hbm, xs, 0).wait_send()
-        swap(k, cot_hbm, cot, 1).wait_send()
 
 
 def finish_kernel(
@@ -1159,12 +1160,13 @@
             (128, 768), (96, 1024), (4, 48, 768),
         )
     ]
-    scratch += [pltpu.VMEM((6, 32, 128), F32), pltpu.VMEM((5, 32, 128), F32), pltpu.VMEM((8, 768), F32)]
+    scratch += [pltpu.VMEM((n, 32, 128), F32) for n in (3, 2, DP)]
+    scratch.append(pltpu.VMEM((8, 768), F32))
     scratch += [
         dma(shape)
         for shape in (
-            (8, 7), (8, 7), (8, 7), (8, 7), (3, 7), (3, 7), (3, 7), (3, 7), (10, 7), (10, 7), (9,), (5, 3), (5, 3),
-            (3, 4), (3, 4), (2,), (2,), (6,), (6,), (6, 4), (6, 4), (6, 2), (5,), (5,),
+            (8,), (10, 7), (8,), (8,), (3,), (3, 7), (3,), (3,), (10,), (9,), (5,), (5,), (3,), (3, 4), (2,), (2,),
+            (6,), (6,), (2,), (2,), (6,), (6,), (6, 2), (3,), (3,),
         )
     ]
     sums = pl.pallas_call(

time: 149 us -> 147 us (0.987)
  Pallas kernels: 148 us -> 146 us
    pallas_call x1, Pallas kernels: 143 us -> 141 us  [passage_shards(): pl.pallas_call(layer_kernel, out_shape=(jax.ShapeDtypeStruct((4, 128, 768...]
where the time goes in v4:
time: 147 us
  Pallas kernels  146 us (99%)
    pallas_call x1, Pallas kernels, passage_shards(): pl.pallas_call(layer_kernel, out_shape=(jax.ShapeDtypeStruct((4, 128, 768...  141 us
    pallas_call x1, Pallas kernels, passage_shards(): pl.pallas_call(finish_kernel, out_shape=(jax.ShapeDtypeStruct((4, 128, 76...  4.9 us

profile of v4, /device:TPU:0, one launch (start us, length us, event | category | flops | bytes accessed | tf_op | source)
XLA Modules:
  0.0 147.1 jit_solution(11961772555558762348)
XLA Ops:
  0.6 141.4 %layer.1 = (bf16[4,128,768]{2,1,0:T(8,128)(2,1)}, bf16[4,128,768]{2,1,0:T(8,128)(2,1)}, bf16[4,96,768]{2,1,0:T(8,128)(2,1)}, bf16[96,3072]{1,0:T(8,128)(2,1)}, b...) custom-call(bf16[4,128,768]{2,1,0:T(8,128)(2,1)} %x_hbm.1, bf16[4,128,768]{2,1,0:T(8,128)(2,1)} %cot_hbm.1, ...), custom_call_target="tpu_custom_call" | custom-call | tf_op jit(solution)/shard_map/layer/pallas_call | solution.py:1172
  142.1 4.9 %finish.1 = (bf16[4,128,768]{2,1,0:T(8,128)(2,1)}, bf16[4,128,768]{2,1,0:T(8,128)(2,1)}, f32[4,768]{1,0:T(4,128)}, f32[768]{0:T(1024)}, f32[96,768]{1,0:T(8,128)...) custom-call(bf16[4,128,768]{2,1,0:T(8,128)(2,1)} %get-tuple-element., ...), custom_call_target="tpu_custom_call" | custom-call | tf_op jit(solution)/shard_map/finish/pallas_call | solution.py:1194

commit v5 on v4

--- a/solution.py
+++ b/solution.py
@@ -268,16 +268,15 @@
     AT_ATT: (
         (CR, 2, 0), (AG, 1, 2), (CR, 2, 4), (AG, 1, 6), (CR, 2, 1), (AG, 0, 2), (BEGIN, 3), (BEGIN, 1), (CR, 2, 5),
         (AG, 0, 6), (AG, 2, 3), (CR, 2, 2), (AG, 1, 3), (CR, 2, 6), (AG, 0, 3), (AG, 7, 0), (CR, 2, 3), (AG, 7, 4),
-        (AG, 4, 0),
     ),
     (AT_PROJECT, 0): (
-        (AG, 4, 4),
+        (AG, 4, 0), (AG, 4, 4),
     ),
     (AT_PROJECT, 2): (
         (AG, 3, 0),
     ),
     (AT_ATTEND, 0): (
-        (CR, 4, 0), (AG, 3, 4), (AG, 7, 1),
+        (AG, 3, 4), (AG, 7, 1),
     ),
     (AT_ATTEND, 1): (
         (AG, 7, 5), (AG, 4, 1),
@@ -289,19 +288,22 @@
         (AG, 3, 5), (AG, 7, 2),
     ),
     (AT_ATTEND, 4): (
-        (AG, 7, 6), (AG, 4, 2),
+        (AG, 7, 6), (AG, 4, 2), (CR, 4, 0),
     ),
     (AT_ATTEND, 5): (
-        (AG, 4, 6), (CR, 4, 4), (AG, 3, 2), (CR, 4, 1), (BEGIN, 2),
+        (AG, 4, 6), (CR, 4, 4), (AG, 3, 2), (BEGIN, 2),
     ),
     AT_WO: (
-        (AG, 3, 6), (CR, 4, 5), (AG, 7, 3), (AG, 4, 3), (CR, 4, 2),
+        (CR, 4, 1), (AG, 3, 6), (AG, 7, 3), (CR, 4, 5), (AG, 4, 3),
+    ),
+    (AT_RESIDUAL, 0): (
+        (CR, 4, 2),
     ),
     (AT_RESIDUAL, 1): (
-        (AG, 3, 3), (CR, 4, 6),
+        (AG, 3, 3),
     ),
     AT_IN: (
-        (AG, 6, 0), (AG, 6, 4), (CR, 4, 3), (AG, 5, 0),
+        (AG, 6, 0), (CR, 4, 6), (AG, 6, 4), (CR, 4, 3), (AG, 5, 0),
     ),
     (AT_WIDEN, 0): (
         (AG, 5, 4), (AG, 6, 1), (CR, 6, 0),
@@ -313,7 +315,10 @@
         (AG, 5, 1), (CR, 6, 4),
     ),
     (AT_WIDEN, 3): (
-        (AG, 5, 5), (AG, 6, 2), (CR, 6, 1),
+        (AG, 5, 5),
+    ),
+    (AT_GFF, 0): (
+        (AG, 6, 2), (CR, 6, 1),
     ),
     (AT_GFF, 1): (
         (AG, 6, 6),
@@ -325,17 +330,14 @@
         (AG, 5, 6), (HALF, 0, 0), (LEAVE, 0),
     ),
     AT_MFF: (
-        (AG, 6, 3), (CR, 6, 2), (HALF, 0, 1), (HALF, 0, 2), (LEAVE, 4), (AG, 5, 3), (CR, 6, 6), (HALF, 0, 3), (GO, 0),
+        (AG, 6, 3), (HALF, 0, 1), (CR, 6, 2), (HALF, 0, 2), (LEAVE, 4), (AG, 5, 3), (CR, 6, 6), (HALF, 0, 3), (GO, 0),
         (RS, 0, 0),
     ),
     AT_FF: (
         (RS, 1, 0), (CR, 6, 3), (RS, 0, 4),
     ),
     (AT_GUP, 0): (
-        (RS, 1, 4),
-    ),
-    (AT_GUP, 1): (
-        (RS, 0, 1),
+        (RS, 1, 4), (RS, 0, 1),
     ),
     (AT_GUP, 2): (
         (RS, 1, 1),
@@ -353,16 +355,16 @@
         (RS, 1, 2),
     ),
     (AT_GNF, 0): (
-        (RS, 0, 6), (HALF, 1, 0), (XC, 0),
+        (XC, 0), (RS, 0, 6), (HALF, 1, 0),
     ),
     (AT_GNF, 1): (
         (RS, 1, 6), (HALF, 1, 1),
     ),
     (AT_GNF, 2): (
-        (RS, 0, 3), (HALF, 1, 2), (RS, 1, 3), (SHARE_A, 0),
+        (RS, 0, 3), (HALF, 1, 2),
     ),
     (AT_GNF, 3): (
-        (HALF, 1, 3), (GO, 1), (RS, 2, 0), (RS, 2, 4),
+        (RS, 1, 3), (SHARE_A, 0), (HALF, 1, 3), (GO, 1), (RS, 2, 0), (RS, 2, 4),
     ),
     (AT_NARROW, 0): (
         (RS, 3, 0),
@@ -371,43 +373,46 @@
         (RS, 3, 4), (HALF, 2, 3), (GO, 5),
     ),
     (AT_NARROW, 2): (
-        (FSUM, 0), (RS, 4, 0),
+        (RS, 4, 0),
     ),
     (AT_NARROW, 3): (
-        (RS, 4, 4), (RS, 2, 1),
+        (FSUM, 0), (RS, 4, 4),
+    ),
+    AT_LAY: (
+        (RS, 2, 1),
     ),
     (AT_AB, 0): (
-        (RS, 2, 5), (RS, 3, 1), (RS, 3, 5), (RS, 9, 0),
+        (RS, 2, 5), (RS, 3, 1), (RS, 3, 5),
     ),
     (AT_AB, 1): (
-        (RS, 9, 4), (RS, 4, 1), (RS, 4, 5), (XC, 1), (RS, 2, 2), (RS, 2, 6),
+        (RS, 9, 0), (RS, 9, 4), (RS, 4, 1), (RS, 4, 5), (RS, 2, 2),
     ),
     (AT_AB, 2): (
-        (RS, 3, 2), (RS, 3, 6), (RS, 9, 1), (HALF, 2, 0), (GO, 2), (RS, 9, 5),
+        (RS, 2, 6), (XC, 1), (RS, 3, 2), (RS, 3, 6), (HALF, 2, 0), (GO, 2), (RS, 9, 1),
     ),
     (AT_AB, 3): (
-        (RS, 4, 2), (RS, 4, 6), (RS, 5, 0), (RS, 5, 4), (RS, 2, 3), (FIN_B, 0), (RS, 3, 3),
+        (RS, 9, 5), (RS, 4, 2), (RS, 4, 6), (RS, 2, 3), (FIN_B, 0), (RS, 5, 0),
     ),
     (AT_AB, 4): (
-        (RS, 9, 2), (RS, 6, 0), (RS, 6, 4), (HALF, 2, 1), (GO, 3), (RS, 9, 6),
+        (RS, 5, 4), (RS, 3, 3), (RS, 6, 0), (HALF, 2, 1), (GO, 3), (RS, 6, 4),
     ),
     (AT_AB, 5): (
-        (RS, 4, 3), (SHARE_A, 1), (RS, 5, 1), (RS, 5, 5), (RS, 9, 3), (SHARE_A, 5), (RS, 6, 1),
+        (RS, 9, 2), (RS, 9, 6), (RS, 4, 3), (SHARE_A, 1), (RS, 5, 1), (RS, 5, 5),
     ),
     (AT_GN, 0): (
-        (RS, 6, 5), (RS, 7, 0),
+        (RS, 6, 1), (RS, 7, 0),
     ),
     (AT_GN, 1): (
-        (RS, 7, 4), (HALF, 2, 2), (GO, 4), (RS, 5, 2),
+        (RS, 7, 4), (RS, 6, 5), (HALF, 2, 2), (GO, 4),
     ),
     AT_GX: (
-        (RS, 5, 6),
+        (RS, 9, 3), (SHARE_A, 5), (RS, 5, 2),
     ),
     AT_TAIL: (
-        (RS, 6, 2), (RS, 6, 6), (RS, 7, 1), (FSUM, 1), (RS, 7, 5), (RS, 8, 0), (FSUM, 5), (RS, 8, 4), (RS, 5, 3),
-        (FIN_B, 1), (RS, 6, 3), (SHARE_A, 2), (RS, 7, 2), (HOP, 0), (RS, 7, 6), (RS, 8, 1), (RS, 8, 5), (RS, 7, 3),
-        (SHARE_A, 3), (HOP, 1), (RS, 8, 2), (RS, 8, 6), (RS, 8, 3), (SHARE_A, 4), (FSUM, 2), (HOP, 2), (FSUM, 3),
-        (FSUM, 4),
+        (RS, 5, 6), (RS, 6, 2), (RS, 7, 1), (RS, 7, 5), (FSUM, 1), (RS, 6, 6), (RS, 8, 0), (HOP, 0), (RS, 8, 4),
+        (RS, 5, 3), (FIN_B, 1), (RS, 6, 3), (SHARE_A, 2), (RS, 7, 2), (RS, 7, 6), (RS, 8, 1), (HOP, 1), (RS, 8, 5),
+        (RS, 7, 3), (SHARE_A, 3), (RS, 8, 2), (RS, 8, 6), (FSUM, 5), (HOP, 2), (RS, 8, 3), (SHARE_A, 4), (FSUM, 2),
+        (FSUM, 3), (FSUM, 4),
     ),
 }
 
@@ -984,7 +989,11 @@
     serve(AT_LAY)
 
     flip_sum = lax.broadcasted_iota(jnp.int32, (128, 128), 0) + lax.broadcasted_iota(jnp.int32, (128, 128), 1)
-    flip = (flip_sum == 127).astype(F32)
+    flip = (flip_sum == 127).astype(F32).astype(BF)
+
+    def flipped(v):
+        high = v.astype(BF)
+        return dg(flip, high, 1, 0) + dg(flip, (v - high.astype(F32)).astype(BF), 1, 0)
 
     def attend_back(hp):
         cols = times(128 * hp, 128, 128)
@@ -1013,7 +1022,7 @@
                 d_both[pl.ds(512 * h + 128 * ib, 128), :] = d_low
                 one = dg(d_low, key_h, 1, 0)
                 g_query[ib] = one if h == 0 else g_query[ib] + one
-            tilted = exact(flip, jnp.concatenate(near, axis=1), 1, 0)
+            tilted = flipped(jnp.concatenate(near, axis=1))
             tilted = jnp.concatenate([tilted, jnp.zeros((128, 128), F32)], axis=1)
             flat = jnp.sum(pltpu.roll(tilted, 385, 1, stride=1, stride_axis=0), axis=0, keepdims=True)
             far = jnp.concatenate(

time: 147 us -> 145 us (0.986)
  Pallas kernels: 146 us -> 144 us
    pallas_call x1, Pallas kernels: 141 us -> 139 us  [passage_shards(): pl.pallas_call(layer_kernel, out_shape=(jax.ShapeDtypeStruct((4, 128, 768...]
where the time goes in v5:
time: 145 us
  Pallas kernels  144 us (99%)
    pallas_call x1, Pallas kernels, passage_shards(): pl.pallas_call(layer_kernel, out_shape=(jax.ShapeDtypeStruct((4, 128, 768...  139 us
    pallas_call x1, Pallas kernels, passage_shards(): pl.pallas_call(finish_kernel, out_shape=(jax.ShapeDtypeStruct((4, 128, 76...  4.9 us

profile of v5, /device:TPU:0, one launch (start us, length us, event | category | flops | bytes accessed | tf_op | source)
XLA Modules:
  0.0 145.1 jit_solution(3734226218015902403)
XLA Ops:
  0.6 139.4 %layer.1 = (bf16[4,128,768]{2,1,0:T(8,128)(2,1)}, bf16[4,128,768]{2,1,0:T(8,128)(2,1)}, bf16[4,96,768]{2,1,0:T(8,128)(2,1)}, bf16[96,3072]{1,0:T(8,128)(2,1)}, b...) custom-call(bf16[4,128,768]{2,1,0:T(8,128)(2,1)} %x_hbm.1, bf16[4,128,768]{2,1,0:T(8,128)(2,1)} %cot_hbm.1, ...), custom_call_target="tpu_custom_call" | custom-call | tf_op jit(solution)/shard_map/layer/pallas_call | solution.py:1181
  140.1 4.9 %finish.1 = (bf16[4,128,768]{2,1,0:T(8,128)(2,1)}, bf16[4,128,768]{2,1,0:T(8,128)(2,1)}, f32[4,768]{1,0:T(4,128)}, f32[768]{0:T(1024)}, f32[96,768]{1,0:T(8,128)...) custom-call(bf16[4,128,768]{2,1,0:T(8,128)(2,1)} %get-tuple-element., ...), custom_call_target="tpu_custom_call" | custom-call | tf_op jit(solution)/shard_map/finish/pallas_call | solution.py:1203

commit v6 on v5

--- a/solution.py
+++ b/solution.py
@@ -924,14 +924,6 @@
 
     loop(4, grad_in)
 
-    acc[...] = jnp.zeros_like(acc)
-
-    def grad_nf(j):
-        acc[...] += dg(big[j, down_rows, :], win_block(j), 1, 1)
-        serve_at(AT_GNF, 4, j)
-
-    loop(4, grad_nf)
-
     def norm_back(v, gain, grad):
         s = lax.rsqrt(jnp.mean(v * v, axis=-1, keepdims=True) + EPS)
         scaled = grad * gain
@@ -939,15 +931,19 @@
         return back, jnp.sum(grad * v * s, axis=0, keepdims=True)
 
     def ffn_norm_back(b, total):
-        rows = times(128 * b, 128, 128)
-        v = hid[rows, :]
-        back, part = norm_back(v, gain_f, acc[rows, :])
+        rows, down = times(256 * b, 256, 256), times(TOKENS + 256 * b, 256, 256)
+        grad = dg(big[0, down, :], win_block(0), 1, 1)
+        for j in range(1, 4):
+            grad = grad + dg(big[j, down, :], win_block(j), 1, 1)
+        back, part = norm_back(hid[rows, :], gain_f, grad)
         grad = cot[rows, :].astype(F32) + back
         acc[rows, :] = grad
         cot[rows, :] = grad.astype(BF)
+        serve_at(AT_GNF, 4, 2 * b)
+        serve_at(AT_GNF, 4, 2 * b + 1)
         return total + part
 
-    g_ffn_gain = lax.fori_loop(0, 4, ffn_norm_back, jnp.zeros((1, WIDTH), F32))
+    g_ffn_gain = lax.fori_loop(0, 2, ffn_norm_back, jnp.zeros((1, WIDTH), F32))
 
     serve(AT_FNORM)
     serve(AT_PREWO)

time: 145 us -> 145 us (level)
  no operation moved by 1% of the time
where the time goes in v6:
time: 145 us
  Pallas kernels  144 us (99%)
    pallas_call x1, Pallas kernels, passage_shards(): pl.pallas_call(layer_kernel, out_shape=(jax.ShapeDtypeStruct((4, 128, 768...  139 us
    pallas_call x1, Pallas kernels, passage_shards(): pl.pallas_call(finish_kernel, out_shape=(jax.ShapeDtypeStruct((4, 128, 76...  4.9 us

profile of v6, /device:TPU:0, one launch (start us, length us, event | category | flops | bytes accessed | tf_op | source)
XLA Modules:
  0.0 144.7 jit_solution(7491809158442686627)
XLA Ops:
  0.6 139.0 %layer.1 = (bf16[4,128,768]{2,1,0:T(8,128)(2,1)}, bf16[4,128,768]{2,1,0:T(8,128)(2,1)}, bf16[4,96,768]{2,1,0:T(8,128)(2,1)}, bf16[96,3072]{1,0:T(8,128)(2,1)}, b...) custom-call(bf16[4,128,768]{2,1,0:T(8,128)(2,1)} %x_hbm.1, bf16[4,128,768]{2,1,0:T(8,128)(2,1)} %cot_hbm.1, ...), custom_call_target="tpu_custom_call" | custom-call | tf_op jit(solution)/shard_map/layer/pallas_call | solution.py:1177
  139.7 4.9 %finish.1 = (bf16[4,128,768]{2,1,0:T(8,128)(2,1)}, bf16[4,128,768]{2,1,0:T(8,128)(2,1)}, f32[4,768]{1,0:T(4,128)}, f32[768]{0:T(1024)}, f32[96,768]{1,0:T(8,128)...) custom-call(bf16[4,128,768]{2,1,0:T(8,128)(2,1)} %get-tuple-element., ...), custom_call_target="tpu_custom_call" | custom-call | tf_op jit(solution)/shard_map/finish/pallas_call | solution.py:1199
